TPU v7x, 128 devices: a whole 4x4x4 slice. The times are simulated.
128 devices in a mesh: gz: 32 (over y, x, core), gy: 4 (over z).
Axes of the slice: x: 4, y: 4, z: 4, core: 2. Of those that a mesh axis runs over, the one named last changes fastest.
Arguments:
- iterate: float32 [512, 256, 128], P('gz', 'gy'), may hold values from -13 to 13
- source: float32 [512, 256, 128], P('gz', 'gy'), may hold values from -27 to 27
- region: int32 [512, 256, 128], P('gz', 'gy'), may hold values from 0 to 2, as said below
- fixed_mask: int32 [512, 256, 128], P('gz', 'gy'), may hold values from 0 to 1, as said below
Outputs:
- correction: float32 [512, 256, 128], P('gz', 'gy')
- lin_residual: float32 [512, 256, 128], P('gz', 'gy')
- residual_rms: float32 [], replicated
Inputs may be any that keep to these rules, and one draw needn't show every extreme that they name: `region`: the same at every z. `fixed_mask`: the same at every z.
All inputs are finite; a program needn't handle non-finite values.
Results may differ from a plain program's by a relative error of at most 0.007.
Values sent between devices are 32-bit elements; how exact they have to be, the bound alone decides.
No kernel may reach another device: no remote copies, remote signals or barrier semaphores. Data moves between devices by JAX's collectives and lax.ppermute only.
A program may use at most 64 MiB of HBM per device.

v0:
```python
import jax
import jax.numpy as jnp
from jax import lax
from jax.sharding import PartitionSpec as P

SWEEPS = 4


def with_halo(array, sides, width):
    for axis, dim in sides:
        devices, length = (lax.axis_size(axis), array.shape[dim])
        up = [(i, (i + 1) % devices) for i in range(devices - 1)]
        down = [(j, i) for i, j in up]
        last = lax.slice_in_dim(array, length - width, length, axis=dim)
        first = lax.slice_in_dim(array, 0, width, axis=dim)
        before = lax.ppermute(last, axis, up)
        after = lax.ppermute(first, axis, down)
        array = jnp.concatenate([before, array, after], axis=dim)
    return array


def dst_table(count):
    index = jnp.arange(count, dtype=jnp.int32)
    phase = (index[:, None] + 1) * (index[None, :] + 1) % (2 * (count + 1))
    return jnp.sqrt(2.0 / (count + 1)) * jnp.sin(jnp.pi * phase.astype(jnp.float32) / (count + 1))


def eigen_values(index, count):
    return 2.0 - 2.0 * jnp.cos(jnp.pi * (index.astype(jnp.float32) + 1.0) / (count + 1))


def reluct(bsq, region):
    iron = 0.05 + bsq * bsq / (bsq * bsq + 9.0)
    return jnp.where(region == 2, iron, jnp.float32(1.0))


def slab_rimmed(field):
    padded = with_halo(field, (("gz", 0), ("gy", 1)), 1)
    return jnp.pad(padded, ((0, 0), (0, 0), (1, 1)))


def face_terms(padded):
    center = padded[1:-1, 1:-1, 1:-1]
    return (
        0.5 * (center + padded[2:, 1:-1, 1:-1]),
        0.5 * (center + padded[:-2, 1:-1, 1:-1]),
        0.5 * (center + padded[1:-1, 2:, 1:-1]),
        0.5 * (center + padded[1:-1, :-2, 1:-1]),
        0.5 * (center + padded[1:-1, 1:-1, 2:]),
        0.5 * (center + padded[1:-1, 1:-1, :-2]),
    )


def stencil(field, padded, terms):
    near = (
        padded[2:, 1:-1, 1:-1],
        padded[:-2, 1:-1, 1:-1],
        padded[1:-1, 2:, 1:-1],
        padded[1:-1, :-2, 1:-1],
        padded[1:-1, 1:-1, 2:],
        padded[1:-1, 1:-1, :-2],
    )
    total = jnp.zeros_like(field)
    for coef, other in zip(terms, near):
        total = total + coef * (field - other)
    return total


def smooth(vhat, lam, nbpad, rim_fn):
    center = nbpad[1:-1, 1:-1]
    cyp = 0.5 * (center + nbpad[2:, 1:-1])
    cym = 0.5 * (center + nbpad[:-2, 1:-1])
    cxp = 0.5 * (center + nbpad[1:-1, 2:])
    cxm = 0.5 * (center + nbpad[1:-1, :-2])
    diag = cyp + cym + cxp + cxm + lam[:, None, None] * center
    smoothed = jnp.zeros_like(vhat)
    for sweep in range(SWEEPS):
        wpad = rim_fn(smoothed)
        near = (
            cyp * wpad[:, 2:, 1:-1]
            + cym * wpad[:, :-2, 1:-1]
            + cxp * wpad[:, 1:-1, 2:]
            + cxm * wpad[:, 1:-1, :-2]
        )
        smoothed = smoothed + 0.6 * (vhat - (diag * smoothed - near)) / diag
    return smoothed


def mode_rimmed(field):
    padded = with_halo(field, (("gy", 1),), 1)
    return jnp.pad(padded, ((0, 0), (0, 0), (1, 1)))


def precondition(vector, nbpad, table):
    zcells = vector.shape[0]
    groups = lax.axis_size("gz")
    order = zcells * groups
    group = lax.axis_index("gz")

    def transform(lines):
        return jnp.einsum("kj,jyx->kyx", table, lines, precision=lax.Precision.HIGHEST)

    vhat = transform(lax.all_to_all(vector, "gz", split_axis=2, concat_axis=0, tiled=True))
    modes = lax.all_to_all(vhat, "gz", split_axis=0, concat_axis=2, tiled=True)
    index = group * zcells + jnp.arange(zcells, dtype=jnp.int32)
    smoothed = smooth(modes, eigen_values(index, order), nbpad, mode_rimmed)
    back = transform(lax.all_to_all(smoothed, "gz", split_axis=2, concat_axis=0, tiled=True))
    return lax.all_to_all(back, "gz", split_axis=0, concat_axis=2, tiled=True)


def shards(iterate, source, region, fixed_mask):
    zcells = iterate.shape[0]
    order = zcells * lax.axis_size("gz")
    upad = slab_rimmed(iterate)
    bsq = (
        (upad[2:, 1:-1, 1:-1] - iterate) ** 2
        + (upad[1:-1, 2:, 1:-1] - iterate) ** 2
        + (upad[1:-1, 1:-1, 2:] - iterate) ** 2
    )
    nu = reluct(bsq, region)
    nu_pad = with_halo(nu - 1.0, (("gz", 0), ("gy", 1)), 1) + 1.0
    nu_pad = jnp.pad(nu_pad, ((0, 0), (0, 0), (1, 1)), constant_values=1.0)
    terms = face_terms(nu_pad)
    applied = stencil(iterate, upad, terms)
    resid = -jnp.where(
        fixed_mask == 1, iterate, applied - source * (region == 1).astype(jnp.float32)
    )
    column = lax.psum(jnp.sum(nu, axis=0), "gz") / order
    nbpad = with_halo(column - 1.0, (("gy", 0),), 1) + 1.0
    nbpad = jnp.pad(nbpad, ((0, 0), (1, 1)), constant_values=1.0)
    table = dst_table(order)
    count = order * iterate.shape[1] * lax.axis_size("gy") * iterate.shape[2]
    beta = jnp.sqrt(lax.psum(jnp.sum(resid * resid), ("gz", "gy")) + 1e-06)
    vector = resid / beta
    zdir = precondition(vector, nbpad, table)
    image = jnp.where(fixed_mask == 1, zdir, stencil(zdir, slab_rimmed(zdir), terms))
    h_one = lax.psum(jnp.sum(vector * image), ("gz", "gy"))
    ortho = image - h_one * vector
    h_sq = lax.psum(jnp.sum(ortho * ortho), ("gz", "gy"))
    denom = h_one * h_one + h_sq + 1e-06
    gamma = beta * h_one / denom
    residual_rms = beta / jnp.sqrt(jnp.float32(count))
    return (gamma * zdir, resid - gamma * image, residual_rms)


def solution(mesh):
    placed = (P("gz", "gy", None), P("gz", "gy", None), P("gz", "gy", None), P("gz", "gy", None))
    return jax.shard_map(
        shards,
        mesh=mesh,
        in_specs=placed,
        out_specs=(P("gz", "gy", None), P("gz", "gy", None), P()),
        check_vma=False,
    )
```

profile of v0, /device:TPU:1, one launch (start us, length us, event | category | flops | bytes accessed | tf_op | source)
XLA Modules:
  0.0 589.6 jit_solution(473106492425982772)
XLA Ops:
  1.4 4.5 collective-permute-start.1
  7.9 3.3 collective-permute-done
  14.9 4.2 collective-permute-start.3
  34.5 3.8 collective-permute-start.4
  41.1 4.2 collective-permute-start.6
  53.3 5.9 %multiply_reduce_fusion.2 = (f32[]{:T(128)}, f32[16,64,128]{1,0,2:T(8,128)S(1)}, pred[16,64,128]{1,0,2:T(8,128)(4,1)}) fusion(f32[16,64,128]{1,0,2:T(8,128)S(1)} %copy-done.23, f32[16,64,128]{1,0,2:T(8,128)} %copy.138, s32[16,64,128]{1,0,2:T(8,128)} %copy.118, f32[18,66,128]{1,0,2:T(8,128)S(1)} %copy-done.11, f32[18,66,128]{1,0,2:T(8,128)S(1)} %broadcast_add_fusion, ...), kind=kLoop, calls=%fused_computation.116 | loop fusion | flops 4718591 | bytes 13762564 | tf_op jit(solution)/shard_map/reduce_sum | solution.py:133
  59.2 71.4 %psum.28 = f32[]{:T(128)} all-reduce(f32[]{:T(128)} %get-tuple-element.21), channel_id=1, replica_groups=mesh['gz'=32,'gy'=4] {'gz','gy'}, use_global_device_ids=true, to_apply=%region_1.2 | all-reduce | flops 1 | bytes 8 | tf_op jit(solution)/shard_map/psum | solution.py:133
  135.1 5.5 all-to-all-start
  141.9 4.0 collective-permute-start.11
  148.1 123.5 %psum.29 = f32[64,128]{0,1:T(8,128)S(1)} all-reduce(f32[64,128]{0,1:T(8,128)S(1)} %get-tuple-element.19), channel_id=1, replica_groups=mesh['gz'=32,'gy'=4] {'gz'}, use_global_device_ids=true, to_apply=%region_3.4 | all-reduce | flops 8192 | bytes 65536 | tf_op jit(solution)/shard_map/psum | solution.py:128
  278.6 6.0 %fusion.76 = f32[512,64,4]{0,1,2:T(8,128)S(1)} fusion(f32[512,64,4]{1,0,2:T(8,128)S(1)} %bitcast.55, s32[512]{0:T(512)S(1)} %iota_add_fusion), kind=kOutput, calls=%fused_computation.119 | convolution fusion | flops 807927808 | bytes 1050624 | tf_op jit(solution)/shard_map/kj,jyx->kyx/dot_general | solution.py:101
  288.8 9.9 %all-to-all-start.1 = ((f32[32,1,4096]{2,1,0:T(1,128)}), f32[32,1,4096]{2,1,0:T(1,128)}, u32[]{:S(2)}, u32[]{:S(2)}) async-start(f32[32,1,4096]{2,1,0:T(1,128)} %reshape.37), calls=%async_computation.1 | async-start | bytes 1048576 | tf_op jit(solution)/shard_map/all_to_all | solution.py:104
  300.2 4.9 collective-permute-start.8
  323.1 4.5 collective-permute-start.13
  341.0 4.2 collective-permute-start.15
  358.6 4.0 collective-permute-start.17
  372.6 17.5 %all_to_all.72 = f32[32,1,4096]{2,1,0:T(1,128)S(1)} all-to-all(f32[32,1,4096]{2,1,0:T(1,128)S(1)} %reshape.39), channel_id=1, replica_groups=mesh['gz'=32,'gy'=4] {'gz'}, dimensions={0} | all-to-all | bytes 1048576 | tf_op jit(solution)/shard_map/all_to_all | solution.py:107
  392.5 6.0 %fusion.74 = f32[512,64,4]{0,1,2:T(8,128)S(1)} fusion(f32[512,64,4]{1,0,2:T(8,128)S(1)} %bitcast.54, s32[512]{0:T(512)S(1)} %iota_add_fusion), kind=kOutput, calls=%fused_computation.118 | convolution fusion | flops 807927808 | bytes 1050624 | tf_op jit(solution)/shard_map/kj,jyx->kyx/dot_general | solution.py:101
  399.9 15.2 %all_to_all.73 = f32[32,1,4096]{2,1,0:T(1,128)S(1)} all-to-all(f32[32,1,4096]{2,1,0:T(1,128)S(1)} %reshape.41), channel_id=1, replica_groups=mesh['gz'=32,'gy'=4] {'gz'}, dimensions={0} | all-to-all | bytes 1048576 | tf_op jit(solution)/shard_map/all_to_all | solution.py:108
  420.3 3.5 collective-permute-start.19
  426.2 4.4 collective-permute-start.21
  436.9 6.3 %multiply_reduce_fusion.1 = (f32[]{:T(128)}, f32[16,64,128]{1,0,2:T(8,128)}) fusion(pred[16,64,128]{1,0,2:T(8,128)(4,1)S(1)} %copy-done.31, f32[16,64,128]{1,0,2:T(8,128)} %bitcast.43, f32[18,66,128]{1,0,2:T(8,128)} %copy.181, f32[18,66,128]{1,0,2:T(8,128)S(1)} %broadcast_add_fusion, f32[16,64,128]{1,0,2:T(8,128)} %copy.191, f32[16,64,128]{1,0,2:T(8,128)} %copy.190, ...), kind=kLoop, calls=%fused_computation.111 | loop fusion | flops 4718591 | bytes 10962952 | tf_op jit(solution)/shard_map/reduce_sum | solution.py:137
  443.3 70.1 %psum.30 = f32[]{:T(128)} all-reduce(f32[]{:T(128)} %get-tuple-element.12), channel_id=1, replica_groups=mesh['gz'=32,'gy'=4] {'gz','gy'}, use_global_device_ids=true, to_apply=%region_5.6 | all-reduce | flops 1 | bytes 8 | tf_op jit(solution)/shard_map/psum | solution.py:137
  518.1 62.7 %psum.31 = f32[]{:T(128)} all-reduce(f32[]{:T(128)} %multiply_reduce_fusion), channel_id=1, replica_groups=mesh['gz'=32,'gy'=4] {'gz','gy'}, use_global_device_ids=true, to_apply=%region_7.8 | all-reduce | flops 1 | bytes 8 | tf_op jit(solution)/shard_map/psum | solution.py:139
  (199 shorter events, 133.8 us)
Async XLA Ops:
  1.4 6.4 %collective-permute-start.1 = (f32[1,64,128]{2,1,0:T(8,128)S(1)}, f32[1,64,128]{2,1,0:T(8,128)S(1)}, u32[]{:S(2)}, u32[]{:S(2)}) collective-permute-start(f32[1,64,128]{2,1,0:T(8,128)S(1)} %get-tuple-element.48), channel_id=1, source_target_pairs={{0,4},{4,8},{8,12},{12,16},{16,20},{20,24},{24,28},{28,32},{32,36}... | collective-permute-start | bytes 98312 | tf_op jit(solution)/shard_map/ppermute | solution.py:16
  5.9 5.2 collective-permute-start
  13.6 10.2 %collective-permute-start.2 = (f32[18,1,128]{2,1,0:T(1,128)S(1)}, f32[18,1,128]{2,1,0:T(1,128)S(1)}, u32[]{:S(2)}, u32[]{:S(2)}) collective-permute-start(f32[18,1,128]{2,1,0:T(1,128)S(1)} %get-tuple-element.43), channel_id=1, source_target_pairs={{1,0},{2,1},{3,2},{5,4},{6,5},{7,6},{9,8},{10,9},{11,10},{13,12},{... | collective-permute-start | bytes 27656 | tf_op jit(solution)/shard_map/ppermute | solution.py:17
  14.9 8.9 %collective-permute-start.3 = (f32[18,1,128]{2,1,0:T(1,128)S(1)}, f32[18,1,128]{2,1,0:T(1,128)S(1)}, u32[]{:S(2)}, u32[]{:S(2)}) collective-permute-start(f32[18,1,128]{2,1,0:T(1,128)S(1)} %get-tuple-element.42), channel_id=1, source_target_pairs={{0,1},{1,2},{2,3},{4,5},{5,6},{6,7},{8,9},{9,10},{10,11},{12,13},{... | collective-permute-start | bytes 27656 | tf_op jit(solution)/shard_map/ppermute | solution.py:16
  32.5 6.2 %collective-permute-start.5 = (f32[1,64,128]{1,0,2:T(1,128)S(1)}, f32[1,64,128]{1,0,2:T(1,128)S(1)}, u32[]{:S(2)}, u32[]{:S(2)}) collective-permute-start(f32[1,64,128]{1,0,2:T(1,128)S(1)} %get-tuple-element.33), channel_id=1, source_target_pairs={{4,0},{8,4},{12,8},{16,12},{20,16},{24,20},{28,24},{32,28},{36,32}... | collective-permute-start | bytes 98312 | tf_op jit(solution)/shard_map/ppermute | solution.py:17
  34.5 5.1 collective-permute-start.4
  39.7 11.3 %collective-permute-start.7 = (f32[18,1,128]{2,1,0:T(1,128)S(1)}, f32[18,1,128]{2,1,0:T(1,128)S(1)}, u32[]{:S(2)}, u32[]{:S(2)}) collective-permute-start(f32[18,1,128]{2,1,0:T(1,128)S(1)} %get-tuple-element.41), channel_id=1, source_target_pairs={{1,0},{2,1},{3,2},{5,4},{6,5},{7,6},{9,8},{10,9},{11,10},{13,12},{... | collective-permute-start | bytes 27656 | tf_op jit(solution)/shard_map/ppermute | solution.py:17
  41.1 9.8 %collective-permute-start.6 = (f32[18,1,128]{2,1,0:T(1,128)S(1)}, f32[18,1,128]{2,1,0:T(1,128)S(1)}, u32[]{:S(2)}, u32[]{:S(2)}) collective-permute-start(f32[18,1,128]{2,1,0:T(1,128)S(1)} %get-tuple-element.40), channel_id=1, source_target_pairs={{0,1},{1,2},{2,3},{4,5},{5,6},{6,7},{8,9},{9,10},{10,11},{12,13},{... | collective-permute-start | bytes 27656 | tf_op jit(solution)/shard_map/ppermute | solution.py:16
  135.1 136.5 %all-to-all-start = ((f32[32,1,4096]{2,1,0:T(1,128)}), f32[32,1,4096]{2,1,0:T(1,128)S(1)}, u32[]{:S(2)}, u32[]{:S(2)}) async-start(f32[32,1,4096]{2,1,0:T(1,128)} %reshape.35), calls=%async_computation | async-start | bytes 1048576 | tf_op jit(solution)/shard_map/all_to_all | solution.py:103
  140.6 5.4 collective-permute-start.10
  141.9 4.8 collective-permute-start.11
  288.8 21.6 %all-to-all-start.1 = ((f32[32,1,4096]{2,1,0:T(1,128)}), f32[32,1,4096]{2,1,0:T(1,128)}, u32[]{:S(2)}, u32[]{:S(2)}) async-start(f32[32,1,4096]{2,1,0:T(1,128)} %reshape.37), calls=%async_computation.1 | async-start | bytes 1048576 | tf_op jit(solution)/shard_map/all_to_all | solution.py:104
  298.8 8.1 %collective-permute-start.9 = (f32[1,128]{0,1:T(8,128)S(1)}, f32[1,128]{0,1:T(8,128)S(1)}, u32[]{:S(2)}, u32[]{:S(2)}) collective-permute-start(f32[1,128]{0,1:T(8,128)S(1)} %get-tuple-element.51), channel_id=1, source_target_pairs={{1,0},{2,1},{3,2},{5,4},{6,5},{7,6},{9,8},{10,9},{11,10},{13,12},{... | collective-permute-start | bytes 1544 | tf_op jit(solution)/shard_map/ppermute | solution.py:17
  300.2 6.7 %collective-permute-start.8 = (f32[1,128]{0,1:T(8,128)S(1)}, f32[1,128]{0,1:T(8,128)S(1)}, u32[]{:S(2)}, u32[]{:S(2)}) collective-permute-start(f32[1,128]{0,1:T(8,128)S(1)} %get-tuple-element.50), channel_id=1, source_target_pairs={{0,1},{1,2},{2,3},{4,5},{5,6},{6,7},{8,9},{9,10},{10,11},{12,13},{... | collective-permute-start | bytes 1544 | tf_op jit(solution)/shard_map/ppermute | solution.py:16
  320.1 7.5 %collective-permute-start.12 = (f32[16,1,128]{2,0,1:T(8,128)S(1)}, f32[16,1,128]{2,0,1:T(8,128)S(1)}, u32[]{:S(2)}, u32[]{:S(2)}) collective-permute-start(f32[16,1,128]{2,0,1:T(8,128)S(1)} %copy.149), channel_id=1, source_target_pairs={{1,0},{2,1},{3,2},{5,4},{6,5},{7,6},{9,8},{10,9},{11,10},{13,12},{... | collective-permute-start | bytes 24584 | tf_op jit(solution)/shard_map/ppermute | solution.py:17
  323.1 6.0 %collective-permute-start.13 = (f32[16,1,128]{2,0,1:T(8,128)S(1)}, f32[16,1,128]{2,0,1:T(8,128)S(1)}, u32[]{:S(2)}, u32[]{:S(2)}) collective-permute-start(f32[16,1,128]{2,0,1:T(8,128)S(1)} %copy.151), channel_id=1, source_target_pairs={{0,1},{1,2},{2,3},{4,5},{5,6},{6,7},{8,9},{9,10},{10,11},{12,13},{... | collective-permute-start | bytes 24584 | tf_op jit(solution)/shard_map/ppermute | solution.py:16
  338.1 7.1 %collective-permute-start.14 = (f32[16,1,128]{2,0,1:T(8,128)S(1)}, f32[16,1,128]{2,0,1:T(8,128)S(1)}, u32[]{:S(2)}, u32[]{:S(2)}) collective-permute-start(f32[16,1,128]{2,0,1:T(8,128)S(1)} %copy.155), channel_id=1, source_target_pairs={{1,0},{2,1},{3,2},{5,4},{6,5},{7,6},{9,8},{10,9},{11,10},{13,12},{... | collective-permute-start | bytes 24584 | tf_op jit(solution)/shard_map/ppermute | solution.py:17
  341.0 5.6 collective-permute-start.15
  355.6 6.9 %collective-permute-start.16 = (f32[16,1,128]{2,0,1:T(8,128)S(1)}, f32[16,1,128]{2,0,1:T(8,128)S(1)}, u32[]{:S(2)}, u32[]{:S(2)}) collective-permute-start(f32[16,1,128]{2,0,1:T(8,128)S(1)} %copy.161), channel_id=1, source_target_pairs={{1,0},{2,1},{3,2},{5,4},{6,5},{7,6},{9,8},{10,9},{11,10},{13,12},{... | collective-permute-start | bytes 24584 | tf_op jit(solution)/shard_map/ppermute | solution.py:17
  358.6 5.4 collective-permute-start.17
  417.9 6.5 %collective-permute-start.18 = (f32[1,64,128]{1,0,2:T(1,128)S(1)}, f32[1,64,128]{1,0,2:T(1,128)S(1)}, u32[]{:S(2)}, u32[]{:S(2)}) collective-permute-start(f32[1,64,128]{1,0,2:T(1,128)S(1)} %bitcast.56), channel_id=1, source_target_pairs={{4,0},{8,4},{12,8},{16,12},{20,16},{24,20},{28,24},{32,28},{36,32}... | collective-permute-start | bytes 98312 | tf_op jit(solution)/shard_map/ppermute | solution.py:17
  420.3 4.5 collective-permute-start.19
  424.9 5.8 collective-permute-start.20
  426.2 5.2 collective-permute-start.21
  (34 other events, 480.5 us)
where the time goes:
time: 600 us; the launch traced here: 590 us
  blocking collectives  360 us (60%)
  starting transfers between devices  78.2 us (13%)
  local copies, waits for them, and re-layouts  69.9 us (12%)
  other arithmetic  54 us (9%)
  matrix products  11.9 us (2%)
  waiting for transfers between devices  8.73 us (1%)
  between operations  6.41 us (1%)
    psum x1, blocking collectives, shards(): column = lax.psum(jnp.sum(nu, axis=0), 'gz') / order  123 us
    psum x1, blocking collectives, shards(): beta = jnp.sqrt(lax.psum(jnp.sum(resid * resid), ('gz', 'gy')) + 1e-06)  71.4 us
    psum x1, blocking collectives, shards(): h_one = lax.psum(jnp.sum(vector * image), ('gz', 'gy'))  70.1 us
    psum x1, blocking collectives, shards(): h_sq = lax.psum(jnp.sum(ortho * ortho), ('gz', 'gy'))  62.7 us
    ppermute x11, starting transfers between devices, with_halo(): before = lax.ppermute(last, axis, up)  46.1 us
    unnamed x89, local copies, waits for them, and re-layouts  35.5 us
    all_to_all x1, blocking collectives, precondition(): lax.all_to_all(smoothed, 'gz', split_axis=2, concat_axis=0, tiled=True)  17.5 us
    ppermute x11, starting transfers between devices, with_halo(): after = lax.ppermute(first, axis, down)  16.8 us
  transfers between devices with their start and end apart: 24, of which 6 were waited for; matrix products, arithmetic and copies ran while one was open for 4% of the time, Pallas kernels for 0%

commit v1 on v0

v1 whole, which is shorter than its diff:
```python
import functools

import jax
import jax.numpy as jnp
import ml_dtypes
import numpy as np
from jax import lax
from jax.experimental import pallas as pl
from jax.experimental.pallas import tpu as pltpu
from jax.sharding import PartitionSpec as P

F32 = jnp.float32
BF16 = jnp.bfloat16
NZ, NY, NX = 512, 256, 128
GZ, GY = 32, 4
ZC, YC = NZ // GZ, NY // GY
FR = YC + 16
WR, WC, RING = 23, 22, 3
LANES = 512
YP, XP = 4, 8
ROW0 = (0, 17, 33, 49)
VMEM_LIMIT = 40 * 1024 * 1024


def tables():
    index = np.arange(NZ, dtype=np.int64)
    phase = (index[:, None] + 1) * (index[None, :] + 1) % (2 * (NZ + 1))
    table = np.sqrt(2.0 / (NZ + 1)) * np.sin(np.pi * phase / (NZ + 1))
    table = table.astype(np.float32)
    high = table.astype(ml_dtypes.bfloat16)
    low = (table - high.astype(np.float32)).astype(ml_dtypes.bfloat16)
    lam = 2.0 - 2.0 * np.cos(np.pi * (index + 1.0) / (NZ + 1))
    lam = np.broadcast_to(lam.astype(np.float32)[:, None], (NZ, 128))
    return high, low, np.ascontiguousarray(lam)


def lane_iota(shape):
    return lax.broadcasted_iota(jnp.int32, shape, len(shape) - 1)


def roll(value, shift, axis):
    return pltpu.roll(value, shift % value.shape[axis], axis)


def halo_pack(first_it, last_it, zlo, zhi, first_src, last_src, first_reg, last_reg,
              first_msk, last_msk, down, up):
    for out, it, src, reg, msk, rows, low in (
        (down, first_it, first_src, first_reg, first_msk, 0, 0),
        (up, last_it, last_src, last_reg, last_msk, YC - 8, 4),
    ):
        out[0] = zlo[0, rows:rows + 8, :]
        out[1:17] = it[...]
        out[17] = zhi[0, rows:rows + 8, :]
        out[18] = zhi[1, rows:rows + 8, :]
        for pair in range(8):
            out[19 + pair, 0:4] = src[2 * pair, low:low + 4, :]
            out[19 + pair, 4:8] = src[2 * pair + 1, low:low + 4, :]
        out[27] = reg[0].astype(F32)
        out[28] = msk[0].astype(F32)


def segments(block):
    found = []
    for row in range(WR):
        start = (WC * (row - RING)) % LANES
        begin, end = max(start, 128 * block), min(start + WC, 128 * block + 128)
        if begin < end:
            found.append((begin - 128 * block, row))
    return sorted(found)


def residual_kernel(it, zlo, zhi, lo, hi, src, reg, msk, chunks, nu, resid, field, rows):
    group = lax.axis_index("gz")
    mid = slice(8, 8 + YC)
    field[0, mid] = zlo[0]
    field[1:17, mid] = it[...]
    field[17:19, mid] = zhi[...]
    field[:, 0:8] = lo[0:19]
    field[:, 8 + YC:] = hi[0:19]
    region = jnp.concatenate([lo[27], reg[0].astype(F32), hi[27]], axis=0)
    fixed = jnp.concatenate([lo[28], msk[0].astype(F32), hi[28]], axis=0)
    lane = lane_iota((FR, 128))
    first, last = lane == 0, lane == 127
    iron, copper, held = region == 2.0, region == 1.0, fixed == 1.0

    def nu_plane(p, total):
        u = field[p]
        dz = field[p + 1] - u
        dy = roll(u, -1, 0) - u
        dx = jnp.where(last, 0.0, roll(u, -1, 1)) - u
        bsq = dz * dz + dy * dy + dx * dx
        bsq = bsq * bsq
        outside = ((p == 0) & (group == 0)) | ((p == 17) & (group == GZ - 1))
        value = jnp.where(iron, 0.05 + bsq / (bsq + 9.0), 1.0)
        value = jnp.where(outside, 1.0, value)
        nu[p] = value
        inner = (p > 0) & (p < 17)
        return total + jnp.where(inner, value, 0.0)

    total = lax.fori_loop(0, 18, nu_plane, jnp.zeros((FR, 128), F32))

    def resid_plane(z, carry):
        u, n = field[z + 1], nu[z + 1]
        uz, nz = field[z + 2], nu[z + 2]
        ub, nb = field[z], nu[z]
        flow = 0.5 * (n + nz) * (u - uz) + 0.5 * (n + nb) * (u - ub)
        fy = 0.5 * (n + roll(n, -1, 0)) * (u - roll(u, -1, 0))
        flow = flow + (fy - roll(fy, 1, 0))
        nx = jnp.where(last, 1.0, roll(n, -1, 1))
        ux = jnp.where(last, 0.0, roll(u, -1, 1))
        fx = 0.5 * (n + nx) * (u - ux)
        flow = flow + (fx - jnp.where(first, -0.5 * (n + 1.0) * u, roll(fx, 1, 1)))
        half = 4 * lax.rem(z, 2)
        before = lo[19 + lax.div(z, 2), pl.ds(half, 4), :]
        after = hi[19 + lax.div(z, 2), pl.ds(half, 4), :]
        drive = jnp.concatenate([before, before, src[z], after, after], axis=0)
        value = -jnp.where(held, u, flow - jnp.where(copper, drive, 0.0))
        rows[pl.ds(pl.multiple_of(z * FR, FR), FR), :] = value
        resid[z] = value[mid]
        return carry

    lax.fori_loop(0, ZC, resid_plane, 0)
    faces = 2.0 * total + 0.5 * (
        roll(total, -1, 0) + roll(total, 1, 0)
        + jnp.where(last, float(ZC), roll(total, -1, 1))
        + jnp.where(first, float(ZC), roll(total, 1, 1))
    )
    rows[16 * FR:17 * FR, :] = total
    rows[17 * FR:18 * FR, :] = faces
    rows[18 * FR:24 * FR, :] = jnp.zeros((6 * FR, 128), F32)

    lane = lane_iota((8, 128))
    for yp in range(YP):
        for tile in range(3):
            turned = []
            for row in range(WR):
                at = ROW0[yp] + row + 4
                line = rows[pl.ds(8 * tile * FR + at, 8, stride=FR), :]
                turned.append(roll(line, WC * (row - RING) + RING, 1))
            for block in range(4):
                parts = segments(block)
                for xp in range(XP):
                    place = (lane - 16 * xp) & 127
                    value = turned[parts[0][1]]
                    for begin, row in parts[1:]:
                        value = jnp.where(place >= begin, turned[row], value)
                    value = roll(value, -16 * xp, 1)
                    if tile < 2:
                        at = 16 * block + 8 * tile
                        chunks[yp * XP + xp, at:at + 8, :] = value
                    else:
                        at = 64 + 2 * block
                        chunks[yp * XP + xp, at:at + 2, :] = value[0:2]


def product(high, low, right_high, right_low):
    dot = functools.partial(jnp.dot, preferred_element_type=F32)
    return dot(high, right_high) + (dot(high, right_low) + dot(low, right_high))


def modes_kernel(got, high, low, lam, out, lines, smooth_high, smooth_low, back):
    group, column = lax.axis_index("gz"), lax.axis_index("gy")
    yp, xp = lax.div(group, XP), lax.rem(group, XP)
    s_high, s_low = high[...], low[...]
    for block in range(4):
        value = got[:, 16 * block:16 * block + 16, :].reshape(NZ, 128)
        v_high = value.astype(BF16)
        v_low = (value - v_high.astype(F32)).astype(BF16)
        lines[:, 128 * block:128 * block + 128] = product(s_high, s_low, v_high, v_low)

    sums = jnp.sum(got[:, 64:72, :], axis=0) * (1.0 / NZ)
    mean = jnp.concatenate([sums[2 * b:2 * b + 1] for b in range(4)], axis=1)
    faces = jnp.concatenate([sums[2 * b + 1:2 * b + 2] for b in range(4)], axis=1)
    spot = (lane_iota((1, LANES)) + RING * WC) & (LANES - 1)
    row = (spot * 2979) >> 16
    col = spot - row * WC
    ypos = column * YC + 16 * yp + jnp.where(yp > 0, 1, 0) + row - 4
    xpos = 16 * xp - RING + col
    inside = (row < WR) & (xpos >= 0) & (xpos < NX) & (ypos >= 0) & (ypos < NY)
    right = 0.5 * (mean + roll(mean, -1, 1))
    left = roll(right, 1, 1)
    above = 0.5 * (mean + roll(mean, -WC, 1))
    below = roll(above, WC, 1)

    def smooth(step, carry):
        at = pl.ds(pl.multiple_of(step * 32, 32), 32)
        vhat = lines[at, :]
        lam_rows = lam[at, :]
        lam_rows = jnp.concatenate([lam_rows] * 4, axis=1)
        factor = jnp.where(inside, 0.6 / (faces + lam_rows * mean), 0.0)
        w = factor * vhat
        for _ in range(3):
            near = (
                above * roll(w, -WC, 1) + below * roll(w, WC, 1)
                + right * roll(w, -1, 1) + left * roll(w, 1, 1)
            )
            w = 0.4 * w + factor * (vhat + near)
        w = w[:, :384]
        w_high = w.astype(BF16)
        smooth_high[at, :] = w_high
        smooth_low[at, :] = (w - w_high.astype(F32)).astype(BF16)
        return carry

    lax.fori_loop(0, NZ // 32, smooth, 0)

    spot = lane_iota((384, 384))
    own = jnp.where(yp == 0, 1, 0)
    halo = jnp.where(yp == 0, 0, 16)
    pick = jnp.where(spot < 256, own + (spot >> 4), halo) * WC + RING + (spot & 15)
    choose = jnp.where(lax.broadcasted_iota(jnp.int32, (384, 384), 0) == pick, 1.0, 0.0)
    choose = choose.astype(BF16)
    w_high = jnp.dot(smooth_high[...], choose, preferred_element_type=F32).astype(BF16)
    w_low = jnp.dot(smooth_low[...], choose, preferred_element_type=F32).astype(BF16)
    back[8:8 + NZ, :] = product(s_high, s_low, w_high, w_low)
    back[0:8, :] = jnp.zeros((8, 384), F32)
    back[8 + NZ:, :] = jnp.zeros((8, 384), F32)

    sub = lax.broadcasted_iota(jnp.int32, (8, 128), 0)
    pattern = (((lane_iota((8, 128)) >> 4) + sub) & 7) == 0
    for peer in range(GZ):
        at = 8 + ZC * peer
        for block in range(2):
            lanes = slice(128 * block, 128 * block + 128)
            out[peer, 16 * block:16 * block + 16, :] = back[at:at + ZC, lanes]
            out[peer, 32 + block:33 + block, :] = back[at - 1:at, lanes]
            out[peer, 34 + block:35 + block, :] = back[at + ZC:at + ZC + 1, lanes]
            piece = back[at + 8 * block:at + 8 * block + 8, 256:384]
            piece = jnp.sum(jnp.where(pattern, piece, 0.0), axis=0, keepdims=True)
            out[peer, 36 + block:37 + block, :] = piece
        out[peer, 38:40, :] = jnp.zeros((2, 128), F32)


def image_kernel(got, nu, resid, msk, zdir, image, sums, frame):
    lane = lane_iota((8, 128))
    places = [(lane >> 4) == k for k in range(8)]

    def spread(tiles, jj):
        value = tiles[0]
        for xp in range(1, XP):
            value = jnp.where(places[(jj + xp) % 8], tiles[xp], value)
        return roll(value, -16 * jj, 1)

    for yp in range(YP):
        for block in range(2):
            for tile in range(2):
                at = 16 * block + 8 * tile
                tiles = [
                    roll(got[yp * XP + xp, at:at + 8, :], 16 * xp, 1) for xp in range(XP)
                ]
                for jj in range(8):
                    y = 8 + 16 * yp + 8 * block + jj
                    frame[pl.ds((1 + 8 * tile) * FR + y, 8, stride=FR), :] = spread(tiles, jj)
        tiles = [roll(got[yp * XP + xp, 32:40, :], 16 * xp, 1) for xp in range(XP)]
        for jj in range(8):
            value = spread(tiles, jj)
            y = 8 + 16 * yp + jj
            for k in range(2):
                frame[y + 8 * k:y + 8 * k + 1, :] = value[k:k + 1]
                at = 17 * FR + y + 8 * k
                frame[at:at + 1, :] = value[2 + k:3 + k]

    sub = lax.broadcasted_iota(jnp.int32, (8, 128), 0)
    turn = ((lane >> 4) + sub) & 7
    for yp, y in ((0, 7), (YP - 1, 8 + YC)):
        for tile in range(2):
            value = jnp.zeros((8, 128), F32)
            for xp in range(XP):
                line = got[yp * XP + xp, 36 + tile:37 + tile, :]
                line = roll(jnp.broadcast_to(line, (8, 128)), 16 * xp, 1)
                value = jnp.where(turn == xp, line, value)
            value = pltpu.roll(value, 0, 1, stride=16, stride_axis=0)
            frame[pl.ds((1 + 8 * tile) * FR + y, 8, stride=FR), :] = value

    lane = lane_iota((YC, 128))
    first, last = lane == 0, lane == 127
    held = msk[0] == 1

    def plane(z, carry):
        at = (z + 1) * FR + 8
        d, n = frame[pl.ds(at, YC), :], nu[z + 1, 8:8 + YC]

        def flux(shift, other):
            return 0.5 * (n + other) * (d - frame[pl.ds(at + shift, YC), :])

        flow = flux(FR, nu[z + 2, 8:8 + YC]) + flux(-FR, nu[z, 8:8 + YC])
        flow = flow + flux(1, nu[z + 1, 9:9 + YC]) + flux(-1, nu[z + 1, 7:7 + YC])
        nx = jnp.where(last, 1.0, roll(n, -1, 1))
        dx = jnp.where(last, 0.0, roll(d, -1, 1))
        fx = 0.5 * (n + nx) * (d - dx)
        flow = flow + (fx - jnp.where(first, -0.5 * (n + 1.0) * d, roll(fx, 1, 1)))
        value = jnp.where(held, d, flow)
        zdir[z] = d
        image[z] = value
        r = resid[z]
        rr, ri, ii = carry
        return rr + r * r, ri + r * value, ii + value * value

    zero = jnp.zeros((YC, 128), F32)
    parts = lax.fori_loop(0, ZC, plane, (zero, zero, zero))
    line = lane_iota((1, 128))
    packed = jnp.zeros((1, 128), F32)
    for k, part in enumerate(parts):
        packed = jnp.where(line == k, jnp.sum(part), packed)
    sums[...] = jnp.broadcast_to(packed[None], sums.shape)


def output_kernel(sums, zdir, image, resid, correction, lin_residual, rms):
    total = jnp.sum(sums[...], axis=0)
    beta_sq = total[0:1, 0:1] + 1e-06
    beta = jnp.sqrt(beta_sq)
    h_one = total[0:1, 1:2] / beta_sq
    denom = total[0:1, 2:3] / beta_sq - h_one * h_one * (1e-06 / beta_sq) + 1e-06
    gamma = h_one / denom
    correction[...] = zdir[...] * gamma[None]
    lin_residual[...] = resid[...] - gamma[None] * image[...]
    rms[...] = jnp.broadcast_to(beta * (1.0 / np.sqrt(float(NZ * NY * NX))), rms.shape)


def call(kernel, out_shape, scratch=(), in_specs=None):
    extra = {} if in_specs is None else {"in_specs": in_specs, "grid": (1,)}
    return pl.pallas_call(
        kernel,
        out_shape=out_shape,
        scratch_shapes=scratch,
        compiler_params=pltpu.CompilerParams(vmem_limit_bytes=VMEM_LIMIT),
        **extra,
    )


def struct(*shape):
    return jax.ShapeDtypeStruct(shape, F32)


def whole(*shape):
    return pl.BlockSpec(shape, lambda i: (0,) * len(shape))


def shards(iterate, source, region, fixed_mask):
    up_z = [(i, i + 1) for i in range(GZ - 1)]
    down_z = [(i + 1, i) for i in range(GZ - 1)]
    up_y = [(i, i + 1) for i in range(GY - 1)]
    down_y = [(i + 1, i) for i in range(GY - 1)]
    zlo = lax.ppermute(iterate[ZC - 1:ZC], "gz", up_z)
    zhi = lax.ppermute(iterate[0:2], "gz", down_z)

    def edge(planes, place):
        return pl.BlockSpec((planes, 8, 128), lambda i: (0, place, 0))

    both = [edge(ZC, 0), edge(ZC, YC // 8 - 1)]
    flat = [edge(1, 0), edge(1, YC // 8 - 1)]
    down, up = call(
        halo_pack,
        (struct(29, 8, 128), struct(29, 8, 128)),
        in_specs=both + [whole(1, YC, 128), whole(2, YC, 128)] + both + flat + flat,
    )(iterate, iterate, zlo, zhi, source, source, region, region, fixed_mask, fixed_mask)
    lo = lax.ppermute(up, "gy", up_y)
    hi = lax.ppermute(down, "gy", down_y)

    cells = (ZC, YC, 128)
    chunks, nu, resid = call(
        residual_kernel,
        (struct(GZ, 72, 128), struct(18, FR, 128), struct(*cells)),
        scratch=[pltpu.VMEM((19, FR, 128), F32), pltpu.VMEM((24 * FR, 128), F32)],
        in_specs=[
            whole(*cells), whole(1, YC, 128), whole(2, YC, 128), whole(29, 8, 128),
            whole(29, 8, 128), whole(*cells), whole(1, YC, 128), whole(1, YC, 128),
        ],
    )(iterate, zlo, zhi, lo, hi, source, region, fixed_mask)
    windows = lax.all_to_all(chunks, "gz", 0, 0, tiled=True)
    high, low, lam = tables()
    sent = call(
        modes_kernel,
        struct(GZ, 40, 128),
        scratch=[
            pltpu.VMEM((NZ, LANES), F32), pltpu.VMEM((NZ, 384), BF16),
            pltpu.VMEM((NZ, 384), BF16), pltpu.VMEM((NZ + 16, 384), F32),
        ],
    )(windows, jnp.asarray(high), jnp.asarray(low), jnp.asarray(lam))
    returned = lax.all_to_all(sent, "gz", 0, 0, tiled=True)
    zdir, image, sums = call(
        image_kernel,
        (struct(*cells), struct(*cells), struct(GZ * GY, 1, 128)),
        scratch=[pltpu.VMEM((18 * FR, 128), F32)],
        in_specs=[
            whole(GZ, 40, 128), whole(18, FR, 128), whole(*cells), whole(1, YC, 128),
        ],
    )(returned, nu, resid, fixed_mask)
    sums = lax.all_to_all(sums, ("gz", "gy"), 0, 0, tiled=True)
    correction, lin_residual, rms = call(
        output_kernel, (struct(*cells), struct(*cells), struct(1, 128))
    )(sums, zdir, image, resid)
    return correction, lin_residual, rms[0, 0]


def solution(mesh):
    placed = (P("gz", "gy", None),) * 4
    return jax.shard_map(
        shards,
        mesh=mesh,
        in_specs=placed,
        out_specs=(P("gz", "gy", None), P("gz", "gy", None), P()),
        check_vma=False,
    )
```

time: 600 us -> 108 us (0.18); the launches traced: 590 us -> 108 us
  blocking collectives: 360 us -> 61.4 us
  starting transfers between devices: 78.2 us -> 11.2 us
  local copies, waits for them, and re-layouts: 69.9 us -> 5.8 us
  other arithmetic: 54 us -> 0 us
  Pallas kernels: 0 us -> 21.8 us
  matrix products: 11.9 us -> 0 us
    psum x4 -> x0, blocking collectives: 328 us -> none  [the longest x1 123 us: shards(): column = lax.psum(jnp.sum(nu, axis=0), 'gz') / order]
    ppermute x22 -> x4, starting transfers between devices: 62.9 us -> 11.2 us  [the longest x1 3.55 us: shards(): lo = lax.ppermute(up, 'gy', up_y)]
    unnamed x89 -> x16, local copies, waits for them, and re-layouts: 35.5 us -> 4.19 us
    all_to_all x2 -> x3, blocking collectives: 32.7 us -> 61.4 us  [the longest x1 29 us: shards(): windows = lax.all_to_all(chunks, 'gz', 0, 0, tiled=True)]
    pallas_call x0 -> x5, Pallas kernels: none -> 21.8 us  [the longest x1 10.3 us: shards(): call(modes_kernel, struct(GZ, 40, 128), scratch=[pltpu.VMEM((NZ, LANES),...]
    reduce_sum x4 -> x0, other arithmetic: 17.8 us -> none  [the longest x1 6.33 us: shards(): h_one = lax.psum(jnp.sum(vector * image), ('gz', 'gy'))]
    concatenate x11 -> x0, other arithmetic: 15.8 us -> none  [with_halo(): array = jnp.concatenate([before, array, after], axis=dim)]
    all_to_all x2 -> x0, starting transfers between devices: 15.3 us -> none  [the longest x1 9.86 us: precondition(): modes = lax.all_to_all(vhat, 'gz', split_axis=0, concat_axis=2, tiled=True)]
  transfers between devices with their start and end apart: 24 -> 4, of which waited for: 6 -> 3; matrix products, arithmetic and copies ran while one was open for 4% -> 1% of each run, Pallas kernels for 0% -> 0%
where the time goes in v1:
time: 108 us
  blocking collectives  61.4 us (57%)
  Pallas kernels  21.8 us (20%)
  starting transfers between devices  11.2 us (10%)
  waiting for transfers between devices  6.62 us (6%)
  local copies, waits for them, and re-layouts  5.8 us (5%)
    all_to_all x1, blocking collectives, shards(): windows = lax.all_to_all(chunks, 'gz', 0, 0, tiled=True)  29 us
    all_to_all x1, blocking collectives, shards(): returned = lax.all_to_all(sent, 'gz', 0, 0, tiled=True)  16.7 us
    all_to_all x1, blocking collectives, shards(): sums = lax.all_to_all(sums, ('gz', 'gy'), 0, 0, tiled=True)  15.7 us
    pallas_call x1, Pallas kernels, shards(): call(modes_kernel, struct(GZ, 40, 128), scratch=[pltpu.VMEM((NZ, LANES),...  10.3 us
    pallas_call x1, Pallas kernels, shards(): call(residual_kernel, (struct(GZ, 72, 128), struct(18, FR, 128), struct(*...  5.91 us
    unnamed x16, local copies, waits for them, and re-layouts  4.19 us
    ppermute x1, waiting for transfers between devices, shards(): hi = lax.ppermute(down, 'gy', down_y)  4.19 us
    pallas_call x1, Pallas kernels, shards(): call(image_kernel, (struct(*cells), struct(*cells), struct(GZ * GY, 1, 12...  4.06 us
  transfers between devices with their start and end apart: 4, of which 3 were waited for; matrix products, arithmetic and copies ran while one was open for 1% of the time, Pallas kernels for 0%

profile of v1, /device:TPU:1, one launch (start us, length us, event | category | flops | bytes accessed | tf_op | source)
XLA Modules:
  0.0 107.6 jit_solution(5973917142222970710)
XLA Ops:
  0.6 0.8 slice.10
  1.5 3.3 %collective-permute-start.1 = (f32[2,64,128]{2,1,0:T(8,128)S(1)}, f32[2,64,128]{2,1,0:T(8,128)S(1)}, u32[]{:S(2)}, u32[]{:S(2)}) collective-permute-start(f32[2,64,128]{2,1,0:T(8,128)S(1)} %slice.10), channel_id=1, source_target_pairs={{4,0},{8,4},{12,8},{16,12},{20,16},{24,20},{28,24},{32,28},{36,32}... | collective-permute-start | bytes 196616 | tf_op jit(solution)/shard_map/ppermute | solution.py:344
  4.8 0.8 slice.9
  5.6 3.1 %collective-permute-start = (f32[1,64,128]{2,1,0:T(8,128)S(1)}, f32[1,64,128]{2,1,0:T(8,128)S(1)}, u32[]{:S(2)}, u32[]{:S(2)}) collective-permute-start(f32[1,64,128]{2,1,0:T(8,128)S(1)} %slice.9), channel_id=1, source_target_pairs={{0,4},{4,8},{8,12},{12,16},{16,20},{20,24},{24,28},{28,32},{32,36}... | collective-permute-start | bytes 98312 | tf_op jit(solution)/shard_map/ppermute | solution.py:343
  8.7 1.0 collective-permute-done.zlo
  9.7 1.0 copy-done
  10.7 1.0 copy-done.2
  11.8 1.0 copy-done.3
  12.8 1.0 copy-done.4
  13.9 3.5 %collective-permute-start.2 = (f32[29,8,128]{2,1,0:T(8,128)S(1)}, f32[29,8,128]{2,1,0:T(8,128)S(1)}, u32[]{:S(2)}, u32[]{:S(2)}) collective-permute-start(f32[29,8,128]{2,1,0:T(8,128)S(1)} %get-tuple-element.14), channel_id=1, source_target_pairs={{0,1},{1,2},{2,3},{4,5},{5,6},{6,7},{8,9},{9,10},{10,11},{12,13},{... | collective-permute-start | bytes 356360 | tf_op jit(solution)/shard_map/ppermute | solution.py:356
  17.4 1.3 %collective-permute-start.3 = (f32[29,8,128]{2,1,0:T(8,128)S(1)}, f32[29,8,128]{2,1,0:T(8,128)S(1)}, u32[]{:S(2)}, u32[]{:S(2)}) collective-permute-start(f32[29,8,128]{2,1,0:T(8,128)S(1)} %get-tuple-element.15), channel_id=1, source_target_pairs={{1,0},{2,1},{3,2},{5,4},{6,5},{7,6},{9,8},{10,9},{11,10},{13,12},{... | collective-permute-start | bytes 356360 | tf_op jit(solution)/shard_map/ppermute | solution.py:357
  18.7 1.4 %collective-permute-done.2.lo = f32[29,8,128]{2,1,0:T(8,128)S(1)} collective-permute-done((f32[29,8,128]{2,1,0:T(8,128)S(1)}, f32[29,8,128]{2,1,0:T(8,128)S(1)}, u32[]{:S(2)}, u32[]{:S(2)}) %collective-permute-start.2) | collective-permute-done | bytes 118816 | tf_op jit(solution)/shard_map/ppermute | solution.py:356
  20.2 4.2 %collective-permute-done.3.hi = f32[29,8,128]{2,1,0:T(8,128)S(1)} collective-permute-done((f32[29,8,128]{2,1,0:T(8,128)S(1)}, f32[29,8,128]{2,1,0:T(8,128)S(1)}, u32[]{:S(2)}, u32[]{:S(2)}) %collective-permute-start.3) | collective-permute-done | bytes 118816 | tf_op jit(solution)/shard_map/ppermute | solution.py:357
  24.4 5.9 %shard_map.95 = (f32[32,72,128]{2,1,0:T(8,128)S(1)}, f32[18,80,128]{2,1,0:T(8,128)S(1)}, f32[16,64,128]{2,1,0:T(8,128)S(1)}) custom-call(f32[16,64,128]{2,1,0:T(8,128)S(1)} %copy-done.2, f32[1,64,128]{2,1,0:T(8,128)S(1)} %collective-permute-done.zlo, f32[2,64,128]{2,1,0:T(8,128)S(1)} %collective-permute-done.1.zhi, ...), custom_call_target="tpu_custom_call" | custom-call | tf_op jit(solution)/shard_map/pallas_call | solution.py:360
  30.3 0.0 copy-start.5
  30.3 0.0 copy-start.6
  30.3 0.0 copy-start.7
  30.3 29.0 %all_to_all.15.got = f32[32,72,128]{2,1,0:T(8,128)S(1)} all-to-all(f32[32,72,128]{2,1,0:T(8,128)S(1)} %get-tuple-element.16), channel_id=1, replica_groups=mesh['gz'=32,'gy'=4] {'gz'}, dimensions={0} | all-to-all | bytes 2359296 | tf_op jit(solution)/shard_map/all_to_all | solution.py:369
  59.3 10.3 %shard_map.96 = f32[32,40,128]{2,1,0:T(8,128)S(1)} custom-call(f32[32,72,128]{2,1,0:T(8,128)S(1)} %all_to_all.15.got, bf16[512,512]{1,0:T(8,128)(2,1)S(1)} %copy-done.6, bf16[512,512]{1,0:T(8,128)(2,1)S(1)} %copy-done.5, f32[512,128]{1,0:T(8,128)S(1)} %copy-done.7), custom_call_target="tpu_custom_call" | custom-call | tf_op jit(solution)/shard_map/pallas_call | solution.py:371
  69.7 0.0 copy-start.1
  69.7 16.7 %all_to_all.16.got = f32[32,40,128]{2,1,0:T(8,128)S(1)} all-to-all(f32[32,40,128]{2,1,0:T(8,128)S(1)} %shard_map.96), channel_id=1, replica_groups=mesh['gz'=32,'gy'=4] {'gz'}, dimensions={0} | all-to-all | bytes 1310720 | tf_op jit(solution)/shard_map/all_to_all | solution.py:379
  86.4 4.1 %shard_map.97 = (f32[16,64,128]{2,1,0:T(8,128)S(1)}, f32[16,64,128]{2,1,0:T(8,128)S(1)}, f32[128,1,128]{2,1,0:T(1,128)S(1)}) custom-call(f32[32,40,128]{2,1,0:T(8,128)S(1)} %all_to_all.16.got, f32[18,80,128]{2,1,0:T(8,128)S(1)} %get-tuple-element.17.nu, f32[16,64,128]{2,1,0:T(8,128)S(1)} %get-tuple-element.18.resid, s32[16,64,128]{2,1,0:T(8,128)S(1)} %copy-done.1), custom_call_target="tpu_custom_call" | custom-call | tf_op jit(solution)/shard_map/pallas_call | solution.py:380
  90.4 15.7 %all_to_all.17.sums = f32[128,1,128]{2,1,0:T(1,128)S(1)} all-to-all(f32[128,1,128]{2,1,0:T(1,128)S(1)} %get-tuple-element.19), channel_id=1, replica_groups=mesh['gz'=32,'gy'=4] {'gz','gy'}, dimensions={0} | all-to-all | bytes 131072 | tf_op jit(solution)/shard_map/all_to_all | solution.py:388
  106.1 1.5 %shard_map.98 = (f32[16,64,128]{2,1,0:T(8,128)}, f32[16,64,128]{2,1,0:T(8,128)}, f32[1,128]{1,0:T(1,128)}) custom-call(f32[128,1,128]{2,1,0:T(1,128)S(1)} %all_to_all.17.sums, f32[16,64,128]{2,1,0:T(8,128)S(1)} %get-tuple-element.20.zdir, f32[16,64,128]{2,1,0:T(8,128)S(1)} %get-tuple-element.21.image, f32[16,64,128]{2,1,0:T(8,128)S(1)} %get-tuple-element.18.resid), custom_call_target="tpu_custom_call" | custom-call | tf_op jit(solution)/shard_map/pallas_call | solution.py:389
  (10 shorter events, 0.1 us)
Async XLA Ops:
  1.5 8.2 %collective-permute-start.1 = (f32[2,64,128]{2,1,0:T(8,128)S(1)}, f32[2,64,128]{2,1,0:T(8,128)S(1)}, u32[]{:S(2)}, u32[]{:S(2)}) collective-permute-start(f32[2,64,128]{2,1,0:T(8,128)S(1)} %slice.10), channel_id=1, source_target_pairs={{4,0},{8,4},{12,8},{16,12},{20,16},{24,20},{28,24},{32,28},{36,32}... | collective-permute-start | bytes 196616 | tf_op jit(solution)/shard_map/ppermute | solution.py:344
  5.6 4.1 %collective-permute-start = (f32[1,64,128]{2,1,0:T(8,128)S(1)}, f32[1,64,128]{2,1,0:T(8,128)S(1)}, u32[]{:S(2)}, u32[]{:S(2)}) collective-permute-start(f32[1,64,128]{2,1,0:T(8,128)S(1)} %slice.9), channel_id=1, source_target_pairs={{0,4},{4,8},{8,12},{12,16},{16,20},{20,24},{24,28},{28,32},{32,36}... | collective-permute-start | bytes 98312 | tf_op jit(solution)/shard_map/ppermute | solution.py:343
  9.7 1.0 copy-start
  10.7 1.0 copy-start.2
  11.8 1.0 copy-start.3
  12.8 1.0 copy-start.4
  13.9 6.3 %collective-permute-start.2 = (f32[29,8,128]{2,1,0:T(8,128)S(1)}, f32[29,8,128]{2,1,0:T(8,128)S(1)}, u32[]{:S(2)}, u32[]{:S(2)}) collective-permute-start(f32[29,8,128]{2,1,0:T(8,128)S(1)} %get-tuple-element.14), channel_id=1, source_target_pairs={{0,1},{1,2},{2,3},{4,5},{5,6},{6,7},{8,9},{9,10},{10,11},{12,13},{... | collective-permute-start | bytes 356360 | tf_op jit(solution)/shard_map/ppermute | solution.py:356
  17.4 6.9 %collective-permute-start.3 = (f32[29,8,128]{2,1,0:T(8,128)S(1)}, f32[29,8,128]{2,1,0:T(8,128)S(1)}, u32[]{:S(2)}, u32[]{:S(2)}) collective-permute-start(f32[29,8,128]{2,1,0:T(8,128)S(1)} %get-tuple-element.15), channel_id=1, source_target_pairs={{1,0},{2,1},{3,2},{5,4},{6,5},{7,6},{9,8},{10,9},{11,10},{13,12},{... | collective-permute-start | bytes 356360 | tf_op jit(solution)/shard_map/ppermute | solution.py:357
  30.3 29.1 %copy-start.5 = (bf16[512,512]{1,0:T(8,128)(2,1)S(1)}, bf16[512,512]{1,0:T(8,128)(2,1)}, u32[]{:S(2)}) copy-start(bf16[512,512]{1,0:T(8,128)(2,1)} %constant.7.clone.low) | copy-start | bytes 1572868
  30.3 29.1 %copy-start.6 = (bf16[512,512]{1,0:T(8,128)(2,1)S(1)}, bf16[512,512]{1,0:T(8,128)(2,1)}, u32[]{:S(2)}) copy-start(bf16[512,512]{1,0:T(8,128)(2,1)} %constant.6.clone.high) | copy-start | bytes 1572868
  30.3 29.1 %copy-start.7 = (f32[512,128]{1,0:T(8,128)S(1)}, f32[512,128]{1,0:T(8,128)}, u32[]{:S(2)}) copy-start(f32[512,128]{1,0:T(8,128)} %constant.8.clone.lam) | copy-start | bytes 786436
  69.7 16.7 %copy-start.1 = (s32[16,64,128]{2,1,0:T(8,128)S(1)}, s32[16,64,128]{2,1,0:T(8,128)}, u32[]{:S(2)}) copy-start(s32[16,64,128]{2,1,0:T(8,128)} %msk.3) | copy-start | bytes 1572868

commit v2 on v1

v2 whole, which is shorter than its diff:
```python
import functools

import jax
import jax.numpy as jnp
import ml_dtypes
import numpy as np
from jax import lax
from jax.experimental import pallas as pl
from jax.experimental.pallas import tpu as pltpu
from jax.sharding import PartitionSpec as P

F32 = jnp.float32
BF16 = jnp.bfloat16
NZ, NY, NX = 512, 256, 128
GZ, GY = 32, 4
ZC, YC = NZ // GZ, NY // GY
FR = YC + 16
WR, WC, RING = 23, 22, 3
LANES = 512
YP, XP = 4, 8
ROW0 = (0, 17, 33, 49)
VMEM_LIMIT = 40 * 1024 * 1024


def tables():
    index = np.arange(NZ, dtype=np.int64)
    phase = (index[:, None] + 1) * (index[None, :] + 1) % (2 * (NZ + 1))
    table = np.sqrt(2.0 / (NZ + 1)) * np.sin(np.pi * phase / (NZ + 1))
    table = table.astype(np.float32)
    high = table.astype(ml_dtypes.bfloat16)
    low = (table - high.astype(np.float32)).astype(ml_dtypes.bfloat16)
    lam = 2.0 - 2.0 * np.cos(np.pi * (index + 1.0) / (NZ + 1))
    lam = np.broadcast_to(lam.astype(np.float32)[:, None], (NZ, 128))
    return np.roll(high, 2, 1), np.roll(low, 2, 1), high, low, np.ascontiguousarray(lam)


def lane_iota(shape):
    return lax.broadcasted_iota(jnp.int32, shape, len(shape) - 1)


def roll(value, shift, axis):
    return pltpu.roll(value, shift % value.shape[axis], axis)


def edge_kernel(it, src, reg, msk, zmsg, up, down, it_out, src_out, reg_out, msk_out,
                e_it, e_src, e_reg, e_msk, sems):
    copies = [(it.at[ZC - 3:ZC], zmsg.at[0:3]), (src.at[ZC - 2:ZC], zmsg.at[3:5])]
    for side, row in enumerate((0, YC - 8)):
        rows = pl.ds(row, 8)
        copies += [
            (it.at[:, rows], e_it.at[side]),
            (src.at[:, rows], e_src.at[side]),
            (reg.at[0:1, rows], e_reg.at[side]),
            (msk.at[0:1, rows], e_msk.at[side]),
        ]
    copies += [
        (it, it_out), (src.at[0:ZC - 2], src_out), (reg.at[0:1], reg_out), (msk.at[0:1], msk_out),
    ]
    copies = [pltpu.make_async_copy(x, y, sems.at[k]) for k, (x, y) in enumerate(copies)]
    for copy in copies:
        copy.start()
    for copy in copies[:-4]:
        copy.wait()
    for z in range(ZC):
        up[5 * z:5 * z + 5] = e_it[1, z, 3:8]
        down[6 * z:6 * z + 6] = e_it[0, z, 0:6]
    for z in range(ZC - 2):
        up[80 + 4 * z:84 + 4 * z] = e_src[1, z, 4:8]
        down[96 + 4 * z:100 + 4 * z] = e_src[0, z, 0:4]
    up[136:141] = e_reg[1, 0, 3:8].astype(F32)
    up[141:145] = e_msk[1, 0, 4:8].astype(F32)
    up[145:152] = jnp.zeros((7, 128), F32)
    down[152:157] = e_reg[0, 0, 0:5].astype(F32)
    down[157:161] = e_msk[0, 0, 0:4].astype(F32)
    down[161:168] = jnp.zeros((7, 128), F32)
    for copy in copies[-4:]:
        copy.wait()


def corner_kernel(zgot, up, down):
    for p in range(3):
        up[5 * p:5 * p + 5] = zgot[p, YC - 5:YC]
        down[6 * p:6 * p + 6] = zgot[p, 0:6]
    for q in range(2):
        up[15 + 4 * q:19 + 4 * q] = zgot[3 + q, YC - 4:YC]
        down[18 + 4 * q:22 + 4 * q] = zgot[3 + q, 0:4]
    up[23:24] = jnp.zeros((1, 128), F32)
    down[26:32] = jnp.zeros((6, 128), F32)


def segments(block):
    found = []
    for row in range(WR):
        start = (WC * (row - RING)) % LANES
        begin, end = max(start, 128 * block), min(start + WC, 128 * block + 128)
        if begin < end:
            found.append((begin - 128 * block, row))
    return sorted(found)


def residual_kernel(it, src, reg, msk, zgot, lo, hi, corner_lo, corner_hi,
                    chunks, nu, resid, message, field, drive, flat, rows):
    group, column = lax.axis_index("gz"), lax.axis_index("gy")
    low_end, high_end = column == 0, column == GY - 1
    start = group == 0
    mid = slice(8, 8 + YC)

    def below(value):
        return jnp.where(low_end, 0.0, value)

    def above(value):
        return jnp.where(high_end, 0.0, value)

    for p in range(19):
        z = p - 3
        field[p, mid] = zgot[p] if p < 3 else it[z]
        field[p, 3:8] = below(
            corner_lo[5 * p:5 * p + 5] if p < 3 else lo[5 * z:5 * z + 5]
        )
        field[p, 72:78] = above(
            corner_hi[6 * p:6 * p + 6] if p < 3 else hi[6 * z:6 * z + 6]
        )
    for t in range(ZC):
        z = t - 2
        drive[t, mid] = zgot[3 + t] if t < 2 else src[z]
        drive[t, 4:8] = (
            corner_lo[15 + 4 * t:19 + 4 * t] if t < 2 else lo[80 + 4 * z:84 + 4 * z]
        )
        drive[t, 72:76] = (
            corner_hi[18 + 4 * t:22 + 4 * t] if t < 2 else hi[96 + 4 * z:100 + 4 * z]
        )
    flat[0, mid] = reg[0].astype(F32)
    flat[0, 3:8] = below(lo[136:141])
    flat[0, 72:77] = above(hi[152:157])
    flat[1, mid] = msk[0].astype(F32)
    flat[1, 4:8] = lo[141:145]
    flat[1, 72:76] = hi[157:161]
    region, fixed = flat[0], flat[1]
    lane = lane_iota((FR, 128))
    first, last = lane == 0, lane == 127
    iron, copper, held = region == 2.0, region == 1.0, fixed == 1.0

    for p in range(18):
        u = field[p]
        uz = field[p + 1]
        if p == 2:
            uz = jnp.where(start, 0.0, uz)
        dz = uz - u
        dy = roll(u, -1, 0) - u
        dx = jnp.where(last, 0.0, roll(u, -1, 1)) - u
        bsq = dz * dz + dy * dy + dx * dx
        bsq = bsq * bsq
        nu[p] = jnp.where(iron, 0.05 + bsq / (bsq + 9.0), 1.0)

    total = nu[1]
    for p in range(2, 17):
        total = total + nu[p]
    flux = 0.5 * (nu[0] + nu[1]) * (field[0] - field[1])
    for t in range(ZC):
        p = t + 1
        u, n = field[p], nu[p]
        uz, nz = field[p + 1], nu[p + 1]
        if p == 2:
            uz, nz = jnp.where(start, 0.0, uz), jnp.where(start, 1.0, nz)
        if p == 3:
            flux = jnp.where(start, -0.5 * (1.0 + n) * u, flux)
        ahead = 0.5 * (n + nz) * (u - uz)
        flow = ahead - flux
        flux = ahead
        fy = 0.5 * (n + roll(n, -1, 0)) * (u - roll(u, -1, 0))
        flow = flow + (fy - roll(fy, 1, 0))
        nx = jnp.where(last, 1.0, roll(n, -1, 1))
        ux = jnp.where(last, 0.0, roll(u, -1, 1))
        fx = 0.5 * (n + nx) * (u - ux)
        flow = flow + (fx - jnp.where(first, -0.5 * (n + 1.0) * u, roll(fx, 1, 1)))
        value = -jnp.where(held, u, flow - jnp.where(copper, drive[t], 0.0))
        rows[t * FR:t * FR + FR, :] = value
        if t < 2:
            message[3 * FR + YC * t:3 * FR + YC * t + YC, :] = value[mid]
        else:
            resid[t - 2] = value[mid]
    for k in range(3):
        message[FR * k:FR * k + FR, :] = nu[1 + k]

    faces = 2.0 * total + 0.5 * (
        roll(total, -1, 0) + roll(total, 1, 0)
        + jnp.where(last, float(ZC), roll(total, -1, 1))
        + jnp.where(first, float(ZC), roll(total, 1, 1))
    )
    rows[16 * FR:17 * FR, :] = total
    rows[17 * FR:18 * FR, :] = faces
    rows[18 * FR:24 * FR, :] = jnp.zeros((6 * FR, 128), F32)

    lane = lane_iota((8, 128))
    places = [(lane - 16 * xp) & 127 for xp in range(XP)]
    for yp in range(YP):
        for block in range(4):
            parts = segments(block)
            lines = []
            for begin, row in parts:
                at = ROW0[yp] + row + 4
                lines.append([
                    roll(
                        rows[pl.ds(8 * tile * FR + at, 8, stride=FR), :],
                        WC * (row - RING) + RING, 1,
                    )
                    for tile in range(3)
                ])
            for xp in range(XP):
                values = lines[0]
                for (begin, row), line in zip(parts[1:], lines[1:]):
                    later = places[xp] >= begin
                    values = [jnp.where(later, x, y) for x, y in zip(line, values)]
                values = [roll(value, -16 * xp, 1) for value in values]
                peer, at = yp * XP + xp, 16 * block
                chunks[peer, at:at + 8, :] = values[0]
                chunks[peer, at + 8:at + 16, :] = values[1]
                chunks[peer, 64 + 2 * block:66 + 2 * block, :] = values[2][0:2]


def product(high, low, right_high, right_low):
    left = jnp.concatenate([high, low, high], axis=1)
    right = jnp.concatenate([right_high, right_high, right_low], axis=0)
    return jnp.dot(left, right, preferred_element_type=F32)


def modes_kernel(got, ahead_high, ahead_low, high, low, lam, out, lines, back):
    group, column = lax.axis_index("gz"), lax.axis_index("gy")
    yp, xp = lax.div(group, XP), lax.rem(group, XP)
    s_high, s_low = ahead_high[...], ahead_low[...]
    for half in range(2):
        value = jnp.concatenate(
            [
                got[:, 16 * block:16 * block + 16, :].reshape(NZ, 128)
                for block in (2 * half, 2 * half + 1)
            ],
            axis=1,
        )
        v_high = value.astype(BF16)
        v_low = (value - v_high.astype(F32)).astype(BF16)
        lines[:, 256 * half:256 * half + 256] = product(s_high, s_low, v_high, v_low)

    sums = jnp.sum(got[:, 64:72, :], axis=0) * (1.0 / NZ)
    mean = jnp.concatenate([sums[2 * b:2 * b + 1] for b in range(4)], axis=1)
    faces = jnp.concatenate([sums[2 * b + 1:2 * b + 2] for b in range(4)], axis=1)
    spot = (lane_iota((1, LANES)) + RING * WC) & (LANES - 1)
    row = (spot * 2979) >> 16
    col = spot - row * WC
    ypos = column * YC + 16 * yp + jnp.where(yp > 0, 1, 0) + row - 4
    xpos = 16 * xp - RING + col
    inside = (row < WR) & (xpos >= 0) & (xpos < NX) & (ypos >= 0) & (ypos < NY)
    right = 0.5 * (mean + roll(mean, -1, 1))
    left = roll(right, 1, 1)
    above = 0.5 * (mean + roll(mean, -WC, 1))
    below = roll(above, WC, 1)

    vhat = lines[...]
    lam_rows = jnp.concatenate([lam[...]] * 4, axis=1)
    factor = jnp.where(inside, 0.6 / (faces + lam_rows * mean), 0.0)
    w = factor * vhat
    for _ in range(3):
        near = (
            above * roll(w, -WC, 1) + below * roll(w, WC, 1)
            + right * roll(w, -1, 1) + left * roll(w, 1, 1)
        )
        w = 0.4 * w + factor * (vhat + near)
    w = w[:, :384]
    w_high = w.astype(BF16)
    w_low = (w - w_high.astype(F32)).astype(BF16)

    spot = lane_iota((384, 384))
    own = jnp.where(yp == 0, 1, 0)
    halo = jnp.where(yp == 0, 0, 16)
    pick = jnp.where(spot < 256, own + (spot >> 4), halo) * WC + RING + (spot & 15)
    choose = jnp.where(lax.broadcasted_iota(jnp.int32, (384, 384), 0) == pick, 1.0, 0.0)
    choose = choose.astype(BF16)
    s_high, s_low = high[...], low[...]
    w_high = jnp.dot(w_high, choose, preferred_element_type=F32).astype(BF16)
    w_low = jnp.dot(w_low, choose, preferred_element_type=F32).astype(BF16)
    back[8:8 + NZ, :] = product(s_high, s_low, w_high, w_low)
    back[0:8, :] = jnp.zeros((8, 384), F32)
    back[8 + NZ:, :] = jnp.zeros((8, 384), F32)

    sub = lax.broadcasted_iota(jnp.int32, (8, 128), 0)
    pattern = (((lane_iota((8, 128)) >> 4) + sub) & 7) == 0
    for peer in range(GZ):
        at = 8 + ZC * peer
        for block in range(2):
            lanes = slice(128 * block, 128 * block + 128)
            out[peer, 16 * block:16 * block + 16, :] = back[at:at + ZC, lanes]
            out[peer, 32 + block:33 + block, :] = back[at - 1:at, lanes]
            out[peer, 34 + block:35 + block, :] = back[at + ZC:at + ZC + 1, lanes]
            piece = back[at + 8 * block:at + 8 * block + 8, 256:384]
            piece = jnp.sum(jnp.where(pattern, piece, 0.0), axis=0, keepdims=True)
            out[peer, 36 + block:37 + block, :] = piece
        out[peer, 38:40, :] = jnp.zeros((2, 128), F32)


def resid_plane(resid, message, z):
    if z < ZC - 2:
        return resid[z]
    at = 3 * FR + YC * (z - ZC + 2)
    return message[at:at + YC, :]


def image_kernel(got, nu, resid, message, msk, zdir, image, sums, frame):
    lane = lane_iota((8, 128))
    places = [(lane >> 4) == k for k in range(8)]

    def spread(tiles, jj):
        value = tiles[0]
        for xp in range(1, XP):
            value = jnp.where(places[(jj + xp) % 8], tiles[xp], value)
        return roll(value, -16 * jj, 1)

    for yp in range(YP):
        for block in range(2):
            for tile in range(2):
                at = 16 * block + 8 * tile
                tiles = [
                    roll(got[yp * XP + xp, at:at + 8, :], 16 * xp, 1) for xp in range(XP)
                ]
                for jj in range(8):
                    y = 8 + 16 * yp + 8 * block + jj
                    frame[pl.ds((1 + 8 * tile) * FR + y, 8, stride=FR), :] = spread(tiles, jj)
        tiles = [roll(got[yp * XP + xp, 32:40, :], 16 * xp, 1) for xp in range(XP)]
        for jj in range(8):
            value = spread(tiles, jj)
            y = 8 + 16 * yp + jj
            for k in range(2):
                frame[y + 8 * k:y + 8 * k + 1, :] = value[k:k + 1]
                at = 17 * FR + y + 8 * k
                frame[at:at + 1, :] = value[2 + k:3 + k]

    sub = lax.broadcasted_iota(jnp.int32, (8, 128), 0)
    turn = ((lane >> 4) + sub) & 7
    for yp, y in ((0, 7), (YP - 1, 8 + YC)):
        for tile in range(2):
            value = jnp.zeros((8, 128), F32)
            for xp in range(XP):
                line = got[yp * XP + xp, 36 + tile:37 + tile, :]
                line = roll(jnp.broadcast_to(line, (8, 128)), 16 * xp, 1)
                value = jnp.where(turn == xp, line, value)
            value = pltpu.roll(value, 0, 1, stride=16, stride_axis=0)
            frame[pl.ds((1 + 8 * tile) * FR + y, 8, stride=FR), :] = value

    lane = lane_iota((YC, 128))
    first, last = lane == 0, lane == 127
    held = msk[0] == 1

    group = lax.axis_index("gz")

    def nu_rows(z, shift):
        at = 8 + shift
        if z >= ZC - 2:
            value = message[FR * (z - ZC + 2) + at:FR * (z - ZC + 2) + at + YC, :]
        else:
            value = nu[z + 3, at:at + YC]
        if z == -1:
            value = jnp.where(group == 0, 1.0, value)
        if z == ZC:
            value = jnp.where(group == GZ - 1, 1.0, value)
        return value

    def dir_rows(z, shift):
        at = (z + 1) * FR + 8 + shift
        return frame[at:at + YC, :]

    d, n = dir_rows(0, 0), nu_rows(0, 0)
    flux = 0.5 * (nu_rows(-1, 0) + n) * (dir_rows(-1, 0) - d)
    rr = ri = ii = jnp.zeros((8, 128), F32)

    def fold(value):
        return jnp.sum(value.reshape(YC // 8, 8, 128), axis=0)

    for z in range(ZC):
        dz, nz = dir_rows(z + 1, 0), nu_rows(z + 1, 0)
        ahead = 0.5 * (n + nz) * (d - dz)
        flow = ahead - flux
        flow = flow + 0.5 * (n + nu_rows(z, 1)) * (d - dir_rows(z, 1))
        flow = flow + 0.5 * (n + nu_rows(z, -1)) * (d - dir_rows(z, -1))
        nx = jnp.where(last, 1.0, roll(n, -1, 1))
        dx = jnp.where(last, 0.0, roll(d, -1, 1))
        fx = 0.5 * (n + nx) * (d - dx)
        flow = flow + (fx - jnp.where(first, -0.5 * (n + 1.0) * d, roll(fx, 1, 1)))
        value = jnp.where(held, d, flow)
        zdir[z] = d
        image[z] = value
        r = resid_plane(resid, message, z)
        rr, ri, ii = rr + fold(r * r), ri + fold(r * value), ii + fold(value * value)
        d, n, flux = dz, nz, ahead

    parts = (rr, ri, ii)
    line = lane_iota((1, 128))
    packed = jnp.zeros((1, 128), F32)
    for k, part in enumerate(parts):
        packed = jnp.where(line == k, jnp.sum(part), packed)
    sums[...] = jnp.broadcast_to(packed[None], sums.shape)


def output_kernel(sums, zdir, image, resid, message, correction, lin_residual, rms):
    total = jnp.sum(sums[...], axis=0)
    beta_sq = total[0:1, 0:1] + 1e-06
    beta = jnp.sqrt(beta_sq)
    h_one = total[0:1, 1:2] / beta_sq
    denom = total[0:1, 2:3] / beta_sq - h_one * h_one * (1e-06 / beta_sq) + 1e-06
    gamma = h_one / denom
    correction[...] = zdir[...] * gamma[None]
    for z in range(ZC):
        lin_residual[z] = resid_plane(resid, message, z) - gamma * image[z]
    rms[...] = jnp.broadcast_to(beta * (1.0 / np.sqrt(float(NZ * NY * NX))), rms.shape)


def call(kernel, out_shape, scratch=(), in_specs=None):
    extra = {} if in_specs is None else {"in_specs": in_specs}
    return pl.pallas_call(
        kernel,
        out_shape=out_shape,
        scratch_shapes=scratch,
        compiler_params=pltpu.CompilerParams(vmem_limit_bytes=VMEM_LIMIT),
        **extra,
    )


def struct(*shape):
    return jax.ShapeDtypeStruct(shape, F32)


def cyclic(count, step):
    return [(i, (i + step) % count) for i in range(count)]


def shards(iterate, source, region, fixed_mask):
    far = [pl.BlockSpec(memory_space=pltpu.HBM)] * 4
    arguments = [
        pltpu.with_memory_space_constraint(argument, pltpu.HBM)
        for argument in (iterate, source, region, fixed_mask)
    ]
    edge = (2, ZC, 8, 128)
    flat = jax.ShapeDtypeStruct((1, YC, 128), jnp.int32)
    zmsg, up, down, it, src, reg, msk = call(
        edge_kernel,
        (
            struct(5, YC, 128), struct(152, 128), struct(168, 128),
            struct(ZC, YC, 128), struct(ZC - 2, YC, 128), flat, flat,
        ),
        scratch=[
            pltpu.VMEM(edge, F32), pltpu.VMEM(edge, F32),
            pltpu.VMEM((2, 1, 8, 128), jnp.int32), pltpu.VMEM((2, 1, 8, 128), jnp.int32),
            pltpu.SemaphoreType.DMA((14,)),
        ],
        in_specs=far,
    )(*arguments)
    zgot = lax.ppermute(zmsg, "gz", cyclic(GZ, 1))
    lo = lax.ppermute(up, "gy", cyclic(GY, 1))
    hi = lax.ppermute(down, "gy", cyclic(GY, -1))
    corner_up, corner_down = call(corner_kernel, (struct(24, 128), struct(32, 128)))(zgot)
    corner_lo = lax.ppermute(corner_up, "gy", cyclic(GY, 1))
    corner_hi = lax.ppermute(corner_down, "gy", cyclic(GY, -1))

    cells = (ZC, YC, 128)
    chunks, nu, resid, message = call(
        residual_kernel,
        (
            struct(GZ, 72, 128), struct(18, FR, 128), struct(ZC - 2, YC, 128),
            struct(3 * FR + 2 * YC, 128),
        ),
        scratch=[
            pltpu.VMEM((19, FR, 128), F32), pltpu.VMEM((ZC, FR, 128), F32),
            pltpu.VMEM((2, FR, 128), F32), pltpu.VMEM((24 * FR, 128), F32),
        ],
    )(it, src, reg, msk, zgot, lo, hi, corner_lo, corner_hi)
    message = lax.ppermute(message, "gz", cyclic(GZ, -1))
    windows = lax.all_to_all(chunks, "gz", 0, 0, tiled=True)
    sent = call(
        modes_kernel,
        struct(GZ, 40, 128),
        scratch=[
            pltpu.VMEM((NZ, LANES), F32), pltpu.VMEM((NZ + 16, 384), F32),
        ],
    )(windows, *[jnp.asarray(table) for table in tables()])
    returned = lax.all_to_all(sent, "gz", 0, 0, tiled=True)
    zdir, image, sums = call(
        image_kernel,
        (struct(*cells), struct(*cells), struct(GZ * GY, 1, 128)),
        scratch=[pltpu.VMEM((18 * FR, 128), F32)],
    )(returned, nu, resid, message, msk)
    sums = lax.all_to_all(sums, ("gz", "gy"), 0, 0, tiled=True)
    correction, lin_residual, rms = call(
        output_kernel, (struct(*cells), struct(*cells), struct(1, 128))
    )(sums, zdir, image, resid, message)
    return correction, lin_residual, rms[0, 0]


def solution(mesh):
    placed = (P("gz", "gy", None),) * 4
    return jax.shard_map(
        shards,
        mesh=mesh,
        in_specs=placed,
        out_specs=(P("gz", "gy", None), P("gz", "gy", None), P()),
        check_vma=False,
    )
```

time: 108 us -> 89.5 us (0.83)
  blocking collectives: 61.4 us -> 42.3 us
  waiting for transfers between devices: 6.62 us -> 16.4 us
  local copies, waits for them, and re-layouts: 5.8 us -> 0.03 us
  Pallas kernels: 21.8 us -> 16.2 us
  starting transfers between devices: 11.2 us -> 13.5 us
    all_to_all x1 -> x0, blocking collectives: 16.7 us -> none  [shards(): returned = lax.all_to_all(sent, 'gz', 0, 0, tiled=True)]
    ppermute x4 -> x6, waiting for transfers between devices: 6.62 us -> 15.1 us  [the longest x1 11.4 us: shards(): message = lax.ppermute(message, 'gz', cyclic(GZ, -1))]
    unnamed x16 -> x10, local copies, waits for them, and re-layouts: 4.19 us -> 0.03 us
    pallas_call x1, Pallas kernels: 10.3 us -> 6.37 us  [shards(): call(modes_kernel, struct(GZ, 40, 128), scratch=[pltpu.VMEM((NZ, LANES),...]
    all_to_all x0 -> x1, starting transfers between devices: none -> 3.96 us  [shards(): returned = lax.all_to_all(sent, 'gz', 0, 0, tiled=True)]
    ppermute x4 -> x6, starting transfers between devices: 11.2 us -> 9.59 us  [the longest x1 3.76 us: shards(): hi = lax.ppermute(down, 'gy', cyclic(GY, -1))]
    slice x2 -> x0, local copies, waits for them, and re-layouts: 1.61 us -> none  [the longest x1 0.85 us: shards(): zhi = lax.ppermute(iterate[0:2], 'gz', down_z)]
    all_to_all x1, blocking collectives: 15.7 us -> 14.1 us  [shards(): sums = lax.all_to_all(sums, ('gz', 'gy'), 0, 0, tiled=True)]
  transfers between devices with their start and end apart: 4 -> 7, of which waited for: 3 -> 4; matrix products, arithmetic and copies ran while one was open for 1% -> 0% of each run, Pallas kernels for 0% -> 0%
where the time goes in v2:
time: 89.5 us; the launch traced here: 89.2 us
  blocking collectives  42.3 us (47%)
  waiting for transfers between devices  16.4 us (18%)
  Pallas kernels  16.2 us (18%)
  starting transfers between devices  13.5 us (15%)
    all_to_all x1, blocking collectives, shards(): windows = lax.all_to_all(chunks, 'gz', 0, 0, tiled=True)  28.2 us
    all_to_all x1, blocking collectives, shards(): sums = lax.all_to_all(sums, ('gz', 'gy'), 0, 0, tiled=True)  14.1 us
    ppermute x1, waiting for transfers between devices, shards(): message = lax.ppermute(message, 'gz', cyclic(GZ, -1))  11.4 us
    pallas_call x1, Pallas kernels, shards(): call(modes_kernel, struct(GZ, 40, 128), scratch=[pltpu.VMEM((NZ, LANES),...  6.37 us
    all_to_all x1, starting transfers between devices, shards(): returned = lax.all_to_all(sent, 'gz', 0, 0, tiled=True)  3.96 us
    pallas_call x1, Pallas kernels, shards(): call(residual_kernel, (struct(GZ, 72, 128), struct(18, FR, 128), struct(Z...  3.76 us
    ppermute x1, starting transfers between devices, shards(): hi = lax.ppermute(down, 'gy', cyclic(GY, -1))  3.76 us
    pallas_call x1, Pallas kernels, shards(): call(image_kernel, (struct(*cells), struct(*cells), struct(GZ * GY, 1, 12...  3.01 us
  transfers between devices with their start and end apart: 7, of which 4 were waited for; matrix products, arithmetic and copies ran while one was open for 0% of the time, Pallas kernels for 0%

profile of v2, /device:TPU:1, one launch (start us, length us, event | category | flops | bytes accessed | tf_op | source)
XLA Modules:
  0.0 89.2 jit_solution(6293235994551092067)
XLA Ops:
  0.6 1.6 %shard_map.112 = (f32[5,64,128]{2,1,0:T(8,128)S(1)}, f32[152,128]{1,0:T(8,128)S(1)}, f32[168,128]{1,0:T(8,128)S(1)}, f32[16,64,128]{2,1,0:T(8,128)S(1)}, f32[14,...) custom-call(f32[16,64,128]{2,1,0:T(8,128)} %it.1, f32[16,64,128]{2,1,0:T(8,128)} %src.1, ...), custom_call_target="tpu_custom_call" | custom-call | tf_op jit(solution)/shard_map/pallas_call | solution.py:441
  2.2 2.7 %collective-permute-start = (f32[5,64,128]{2,1,0:T(8,128)S(1)}, f32[5,64,128]{2,1,0:T(8,128)S(1)}, u32[]{:S(2)}, u32[]{:S(2)}) collective-permute-start(f32[5,64,128]{2,1,0:T(8,128)S(1)} %get-tuple-element.26), channel_id=1, source_target_pairs={{0,4},{4,8},{8,12},{12,16},{16,20},{20,24},{24,28},{28,32},{32,36}... | collective-permute-start | bytes 491528 | tf_op jit(solution)/shard_map/ppermute | solution.py:454
  4.9 3.8 %collective-permute-start.2 = (f32[168,128]{1,0:T(8,128)S(1)}, f32[168,128]{1,0:T(8,128)S(1)}, u32[]{:S(2)}, u32[]{:S(2)}) collective-permute-start(f32[168,128]{1,0:T(8,128)S(1)} %get-tuple-element.28), channel_id=1, source_target_pairs={{0,3},{1,0},{2,1},{3,2},{4,7},{5,4},{6,5},{7,6},{8,11},{9,8},{10,9... | collective-permute-start | bytes 258056 | tf_op jit(solution)/shard_map/ppermute | solution.py:456
  8.6 0.0 collective-permute-start.1
  8.6 0.0 collective-permute-done.zgot
  8.7 2.7 %collective-permute-start.4 = (f32[32,128]{1,0:T(8,128)S(1)}, f32[32,128]{1,0:T(8,128)S(1)}, u32[]{:S(2)}, u32[]{:S(2)}) collective-permute-start(f32[32,128]{1,0:T(8,128)S(1)} %get-tuple-element.30), channel_id=1, source_target_pairs={{0,3},{1,0},{2,1},{3,2},{4,7},{5,4},{6,5},{7,6},{8,11},{9,8},{10,9... | collective-permute-start | bytes 49160 | tf_op jit(solution)/shard_map/ppermute | solution.py:459
  11.4 0.0 collective-permute-start.3
  11.4 2.3 %collective-permute-done.1.lo = f32[152,128]{1,0:T(8,128)S(1)} collective-permute-done((f32[152,128]{1,0:T(8,128)S(1)}, f32[152,128]{1,0:T(8,128)S(1)}, u32[]{:S(2)}, u32[]{:S(2)}) %collective-permute-start.1) | collective-permute-done | bytes 77856 | tf_op jit(solution)/shard_map/ppermute | solution.py:455
  13.7 1.5 %collective-permute-done.3.corner_lo = f32[24,128]{1,0:T(8,128)S(1)} collective-permute-done((f32[24,128]{1,0:T(8,128)S(1)}, f32[24,128]{1,0:T(8,128)S(1)}, u32[]{:S(2)}, u32[]{:S(2)}) %collective-permute-start.3) | collective-permute-done | bytes 12320 | tf_op jit(solution)/shard_map/ppermute | solution.py:458
  15.2 3.8 %shard_map.114 = (f32[32,72,128]{2,1,0:T(8,128)S(1)}, f32[18,80,128]{2,1,0:T(8,128)S(1)}, f32[14,64,128]{2,1,0:T(8,128)S(1)}, f32[368,128]{1,0:T(8,128)S(1)}) custom-call(f32[16,64,128]{2,1,0:T(8,128)S(1)} %get-tuple-element.22.it, f32[14,64,128]{2,1,0:T(8,128)S(1)} %get-tuple-element.23.src, s32[1,64,128]{2,1,0:T(8,128)S(1)} %get-tuple-element.24.reg, ...), custom_call_target="tpu_custom_call" | custom-call | tf_op jit(solution)/shard_map/pallas_call | solution.py:462
  18.9 0.0 copy-start
  18.9 0.0 copy-start.1
  19.0 0.0 copy-start.2
  19.0 0.0 copy-start.3
  19.0 0.0 copy-start.4
  19.0 28.2 %all_to_all.15.got = f32[32,72,128]{2,1,0:T(8,128)S(1)} all-to-all(f32[32,72,128]{2,1,0:T(8,128)S(1)} %get-tuple-element.31), channel_id=1, replica_groups=mesh['gz'=32,'gy'=4] {'gz'}, dimensions={0} | all-to-all | bytes 2359296 | tf_op jit(solution)/shard_map/all_to_all | solution.py:474
  47.2 6.4 %shard_map.115 = f32[32,40,128]{2,1,0:T(8,128)} custom-call(f32[32,72,128]{2,1,0:T(8,128)S(1)} %all_to_all.15.got, bf16[512,512]{1,0:T(8,128)(2,1)S(1)} %copy-done.3, bf16[512,512]{1,0:T(8,128)(2,1)S(1)} %copy-done.2, bf16[512,512]{1,0:T(8,128)(2,1)S(1)} %copy-done.1, bf16[512,512]{1,0:T(8,128)(2,1)S(1)} %copy-done, f32[512,128]{1,0:T(8,128)S(1)} %copy-done.4), custom_call_target="tpu_custom_call" | custom-call | tf_op jit(solution)/shard_map/pallas_call | solution.py:475
  53.6 4.0 %all-to-all-start.1 = ((f32[32,40,128]{2,1,0:T(8,128)}), f32[32,40,128]{2,1,0:T(8,128)S(1)}, u32[]{:S(2)}, u32[]{:S(2)}) async-start(f32[32,40,128]{2,1,0:T(8,128)} %shard_map.115), calls=%async_computation.1 | async-start | bytes 1310720 | tf_op jit(solution)/shard_map/all_to_all | solution.py:482
  57.6 0.4 collective-permute-start.5
  58.0 11.4 %collective-permute-done.5.message = f32[368,128]{1,0:T(8,128)S(1)} collective-permute-done((f32[368,128]{1,0:T(8,128)S(1)}, f32[368,128]{1,0:T(8,128)S(1)}, u32[]{:S(2)}, u32[]{:S(2)}) %collective-permute-start.5) | collective-permute-done | bytes 188448 | tf_op jit(solution)/shard_map/ppermute | solution.py:473
  69.3 1.2 %all-to-all-done.1.got = f32[32,40,128]{2,1,0:T(8,128)S(1)} async-done(((f32[32,40,128]{2,1,0:T(8,128)}), f32[32,40,128]{2,1,0:T(8,128)S(1)}, u32[]{:S(2)}, u32[]{:S(2)}) %all-to-all-start.1) | async-done | bytes 655392 | tf_op jit(solution)/shard_map/all_to_all | solution.py:482
  70.6 3.0 %shard_map.116 = (f32[16,64,128]{2,1,0:T(8,128)S(1)}, f32[16,64,128]{2,1,0:T(8,128)S(1)}, f32[128,1,128]{2,1,0:T(1,128)S(1)}) custom-call(f32[32,40,128]{2,1,0:T(8,128)S(1)} %all-to-all-done.1.got, f32[18,80,128]{2,1,0:T(8,128)S(1)} %get-tuple-element.32.nu, f32[14,64,128]{2,1,0:T(8,128)S(1)} %get-tuple-element.33.resid, ...), custom_call_target="tpu_custom_call" | custom-call | tf_op jit(solution)/shard_map/pallas_call | solution.py:483
  73.6 14.1 %all_to_all.16.sums = f32[128,1,128]{2,1,0:T(1,128)S(1)} all-to-all(f32[128,1,128]{2,1,0:T(1,128)S(1)} %get-tuple-element.35), channel_id=1, replica_groups=mesh['gz'=32,'gy'=4] {'gz','gy'}, dimensions={0} | all-to-all | bytes 131072 | tf_op jit(solution)/shard_map/all_to_all | solution.py:488
  87.7 1.5 %shard_map.117 = (f32[16,64,128]{2,1,0:T(8,128)}, f32[16,64,128]{2,1,0:T(8,128)}, f32[1,128]{1,0:T(1,128)}) custom-call(f32[128,1,128]{2,1,0:T(1,128)S(1)} %all_to_all.16.sums, f32[16,64,128]{2,1,0:T(8,128)S(1)} %get-tuple-element.36.zdir, f32[16,64,128]{2,1,0:T(8,128)S(1)} %get-tuple-element.37.image, f32[14,64,128]{2,1,0:T(8,128)S(1)} %get-tuple-element.33.resid, ...), custom_call_target="tpu_custom_call" | custom-call | tf_op jit(solution)/shard_map/pallas_call | solution.py:489
  (8 shorter events, 0.0 us)
Async XLA Ops:
  2.2 6.4 %collective-permute-start = (f32[5,64,128]{2,1,0:T(8,128)S(1)}, f32[5,64,128]{2,1,0:T(8,128)S(1)}, u32[]{:S(2)}, u32[]{:S(2)}) collective-permute-start(f32[5,64,128]{2,1,0:T(8,128)S(1)} %get-tuple-element.26), channel_id=1, source_target_pairs={{0,4},{4,8},{8,12},{12,16},{16,20},{20,24},{24,28},{28,32},{32,36}... | collective-permute-start | bytes 491528 | tf_op jit(solution)/shard_map/ppermute | solution.py:454
  4.9 8.8 %collective-permute-start.2 = (f32[168,128]{1,0:T(8,128)S(1)}, f32[168,128]{1,0:T(8,128)S(1)}, u32[]{:S(2)}, u32[]{:S(2)}) collective-permute-start(f32[168,128]{1,0:T(8,128)S(1)} %get-tuple-element.28), channel_id=1, source_target_pairs={{0,3},{1,0},{2,1},{3,2},{4,7},{5,4},{6,5},{7,6},{8,11},{9,8},{10,9... | collective-permute-start | bytes 258056 | tf_op jit(solution)/shard_map/ppermute | solution.py:456
  8.6 5.0 %collective-permute-start.1 = (f32[152,128]{1,0:T(8,128)S(1)}, f32[152,128]{1,0:T(8,128)S(1)}, u32[]{:S(2)}, u32[]{:S(2)}) collective-permute-start(f32[152,128]{1,0:T(8,128)S(1)} %get-tuple-element.27), channel_id=1, source_target_pairs={{0,1},{1,2},{2,3},{3,0},{4,5},{5,6},{6,7},{7,4},{8,9},{9,10},{10,1... | collective-permute-start | bytes 233480 | tf_op jit(solution)/shard_map/ppermute | solution.py:455
  8.7 6.5 %collective-permute-start.4 = (f32[32,128]{1,0:T(8,128)S(1)}, f32[32,128]{1,0:T(8,128)S(1)}, u32[]{:S(2)}, u32[]{:S(2)}) collective-permute-start(f32[32,128]{1,0:T(8,128)S(1)} %get-tuple-element.30), channel_id=1, source_target_pairs={{0,3},{1,0},{2,1},{3,2},{4,7},{5,4},{6,5},{7,6},{8,11},{9,8},{10,9... | collective-permute-start | bytes 49160 | tf_op jit(solution)/shard_map/ppermute | solution.py:459
  11.4 3.8 %collective-permute-start.3 = (f32[24,128]{1,0:T(8,128)S(1)}, f32[24,128]{1,0:T(8,128)S(1)}, u32[]{:S(2)}, u32[]{:S(2)}) collective-permute-start(f32[24,128]{1,0:T(8,128)S(1)} %get-tuple-element.29), channel_id=1, source_target_pairs={{0,1},{1,2},{2,3},{3,0},{4,5},{5,6},{6,7},{7,4},{8,9},{9,10},{10,1... | collective-permute-start | bytes 36872 | tf_op jit(solution)/shard_map/ppermute | solution.py:458
  18.9 28.3 %copy-start = (bf16[512,512]{1,0:T(8,128)(2,1)S(1)}, bf16[512,512]{1,0:T(8,128)(2,1)}, u32[]{:S(2)}) copy-start(bf16[512,512]{1,0:T(8,128)(2,1)} %constant.13.clone.low) | copy-start | bytes 1572868
  18.9 28.3 %copy-start.1 = (bf16[512,512]{1,0:T(8,128)(2,1)S(1)}, bf16[512,512]{1,0:T(8,128)(2,1)}, u32[]{:S(2)}) copy-start(bf16[512,512]{1,0:T(8,128)(2,1)} %constant.12.clone.high) | copy-start | bytes 1572868
  19.0 28.3 %copy-start.2 = (bf16[512,512]{1,0:T(8,128)(2,1)S(1)}, bf16[512,512]{1,0:T(8,128)(2,1)}, u32[]{:S(2)}) copy-start(bf16[512,512]{1,0:T(8,128)(2,1)} %constant.11.clone.ahead_low) | copy-start | bytes 1572868
  19.0 28.2 %copy-start.3 = (bf16[512,512]{1,0:T(8,128)(2,1)S(1)}, bf16[512,512]{1,0:T(8,128)(2,1)}, u32[]{:S(2)}) copy-start(bf16[512,512]{1,0:T(8,128)(2,1)} %constant.10.clone.ahead_high) | copy-start | bytes 1572868
  19.0 28.2 %copy-start.4 = (f32[512,128]{1,0:T(8,128)S(1)}, f32[512,128]{1,0:T(8,128)}, u32[]{:S(2)}) copy-start(f32[512,128]{1,0:T(8,128)} %constant.14.clone.lam) | copy-start | bytes 786436
  53.6 17.0 %all-to-all-start.1 = ((f32[32,40,128]{2,1,0:T(8,128)}), f32[32,40,128]{2,1,0:T(8,128)S(1)}, u32[]{:S(2)}, u32[]{:S(2)}) async-start(f32[32,40,128]{2,1,0:T(8,128)} %shard_map.115), calls=%async_computation.1 | async-start | bytes 1310720 | tf_op jit(solution)/shard_map/all_to_all | solution.py:482
  57.6 11.8 %collective-permute-start.5 = (f32[368,128]{1,0:T(8,128)S(1)}, f32[368,128]{1,0:T(8,128)S(1)}, u32[]{:S(2)}, u32[]{:S(2)}) collective-permute-start(f32[368,128]{1,0:T(8,128)S(1)} %get-tuple-element.34), channel_id=1, source_target_pairs={{0,124},{4,0},{8,4},{12,8},{16,12},{20,16},{24,20},{28,24},{32,28}... | collective-permute-start | bytes 565256 | tf_op jit(solution)/shard_map/ppermute | solution.py:473

commit v3 on v2

v3 whole, which is shorter than its diff:
```python
import functools

import jax
import jax.numpy as jnp
import ml_dtypes
import numpy as np
from jax import lax
from jax.experimental import pallas as pl
from jax.experimental.pallas import tpu as pltpu
from jax.sharding import PartitionSpec as P

F32 = jnp.float32
BF16 = jnp.bfloat16
NZ, NY, NX = 512, 256, 128
GZ, GY = 32, 4
ZC, YC = NZ // GZ, NY // GY
FR = YC + 16
WIDE = FR + 16
WR, WC, RING = 23, 22, 3
LANES = 512
YP, XP = 4, 8
ROW0 = (0, 17, 33, 49)
VMEM_LIMIT = 40 * 1024 * 1024


def segments(block):
    found = [(WC * (row // 4), row) for row in range(block, WR, 4)]
    if block < 3:
        found = [(0, found[-1][1]), (RING - block, found[0][1])] + found[1:]
    return found


def window_places():
    place = np.full((8, LANES), -1000, np.int32)
    for block in range(4):
        parts = segments(block) + [(128, None)]
        for (begin, row), (end, _) in zip(parts[:-1], parts[1:]):
            for lane in range(begin, end):
                column = (lane - WC * (row // 4)) % 128
                if column < WC:
                    place[0, 128 * block + lane] = row
                    place[1, 128 * block + lane] = column
    return place


def tables():
    index = np.arange(NZ, dtype=np.int64)
    phase = (index[:, None] + 1) * (index[None, :] + 1) % (2 * (NZ + 1))
    table = np.sqrt(2.0 / (NZ + 1)) * np.sin(np.pi * phase / (NZ + 1))
    table = table.astype(np.float32)
    high = table.astype(ml_dtypes.bfloat16)
    low = (table - high.astype(np.float32)).astype(ml_dtypes.bfloat16)
    lam = 2.0 - 2.0 * np.cos(np.pi * (index + 1.0) / (NZ + 1))
    lam = np.broadcast_to(lam.astype(np.float32)[:, None], (NZ, 128))
    ahead_high, ahead_low = np.roll(high, 2, 1), np.roll(low, 2, 1)
    return ahead_high, ahead_low, high, low, np.ascontiguousarray(lam), window_places()


def lane_iota(shape):
    return lax.broadcasted_iota(jnp.int32, shape, len(shape) - 1)


def roll(value, shift, axis):
    return pltpu.roll(value, shift % value.shape[axis], axis)


def start_all(pairs, sems):
    copies = [pltpu.make_async_copy(x, y, sems.at[k]) for k, (x, y) in enumerate(pairs)]
    for copy in copies:
        copy.start()
    return copies


def behind_kernel(it, src, out, sems):
    for copy in start_all(
        ((it.at[ZC - 3:ZC], out.at[0:3]), (src.at[ZC - 2:ZC], out.at[3:5])), sems
    ):
        copy.wait()


def edge_kernel(it, src, reg, msk, up, down, it_out, src_out, reg_out, msk_out,
                e_it, e_src, e_reg, e_msk, sems):
    pairs = []
    for side, row in enumerate((0, YC - 8)):
        rows = pl.ds(row, 8)
        pairs += [
            (it.at[:, rows], e_it.at[side]),
            (src.at[:, rows], e_src.at[side]),
            (reg.at[0:1, rows], e_reg.at[side]),
            (msk.at[0:1, rows], e_msk.at[side]),
        ]
    pairs += [
        (it, it_out), (src.at[0:ZC - 2], src_out), (reg.at[0:1], reg_out), (msk.at[0:1], msk_out),
    ]
    copies = start_all(pairs, sems)
    for copy in copies[:-4]:
        copy.wait()
    for z in range(ZC):
        up[5 * z:5 * z + 5] = e_it[1, z, 3:8]
        down[6 * z:6 * z + 6] = e_it[0, z, 0:6]
    for z in range(ZC - 2):
        up[80 + 4 * z:84 + 4 * z] = e_src[1, z, 4:8]
        down[96 + 4 * z:100 + 4 * z] = e_src[0, z, 0:4]
    up[136:141] = e_reg[1, 0, 3:8].astype(F32)
    up[141:145] = e_msk[1, 0, 4:8].astype(F32)
    up[145:152] = jnp.zeros((7, 128), F32)
    down[152:157] = e_reg[0, 0, 0:5].astype(F32)
    down[157:161] = e_msk[0, 0, 0:4].astype(F32)
    down[161:168] = jnp.zeros((7, 128), F32)
    for copy in copies[-4:]:
        copy.wait()


def corner_kernel(zgot, up, down):
    for p in range(3):
        up[5 * p:5 * p + 5] = zgot[p, YC - 5:YC]
        down[6 * p:6 * p + 6] = zgot[p, 0:6]
    for q in range(2):
        up[15 + 4 * q:19 + 4 * q] = zgot[3 + q, YC - 4:YC]
        down[18 + 4 * q:22 + 4 * q] = zgot[3 + q, 0:4]
    up[23:24] = jnp.zeros((1, 128), F32)
    down[26:32] = jnp.zeros((6, 128), F32)


MID = slice(8, 8 + YC)


def edge_lanes():
    lane = lane_iota((FR, 128))
    return lane == 0, lane == 127


def level(frame, p, shift=0):
    return frame[p, 8 + shift:8 + shift + FR]


def set_nu(p, field, right, nu, iron, last):
    u, uz = level(field, p), level(field, p + 1)
    if p == 2:
        uz = jnp.where(lax.axis_index("gz") == 0, 0.0, uz)
    ux = jnp.where(last, 0.0, roll(u, -1, 1))
    right[p] = ux
    dz = uz - u
    dy = level(field, p, 1) - u
    dx = ux - u
    bsq = dz * dz + dy * dy + dx * dx
    bsq = bsq * bsq
    nu[p, 8:8 + FR] = jnp.where(iron, 0.05 + bsq / (bsq + 9.0), 1.0)


def set_residuals(count, field, right, nu, drive, flat, rows, resid, message, first, last):
    start = lax.axis_index("gz") == 0
    copper, held = flat[0] == 1.0, flat[1] == 1.0
    flux = 0.5 * (level(nu, 0) + level(nu, 1)) * (level(field, 0) - level(field, 1))
    for t in range(count):
        p = t + 1
        u, n = level(field, p), level(nu, p)
        uz, nz = level(field, p + 1), level(nu, p + 1)
        if p == 2:
            uz, nz = jnp.where(start, 0.0, uz), jnp.where(start, 1.0, nz)
        if p == 3:
            flux = jnp.where(start, -0.5 * (1.0 + n) * u, flux)
        ahead = 0.5 * (n + nz) * (u - uz)
        flow = ahead - flux
        flux = ahead
        flow = flow + 0.5 * (n + level(nu, p, 1)) * (u - level(field, p, 1))
        flow = flow + 0.5 * (n + level(nu, p, -1)) * (u - level(field, p, -1))
        nx = jnp.where(last, 1.0, roll(n, -1, 1))
        fx = 0.5 * (n + nx) * (u - right[p])
        flow = flow + (fx - jnp.where(first, -0.5 * (n + 1.0) * u, roll(fx, 1, 1)))
        value = -jnp.where(held, u, flow - jnp.where(copper, drive[t], 0.0))
        rows[t * FR:t * FR + FR, :] = value
        if t < 2:
            message[3 * FR + YC * t:3 * FR + YC * t + YC, :] = value[MID]
        else:
            resid[t - 2] = value[MID]


def set_means(total, rows, first, last):
    rows[16 * FR:17 * FR, :] = total
    rows[17 * FR:18 * FR, :] = 2.0 * total + 0.5 * (
        roll(total, -1, 0) + roll(total, 1, 0)
        + jnp.where(last, float(ZC), roll(total, -1, 1))
        + jnp.where(first, float(ZC), roll(total, 1, 1))
    )


def pack(rows, chunks, parts_y, tiles):
    lane = lane_iota((8, 128))
    places = [(lane - 16 * xp) & 127 for xp in range(XP)]
    for yp in parts_y:
        for block in range(4):
            parts = segments(block)
            turned = {}
            for begin, row in parts:
                at = ROW0[yp] + row + 4
                turned[row] = [
                    roll(
                        rows[pl.ds(8 * tile * FR + at, 8, stride=FR), :],
                        WC * (row // 4) + RING, 1,
                    )
                    for tile in tiles
                ]
            for xp in range(XP):
                values = turned[parts[0][1]]
                for begin, row in parts[1:]:
                    later = places[xp] >= begin
                    values = [jnp.where(later, x, y) for x, y in zip(turned[row], values)]
                peer, at = yp * XP + xp, 16 * block
                for tile, value in zip(tiles, values):
                    if tile < 2:
                        chunks[peer, at + 8 * tile:at + 8 * tile + 8, :] = value
                    else:
                        chunks[peer, 64 + 2 * block:66 + 2 * block, :] = value[0:2]


def residual_kernel(it, src, reg, msk, zgot, lo, hi,
                    chunks, nu, resid, message, rows, field, right, drive, flat, rest):
    column = lax.axis_index("gy")

    def below(value):
        return jnp.where(column == 0, 0.0, value)

    def above(value):
        return jnp.where(column == GY - 1, 0.0, value)

    for p in range(3):
        field[p, 16:16 + YC] = zgot[p]
    for z in range(ZC):
        field[z + 3, 16:16 + YC] = it[z]
        field[z + 3, 11:16] = below(lo[5 * z:5 * z + 5])
        field[z + 3, 80:86] = above(hi[6 * z:6 * z + 6])
    for t in range(2):
        drive[t, MID] = zgot[3 + t]
    for z in range(ZC - 2):
        drive[z + 2, MID] = src[z]
        drive[z + 2, 4:8] = lo[80 + 4 * z:84 + 4 * z]
        drive[z + 2, 72:76] = hi[96 + 4 * z:100 + 4 * z]
    flat[0, MID] = reg[0].astype(F32)
    flat[0, 3:8] = below(lo[136:141])
    flat[0, 72:77] = above(hi[152:157])
    flat[1, MID] = msk[0].astype(F32)
    flat[1, 4:8] = lo[141:145]
    flat[1, 72:76] = hi[157:161]
    first, last = edge_lanes()
    iron = flat[0] == 2.0
    for p in range(18):
        set_nu(p, field, right, nu, iron, last)
    total = level(nu, 3)
    for p in range(4, 17):
        total = total + level(nu, p)
    rest[...] = total
    for k in range(3):
        message[FR * k:FR * k + FR, :] = level(nu, 1 + k)
    set_residuals(ZC, field, right, nu, drive, flat, rows, resid, message, first, last)
    set_means(total + (level(nu, 1) + level(nu, 2)), rows, first, last)
    rows[18 * FR:24 * FR, :] = jnp.zeros((6 * FR, 128), F32)
    pack(rows, chunks, (1, 2), (0, 1, 2))
    pack(rows, chunks, (0, 3), (1,))


def corner_residual_kernel(corner_lo, corner_hi, flat, rest, *refs):
    chunks, nu, resid, message, rows, field, right, drive = refs[8:]
    column = lax.axis_index("gy")
    for p in range(3):
        field[p, 11:16] = jnp.where(column == 0, 0.0, corner_lo[5 * p:5 * p + 5])
        field[p, 80:86] = jnp.where(column == GY - 1, 0.0, corner_hi[6 * p:6 * p + 6])
    for t in range(2):
        drive[t, 4:8] = corner_lo[15 + 4 * t:19 + 4 * t]
        drive[t, 72:76] = corner_hi[18 + 4 * t:22 + 4 * t]
    first, last = edge_lanes()
    iron = flat[0] == 2.0
    for p in range(3):
        set_nu(p, field, right, nu, iron, last)
    for k in range(2):
        message[FR * k:FR * k + FR, :] = level(nu, 1 + k)
    set_residuals(3, field, right, nu, drive, flat, rows, resid, message, first, last)
    set_means(rest[...] + (level(nu, 1) + level(nu, 2)), rows, first, last)
    pack(rows, chunks, (0, 3), (0, 2))


def product(high, low, right_high, right_low):
    left = jnp.concatenate([high, low, high], axis=1)
    right = jnp.concatenate([right_high, right_high, right_low], axis=0)
    return jnp.dot(left, right, preferred_element_type=F32)


def modes_kernel(got, ahead_high, ahead_low, high, low, lam, spots, out, lines, back):
    group, column = lax.axis_index("gz"), lax.axis_index("gy")
    yp, xp = lax.div(group, XP), lax.rem(group, XP)
    s_high, s_low = ahead_high[...], ahead_low[...]
    for half in range(2):
        value = jnp.concatenate(
            [
                got[:, 16 * block:16 * block + 16, :].reshape(NZ, 128)
                for block in (2 * half, 2 * half + 1)
            ],
            axis=1,
        )
        v_high = value.astype(BF16)
        v_low = (value - v_high.astype(F32)).astype(BF16)
        lines[:, 256 * half:256 * half + 256] = product(s_high, s_low, v_high, v_low)

    sums = jnp.sum(got[:, 64:72, :], axis=0) * (1.0 / NZ)
    mean = [sums[2 * b:2 * b + 1] for b in range(4)]
    faces = [sums[2 * b + 1:2 * b + 2] for b in range(4)]
    turned = [pltpu.roll(spots[:, 128 * b:128 * b + 128], 16 * xp, 1) for b in range(4)]
    row = jnp.concatenate([place[0:1] for place in turned], axis=1)
    col = jnp.concatenate([place[1:2] for place in turned], axis=1)
    ypos = column * YC + 16 * yp + jnp.where(yp > 0, 1, 0) + row - 4
    xpos = 16 * xp - RING + col
    inside = (row >= 0) & (xpos >= 0) & (xpos < NX) & (ypos >= 0) & (ypos < NY)
    right = [0.5 * (m + roll(m, -1, 1)) for m in mean]
    left = [roll(r, 1, 1) for r in right]
    above = [0.5 * (mean[b] + mean[b + 1]) for b in range(3)]
    above.append(0.5 * (mean[3] + roll(mean[0], -WC, 1)))
    below = [roll(above[3], WC, 1)] + above[:3]

    lam_rows = lam[...]
    vhat = [lines[:, 128 * b:128 * b + 128] for b in range(4)]
    factor = [
        jnp.where(inside[:, 128 * b:128 * b + 128], 0.6 / (faces[b] + lam_rows * mean[b]), 0.0)
        for b in range(4)
    ]
    w = [factor[b] * vhat[b] for b in range(4)]
    for _ in range(3):
        after = w[1:] + [roll(w[0], -WC, 1)]
        before = [roll(w[3], WC, 1)] + w[:3]
        near = [
            above[b] * after[b] + below[b] * before[b]
            + right[b] * roll(w[b], -1, 1) + left[b] * roll(w[b], 1, 1)
            for b in range(4)
        ]
        w = [0.4 * w[b] + factor[b] * (vhat[b] + near[b]) for b in range(4)]
    w = jnp.concatenate(w, axis=1)
    w_high = w.astype(BF16)
    w_low = (w - w_high.astype(F32)).astype(BF16)

    spot = lane_iota((LANES, 384))
    own = jnp.where(yp == 0, 1, 0)
    halo = jnp.where(yp == 0, 0, 16)
    inner = (spot - 16 * xp) & 127
    line = RING + jnp.where(spot < 256, own + 8 * (spot >> 7) + (inner >> 4), halo)
    pick = 128 * (line & 3) + ((WC * (line >> 2) + RING + (spot & 15) + 16 * xp) & 127)
    choose = jnp.where(lax.broadcasted_iota(jnp.int32, (LANES, 384), 0) == pick, 1.0, 0.0)
    choose = choose.astype(BF16)
    s_high, s_low = high[...], low[...]
    w_high = jnp.dot(w_high, choose, preferred_element_type=F32).astype(BF16)
    w_low = jnp.dot(w_low, choose, preferred_element_type=F32).astype(BF16)
    back[8:8 + NZ, :] = product(s_high, s_low, w_high, w_low)
    back[0:8, :] = jnp.zeros((8, 384), F32)
    back[8 + NZ:, :] = jnp.zeros((8, 384), F32)

    sub = lax.broadcasted_iota(jnp.int32, (8, 128), 0)
    pattern = (((lane_iota((8, 128)) >> 4) + sub - xp) & 7) == 0
    for peer in range(GZ):
        at = 8 + ZC * peer
        for block in range(2):
            lanes = slice(128 * block, 128 * block + 128)
            out[peer, 16 * block:16 * block + 16, :] = back[at:at + ZC, lanes]
            out[peer, 32 + block:33 + block, :] = back[at - 1:at, lanes]
            out[peer, 34 + block:35 + block, :] = back[at + ZC:at + ZC + 1, lanes]
            piece = back[at + 8 * block:at + 8 * block + 8, 256:384]
            piece = jnp.sum(jnp.where(pattern, piece, 0.0), axis=0, keepdims=True)
            out[peer, 36 + block:37 + block, :] = piece
        out[peer, 38:40, :] = jnp.zeros((2, 128), F32)


def resid_plane(resid, message, z):
    if z < ZC - 2:
        return resid[z]
    at = 3 * FR + YC * (z - ZC + 2)
    return message[at:at + YC, :]


def image_kernel(got, nu, resid, message, msk, zdir, image, sums, frame):
    lane = lane_iota((8, 128))
    places = [(lane >> 4) == k for k in range(8)]

    def spread(tiles, jj):
        value = tiles[0]
        for xp in range(1, XP):
            value = jnp.where(places[(jj + xp) % 8], tiles[xp], value)
        return roll(value, -16 * jj, 1)

    for yp in range(YP):
        for block in range(2):
            for tile in range(2):
                at = 16 * block + 8 * tile
                tiles = [got[yp * XP + xp, at:at + 8, :] for xp in range(XP)]
                for jj in range(8):
                    y = 8 + 16 * yp + 8 * block + jj
                    frame[pl.ds((1 + 8 * tile) * FR + y, 8, stride=FR), :] = spread(tiles, jj)
        tiles = [got[yp * XP + xp, 32:40, :] for xp in range(XP)]
        for jj in range(8):
            value = spread(tiles, jj)
            y = 8 + 16 * yp + jj
            for k in range(2):
                frame[y + 8 * k:y + 8 * k + 1, :] = value[k:k + 1]
                at = 17 * FR + y + 8 * k
                frame[at:at + 1, :] = value[2 + k:3 + k]

    sub = lax.broadcasted_iota(jnp.int32, (8, 128), 0)
    turn = ((lane >> 4) + sub) & 7
    for yp, y in ((0, 7), (YP - 1, 8 + YC)):
        for tile in range(2):
            value = jnp.zeros((8, 128), F32)
            for xp in range(XP):
                line = got[yp * XP + xp, 36 + tile:37 + tile, :]
                value = jnp.where(turn == xp, jnp.broadcast_to(line, (8, 128)), value)
            value = pltpu.roll(value, 0, 1, stride=16, stride_axis=0)
            frame[pl.ds((1 + 8 * tile) * FR + y, 8, stride=FR), :] = value

    lane = lane_iota((YC, 128))
    first, last = lane == 0, lane == 127
    held = msk[0] == 1

    group = lax.axis_index("gz")

    def nu_rows(z, shift):
        at = 8 + shift
        if z >= ZC - 2:
            value = message[FR * (z - ZC + 2) + at:FR * (z - ZC + 2) + at + YC, :]
        else:
            value = nu[z + 3, at + 8:at + 8 + YC]
        if z == -1:
            value = jnp.where(group == 0, 1.0, value)
        if z == ZC:
            value = jnp.where(group == GZ - 1, 1.0, value)
        return value

    def dir_rows(z, shift):
        at = (z + 1) * FR + 8 + shift
        return frame[at:at + YC, :]

    d, n = dir_rows(0, 0), nu_rows(0, 0)
    flux = 0.5 * (nu_rows(-1, 0) + n) * (dir_rows(-1, 0) - d)
    rr = ri = ii = jnp.zeros((8, 128), F32)

    def fold(value):
        return jnp.sum(value.reshape(YC // 8, 8, 128), axis=0)

    for z in range(ZC):
        dz, nz = dir_rows(z + 1, 0), nu_rows(z + 1, 0)
        ahead = 0.5 * (n + nz) * (d - dz)
        flow = ahead - flux
        flow = flow + 0.5 * (n + nu_rows(z, 1)) * (d - dir_rows(z, 1))
        flow = flow + 0.5 * (n + nu_rows(z, -1)) * (d - dir_rows(z, -1))
        nx = jnp.where(last, 1.0, roll(n, -1, 1))
        dx = jnp.where(last, 0.0, roll(d, -1, 1))
        fx = 0.5 * (n + nx) * (d - dx)
        flow = flow + (fx - jnp.where(first, -0.5 * (n + 1.0) * d, roll(fx, 1, 1)))
        value = jnp.where(held, d, flow)
        zdir[z] = d
        image[z] = value
        r = resid_plane(resid, message, z)
        rr, ri, ii = rr + fold(r * r), ri + fold(r * value), ii + fold(value * value)
        d, n, flux = dz, nz, ahead

    parts = (rr, ri, ii)
    line = lane_iota((1, 128))
    packed = jnp.zeros((1, 128), F32)
    for k, part in enumerate(parts):
        packed = jnp.where(line == k, jnp.sum(part), packed)
    sums[...] = jnp.broadcast_to(packed[None], sums.shape)


def output_kernel(sums, zdir, image, resid, message, correction, lin_residual, rms):
    total = jnp.sum(sums[...], axis=0)
    beta_sq = total[0:1, 0:1] + 1e-06
    beta = jnp.sqrt(beta_sq)
    h_one = total[0:1, 1:2] / beta_sq
    denom = total[0:1, 2:3] / beta_sq - h_one * h_one * (1e-06 / beta_sq) + 1e-06
    gamma = h_one / denom
    correction[...] = zdir[...] * gamma[None]
    for z in range(ZC):
        lin_residual[z] = resid_plane(resid, message, z) - gamma * image[z]
    rms[...] = jnp.broadcast_to(beta * (1.0 / np.sqrt(float(NZ * NY * NX))), rms.shape)


def call(kernel, out_shape, scratch=(), **extra):
    return pl.pallas_call(
        kernel,
        out_shape=out_shape,
        scratch_shapes=scratch,
        compiler_params=pltpu.CompilerParams(vmem_limit_bytes=VMEM_LIMIT),
        **extra,
    )


def struct(*shape):
    return jax.ShapeDtypeStruct(shape, F32)


def cyclic(count, step):
    return [(i, (i + step) % count) for i in range(count)]


def shards(iterate, source, region, fixed_mask):
    far = pl.BlockSpec(memory_space=pltpu.HBM)
    cells = (ZC, YC, 128)
    arguments = [
        pltpu.with_memory_space_constraint(argument, pltpu.HBM)
        for argument in (iterate, source, region, fixed_mask)
    ]
    edge = (2, ZC, 8, 128)
    flat = jax.ShapeDtypeStruct((1, YC, 128), jnp.int32)
    zmsg = call(
        behind_kernel, struct(5, YC, 128),
        scratch=[pltpu.SemaphoreType.DMA((2,))], in_specs=[far] * 2,
    )(*arguments[:2])
    zgot = lax.ppermute(zmsg, "gz", cyclic(GZ, 1))
    up, down, it, src, reg, msk = call(
        edge_kernel,
        (
            struct(152, 128), struct(168, 128),
            struct(*cells), struct(ZC - 2, YC, 128), flat, flat,
        ),
        scratch=[
            pltpu.VMEM(edge, F32), pltpu.VMEM(edge, F32),
            pltpu.VMEM((2, 1, 8, 128), jnp.int32), pltpu.VMEM((2, 1, 8, 128), jnp.int32),
            pltpu.SemaphoreType.DMA((12,)),
        ],
        in_specs=[far] * 4,
    )(*arguments)
    lo = lax.ppermute(up, "gy", cyclic(GY, 1))
    hi = lax.ppermute(down, "gy", cyclic(GY, -1))
    corner_up, corner_down = call(corner_kernel, (struct(24, 128), struct(32, 128)))(zgot)
    corner_lo = lax.ppermute(corner_up, "gy", cyclic(GY, 1))
    corner_hi = lax.ppermute(corner_down, "gy", cyclic(GY, -1))

    kept = (
        struct(GZ, 72, 128), struct(18, WIDE, 128), struct(ZC - 2, YC, 128),
        struct(3 * FR + 2 * YC, 128), struct(24 * FR, 128), struct(19, WIDE, 128),
        struct(18, FR, 128), struct(ZC, FR, 128),
    )
    *early, frames, rest = call(
        residual_kernel, kept + (struct(2, FR, 128), struct(FR, 128))
    )(it, src, reg, msk, zgot, lo, hi)
    chunks, nu, resid, message, *_ = call(
        corner_residual_kernel, kept, input_output_aliases={4 + k: k for k in range(len(kept))}
    )(corner_lo, corner_hi, frames, rest, *early)
    message = lax.ppermute(message, "gz", cyclic(GZ, -1))
    windows = lax.all_to_all(chunks, "gz", 0, 0, tiled=True)
    sent = call(
        modes_kernel,
        struct(GZ, 40, 128),
        scratch=[
            pltpu.VMEM((NZ, LANES), F32), pltpu.VMEM((NZ + 16, 384), F32),
        ],
    )(windows, *[jnp.asarray(table) for table in tables()])
    returned = lax.all_to_all(sent, "gz", 0, 0, tiled=True)
    zdir, image, sums = call(
        image_kernel,
        (struct(*cells), struct(*cells), struct(GZ * GY, 1, 128)),
        scratch=[pltpu.VMEM((18 * FR, 128), F32)],
    )(returned, nu, resid, message, msk)
    sums = lax.all_to_all(sums, ("gz", "gy"), 0, 0, tiled=True)
    correction, lin_residual, rms = call(
        output_kernel, (struct(*cells), struct(*cells), struct(1, 128))
    )(sums, zdir, image, resid, message)
    return correction, lin_residual, rms[0, 0]


def solution(mesh):
    placed = (P("gz", "gy", None),) * 4
    return jax.shard_map(
        shards,
        mesh=mesh,
        in_specs=placed,
        out_specs=(P("gz", "gy", None), P("gz", "gy", None), P()),
        check_vma=False,
    )
```

time: 89.5 us -> 83.8 us (0.936)
  Pallas kernels: 16.2 us -> 13.6 us
  blocking collectives: 42.3 us -> 40.6 us
  waiting for transfers between devices: 16.4 us -> 14.8 us
    all_to_all x1, blocking collectives: 28.2 us -> 26.5 us  [shards(): windows = lax.all_to_all(chunks, 'gz', 0, 0, tiled=True)]
    ppermute x1, waiting for transfers between devices: 1.48 us -> 0.01 us  [shards(): corner_lo = lax.ppermute(corner_up, 'gy', cyclic(GY, 1))]
    pallas_call x1, Pallas kernels: 3.01 us -> 1.55 us  [shards(): call(image_kernel, (struct(*cells), struct(*cells), struct(GZ * GY, 1, 12...]
    pallas_call x1, Pallas kernels: 6.37 us -> 5.17 us  [shards(): call(modes_kernel, struct(GZ, 40, 128), scratch=[pltpu.VMEM((NZ, LANES),...]
    pallas_call x2 -> x4, Pallas kernels: 5.34 us -> 5.38 us  [the longest x1 2.38 us: shards(): call(residual_kernel, kept + (struct(2, FR, 128), struct(FR, 128)))]
  transfers between devices with their start and end apart: 7 -> 7, of which waited for: 4 -> 3; matrix products, arithmetic and copies ran while one was open for 0% -> 0% of each run, Pallas kernels for 0% -> 5%
where the time goes in v3:
time: 83.8 us; the launch traced here: 83.5 us
  blocking collectives  40.6 us (48%)
  waiting for transfers between devices  14.8 us (18%)
  Pallas kernels  13.6 us (16%)
  starting transfers between devices  13.6 us (16%)
    all_to_all x1, blocking collectives, shards(): windows = lax.all_to_all(chunks, 'gz', 0, 0, tiled=True)  26.5 us
    all_to_all x1, blocking collectives, shards(): sums = lax.all_to_all(sums, ('gz', 'gy'), 0, 0, tiled=True)  14.1 us
    ppermute x1, waiting for transfers between devices, shards(): message = lax.ppermute(message, 'gz', cyclic(GZ, -1))  11.4 us
    pallas_call x1, Pallas kernels, shards(): call(modes_kernel, struct(GZ, 40, 128), scratch=[pltpu.VMEM((NZ, LANES),...  5.17 us
    all_to_all x1, starting transfers between devices, shards(): returned = lax.all_to_all(sent, 'gz', 0, 0, tiled=True)  3.95 us
    ppermute x1, starting transfers between devices, shards(): hi = lax.ppermute(down, 'gy', cyclic(GY, -1))  3.83 us
    ppermute x1, starting transfers between devices, shards(): corner_hi = lax.ppermute(corner_down, 'gy', cyclic(GY, -1))  2.74 us
    ppermute x1, starting transfers between devices, shards(): zgot = lax.ppermute(zmsg, 'gz', cyclic(GZ, 1))  2.67 us
  transfers between devices with their start and end apart: 7, of which 3 were waited for; matrix products, arithmetic and copies ran while one was open for 0% of the time, Pallas kernels for 5%

profile of v3, /device:TPU:1, one launch (start us, length us, event | category | flops | bytes accessed | tf_op | source)
XLA Modules:
  0.0 83.5 jit_solution(5293369866785791482)
XLA Ops:
  0.6 0.9 %shard_map.121 = f32[5,64,128]{2,1,0:T(8,128)S(1)} custom-call(f32[16,64,128]{2,1,0:T(8,128)} %it.3, f32[16,64,128]{2,1,0:T(8,128)} %src.3), custom_call_target="tpu_custom_call" | custom-call | tf_op jit(solution)/shard_map/pallas_call | solution.py:508
  1.6 2.7 %collective-permute-start = (f32[5,64,128]{2,1,0:T(8,128)S(1)}, f32[5,64,128]{2,1,0:T(8,128)S(1)}, u32[]{:S(2)}, u32[]{:S(2)}) collective-permute-start(f32[5,64,128]{2,1,0:T(8,128)S(1)} %shard_map.121), channel_id=1, source_target_pairs={{0,4},{4,8},{8,12},{12,16},{16,20},{20,24},{24,28},{28,32},{32,36}... | collective-permute-start | bytes 491528 | tf_op jit(solution)/shard_map/ppermute | solution.py:512
  4.2 1.5 %shard_map.123 = (f32[152,128]{1,0:T(8,128)S(1)}, f32[168,128]{1,0:T(8,128)S(1)}, f32[16,64,128]{2,1,0:T(8,128)S(1)}, f32[14,64,128]{2,1,0:T(8,128)S(1)}, s32[1,...) custom-call(f32[16,64,128]{2,1,0:T(8,128)} %it.3, f32[16,64,128]{2,1,0:T(8,128)} %src.3, s32[16,64,128]{2,1,0:T(8,128)} %reg.1, ...), custom_call_target="tpu_custom_call" | custom-call | tf_op jit(solution)/shard_map/pallas_call | solution.py:513
  5.7 3.8 %collective-permute-start.4 = (f32[168,128]{1,0:T(8,128)S(1)}, f32[168,128]{1,0:T(8,128)S(1)}, u32[]{:S(2)}, u32[]{:S(2)}) collective-permute-start(f32[168,128]{1,0:T(8,128)S(1)} %get-tuple-element.38), channel_id=1, source_target_pairs={{0,3},{1,0},{2,1},{3,2},{4,7},{5,4},{6,5},{7,6},{8,11},{9,8},{10,9... | collective-permute-start | bytes 258056 | tf_op jit(solution)/shard_map/ppermute | solution.py:527
  9.6 0.0 collective-permute-start.3
  9.6 2.7 %collective-permute-start.2 = (f32[32,128]{1,0:T(8,128)S(1)}, f32[32,128]{1,0:T(8,128)S(1)}, u32[]{:S(2)}, u32[]{:S(2)}) collective-permute-start(f32[32,128]{1,0:T(8,128)S(1)} %get-tuple-element.32), channel_id=1, source_target_pairs={{0,3},{1,0},{2,1},{3,2},{4,7},{5,4},{6,5},{7,6},{8,11},{9,8},{10,9... | collective-permute-start | bytes 49160 | tf_op jit(solution)/shard_map/ppermute | solution.py:530
  12.3 2.2 %collective-permute-done.3.lo = f32[152,128]{1,0:T(8,128)S(1)} collective-permute-done((f32[152,128]{1,0:T(8,128)S(1)}, f32[152,128]{1,0:T(8,128)S(1)}, u32[]{:S(2)}, u32[]{:S(2)}) %collective-permute-start.3) | collective-permute-done | bytes 77856 | tf_op jit(solution)/shard_map/ppermute | solution.py:526
  14.5 2.4 %shard_map.124 = (f32[32,72,128]{2,1,0:T(8,128)S(1)}, f32[18,96,128]{2,1,0:T(8,128)S(1)}, f32[14,64,128]{2,1,0:T(8,128)S(1)}, f32[368,128]{1,0:T(8,128)S(1)}, f3...) custom-call(f32[16,64,128]{2,1,0:T(8,128)S(1)} %get-tuple-element.33, ...), custom_call_target="tpu_custom_call" | custom-call | tf_op jit(solution)/shard_map/pallas_call | solution.py:537
  16.9 0.0 copy-start.5
  16.9 0.6 shard_map.125
  17.5 0.0 copy-start
  17.5 0.0 copy-start.1
  17.6 0.0 copy-start.2
  17.6 0.0 copy-start.3
  17.6 0.0 copy-start.4
  17.6 26.5 %all_to_all.15.got = f32[32,72,128]{2,1,0:T(8,128)S(1)} all-to-all(f32[32,72,128]{2,1,0:T(8,128)S(1)} %get-tuple-element.49), channel_id=1, replica_groups=mesh['gz'=32,'gy'=4] {'gz'}, dimensions={0} | all-to-all | bytes 2359296 | tf_op jit(solution)/shard_map/all_to_all | solution.py:544
  44.2 5.2 %shard_map.126 = f32[32,40,128]{2,1,0:T(8,128)} custom-call(f32[32,72,128]{2,1,0:T(8,128)S(1)} %all_to_all.15.got, bf16[512,512]{1,0:T(8,128)(2,1)S(1)} %copy-done.3, bf16[512,512]{1,0:T(8,128)(2,1)S(1)} %copy-done.2, bf16[512,512]{1,0:T(8,128)(2,1)S(1)} %copy-done.1, bf16[512,512]{1,0:T(8,128)(2,1)S(1)} %copy-done, f32[512,128]{1,0:T(8,128)S(1)} %copy-done.4, ...), custom_call_target="tpu_custom_call" | custom-call | tf_op jit(solution)/shard_map/pallas_call | solution.py:545
  49.3 4.0 %all-to-all-start.1 = ((f32[32,40,128]{2,1,0:T(8,128)}), f32[32,40,128]{2,1,0:T(8,128)S(1)}, u32[]{:S(2)}, u32[]{:S(2)}) async-start(f32[32,40,128]{2,1,0:T(8,128)} %shard_map.126), calls=%async_computation.1 | async-start | bytes 1310720 | tf_op jit(solution)/shard_map/all_to_all | solution.py:552
  53.3 0.4 collective-permute-start.5
  53.7 11.4 %collective-permute-done.5.message = f32[368,128]{1,0:T(8,128)S(1)} collective-permute-done((f32[368,128]{1,0:T(8,128)S(1)}, f32[368,128]{1,0:T(8,128)S(1)}, u32[]{:S(2)}, u32[]{:S(2)}) %collective-permute-start.5) | collective-permute-done | bytes 188448 | tf_op jit(solution)/shard_map/ppermute | solution.py:543
  65.1 1.2 %all-to-all-done.1.got = f32[32,40,128]{2,1,0:T(8,128)S(1)} async-done(((f32[32,40,128]{2,1,0:T(8,128)}), f32[32,40,128]{2,1,0:T(8,128)S(1)}, u32[]{:S(2)}, u32[]{:S(2)}) %all-to-all-start.1) | async-done | bytes 655392 | tf_op jit(solution)/shard_map/all_to_all | solution.py:552
  66.3 1.5 %shard_map.127 = (f32[16,64,128]{2,1,0:T(8,128)S(1)}, f32[16,64,128]{2,1,0:T(8,128)S(1)}, f32[128,1,128]{2,1,0:T(1,128)S(1)}) custom-call(f32[32,40,128]{2,1,0:T(8,128)S(1)} %all-to-all-done.1.got, f32[18,96,128]{2,1,0:T(8,128)S(1)} %get-tuple-element.50.nu, f32[14,64,128]{2,1,0:T(8,128)S(1)} %get-tuple-element.51.resid, ...), custom_call_target="tpu_custom_call" | custom-call | tf_op jit(solution)/shard_map/pallas_call | solution.py:553
  67.9 14.1 %all_to_all.16.sums = f32[128,1,128]{2,1,0:T(1,128)S(1)} all-to-all(f32[128,1,128]{2,1,0:T(1,128)S(1)} %get-tuple-element.53), channel_id=1, replica_groups=mesh['gz'=32,'gy'=4] {'gz','gy'}, dimensions={0} | all-to-all | bytes 131072 | tf_op jit(solution)/shard_map/all_to_all | solution.py:558
  82.0 1.5 %shard_map.128 = (f32[16,64,128]{2,1,0:T(8,128)}, f32[16,64,128]{2,1,0:T(8,128)}, f32[1,128]{1,0:T(1,128)}) custom-call(f32[128,1,128]{2,1,0:T(1,128)S(1)} %all_to_all.16.sums, f32[16,64,128]{2,1,0:T(8,128)S(1)} %get-tuple-element.54.zdir, f32[16,64,128]{2,1,0:T(8,128)S(1)} %get-tuple-element.55.image, f32[14,64,128]{2,1,0:T(8,128)S(1)} %get-tuple-element.51.resid, ...), custom_call_target="tpu_custom_call" | custom-call | tf_op jit(solution)/shard_map/pallas_call | solution.py:559
  (12 shorter events, 0.0 us)
Async XLA Ops:
  1.6 8.0 %collective-permute-start = (f32[5,64,128]{2,1,0:T(8,128)S(1)}, f32[5,64,128]{2,1,0:T(8,128)S(1)}, u32[]{:S(2)}, u32[]{:S(2)}) collective-permute-start(f32[5,64,128]{2,1,0:T(8,128)S(1)} %shard_map.121), channel_id=1, source_target_pairs={{0,4},{4,8},{8,12},{12,16},{16,20},{20,24},{24,28},{28,32},{32,36}... | collective-permute-start | bytes 491528 | tf_op jit(solution)/shard_map/ppermute | solution.py:512
  5.7 8.8 %collective-permute-start.4 = (f32[168,128]{1,0:T(8,128)S(1)}, f32[168,128]{1,0:T(8,128)S(1)}, u32[]{:S(2)}, u32[]{:S(2)}) collective-permute-start(f32[168,128]{1,0:T(8,128)S(1)} %get-tuple-element.38), channel_id=1, source_target_pairs={{0,3},{1,0},{2,1},{3,2},{4,7},{5,4},{6,5},{7,6},{8,11},{9,8},{10,9... | collective-permute-start | bytes 258056 | tf_op jit(solution)/shard_map/ppermute | solution.py:527
  9.6 5.0 %collective-permute-start.3 = (f32[152,128]{1,0:T(8,128)S(1)}, f32[152,128]{1,0:T(8,128)S(1)}, u32[]{:S(2)}, u32[]{:S(2)}) collective-permute-start(f32[152,128]{1,0:T(8,128)S(1)} %get-tuple-element.37), channel_id=1, source_target_pairs={{0,1},{1,2},{2,3},{3,0},{4,5},{5,6},{6,7},{7,4},{8,9},{9,10},{10,1... | collective-permute-start | bytes 233480 | tf_op jit(solution)/shard_map/ppermute | solution.py:526
  9.6 7.3 %collective-permute-start.2 = (f32[32,128]{1,0:T(8,128)S(1)}, f32[32,128]{1,0:T(8,128)S(1)}, u32[]{:S(2)}, u32[]{:S(2)}) collective-permute-start(f32[32,128]{1,0:T(8,128)S(1)} %get-tuple-element.32), channel_id=1, source_target_pairs={{0,3},{1,0},{2,1},{3,2},{4,7},{5,4},{6,5},{7,6},{8,11},{9,8},{10,9... | collective-permute-start | bytes 49160 | tf_op jit(solution)/shard_map/ppermute | solution.py:530
  12.3 4.6 %collective-permute-start.1 = (f32[24,128]{1,0:T(8,128)S(1)}, f32[24,128]{1,0:T(8,128)S(1)}, u32[]{:S(2)}, u32[]{:S(2)}) collective-permute-start(f32[24,128]{1,0:T(8,128)S(1)} %get-tuple-element.31), channel_id=1, source_target_pairs={{0,1},{1,2},{2,3},{3,0},{4,5},{5,6},{6,7},{7,4},{8,9},{9,10},{10,1... | collective-permute-start | bytes 36872 | tf_op jit(solution)/shard_map/ppermute | solution.py:529
  16.9 27.2 %copy-start.5 = (s32[8,512]{1,0:T(8,128)S(1)}, s32[8,512]{1,0:T(8,128)}, u32[]{:S(2)}) copy-start(s32[8,512]{1,0:T(8,128)} %constant.17.clone.spots) | copy-start | bytes 49156
  17.5 26.6 %copy-start = (bf16[512,512]{1,0:T(8,128)(2,1)S(1)}, bf16[512,512]{1,0:T(8,128)(2,1)}, u32[]{:S(2)}) copy-start(bf16[512,512]{1,0:T(8,128)(2,1)} %constant.15.clone.low) | copy-start | bytes 1572868
  17.5 26.6 %copy-start.1 = (bf16[512,512]{1,0:T(8,128)(2,1)S(1)}, bf16[512,512]{1,0:T(8,128)(2,1)}, u32[]{:S(2)}) copy-start(bf16[512,512]{1,0:T(8,128)(2,1)} %constant.14.clone.high) | copy-start | bytes 1572868
  17.6 26.6 %copy-start.2 = (bf16[512,512]{1,0:T(8,128)(2,1)S(1)}, bf16[512,512]{1,0:T(8,128)(2,1)}, u32[]{:S(2)}) copy-start(bf16[512,512]{1,0:T(8,128)(2,1)} %constant.13.clone.ahead_low) | copy-start | bytes 1572868
  17.6 26.6 %copy-start.3 = (bf16[512,512]{1,0:T(8,128)(2,1)S(1)}, bf16[512,512]{1,0:T(8,128)(2,1)}, u32[]{:S(2)}) copy-start(bf16[512,512]{1,0:T(8,128)(2,1)} %constant.12.clone.ahead_high) | copy-start | bytes 1572868
  17.6 26.6 %copy-start.4 = (f32[512,128]{1,0:T(8,128)S(1)}, f32[512,128]{1,0:T(8,128)}, u32[]{:S(2)}) copy-start(f32[512,128]{1,0:T(8,128)} %constant.16.clone.lam) | copy-start | bytes 786436
  49.3 17.0 %all-to-all-start.1 = ((f32[32,40,128]{2,1,0:T(8,128)}), f32[32,40,128]{2,1,0:T(8,128)S(1)}, u32[]{:S(2)}, u32[]{:S(2)}) async-start(f32[32,40,128]{2,1,0:T(8,128)} %shard_map.126), calls=%async_computation.1 | async-start | bytes 1310720 | tf_op jit(solution)/shard_map/all_to_all | solution.py:552
  53.3 11.8 %collective-permute-start.5 = (f32[368,128]{1,0:T(8,128)S(1)}, f32[368,128]{1,0:T(8,128)S(1)}, u32[]{:S(2)}, u32[]{:S(2)}) collective-permute-start(f32[368,128]{1,0:T(8,128)S(1)} %get-tuple-element.52), channel_id=1, source_target_pairs={{0,124},{4,0},{8,4},{12,8},{16,12},{20,16},{24,20},{28,24},{32,28}... | collective-permute-start | bytes 565256 | tf_op jit(solution)/shard_map/ppermute | solution.py:543

commit v4 on v3

--- a/solution.py
+++ b/solution.py
@@ -21,6 +21,7 @@
 YP, XP = 4, 8
 ROW0 = (0, 17, 33, 49)
 VMEM_LIMIT = 40 * 1024 * 1024
+COST = pl.CostEstimate(flops=4_000_000, bytes_accessed=8_000_000, transcendentals=0)
 
 
 def segments(block):
@@ -71,16 +72,8 @@
     return copies
 
 
-def behind_kernel(it, src, out, sems):
-    for copy in start_all(
-        ((it.at[ZC - 3:ZC], out.at[0:3]), (src.at[ZC - 2:ZC], out.at[3:5])), sems
-    ):
-        copy.wait()
-
-
-def edge_kernel(it, src, reg, msk, up, down, it_out, src_out, reg_out, msk_out,
-                e_it, e_src, e_reg, e_msk, sems):
-    pairs = []
+def edge_kernel(it, src, reg, msk, zmsg, up, down, e_it, e_src, e_reg, e_msk, sems):
+    pairs = [(it.at[ZC - 3:ZC], zmsg.at[0:3]), (src.at[ZC - 2:ZC], zmsg.at[3:5])]
     for side, row in enumerate((0, YC - 8)):
         rows = pl.ds(row, 8)
         pairs += [
@@ -89,73 +82,73 @@
             (reg.at[0:1, rows], e_reg.at[side]),
             (msk.at[0:1, rows], e_msk.at[side]),
         ]
-    pairs += [
-        (it, it_out), (src.at[0:ZC - 2], src_out), (reg.at[0:1], reg_out), (msk.at[0:1], msk_out),
-    ]
     copies = start_all(pairs, sems)
-    for copy in copies[:-4]:
+    for copy in copies[2:]:
         copy.wait()
     for z in range(ZC):
         up[5 * z:5 * z + 5] = e_it[1, z, 3:8]
         down[6 * z:6 * z + 6] = e_it[0, z, 0:6]
-    for z in range(ZC - 2):
         up[80 + 4 * z:84 + 4 * z] = e_src[1, z, 4:8]
         down[96 + 4 * z:100 + 4 * z] = e_src[0, z, 0:4]
-    up[136:141] = e_reg[1, 0, 3:8].astype(F32)
-    up[141:145] = e_msk[1, 0, 4:8].astype(F32)
-    up[145:152] = jnp.zeros((7, 128), F32)
-    down[152:157] = e_reg[0, 0, 0:5].astype(F32)
-    down[157:161] = e_msk[0, 0, 0:4].astype(F32)
-    down[161:168] = jnp.zeros((7, 128), F32)
-    for copy in copies[-4:]:
+    up[144:149] = e_reg[1, 0, 3:8].astype(F32)
+    up[149:153] = e_msk[1, 0, 4:8].astype(F32)
+    up[153:160] = jnp.zeros((7, 128), F32)
+    down[160:165] = e_reg[0, 0, 0:5].astype(F32)
+    down[165:169] = e_msk[0, 0, 0:4].astype(F32)
+    down[169:176] = jnp.zeros((7, 128), F32)
+    for copy in copies[:2]:
         copy.wait()
 
 
-def corner_kernel(zgot, up, down):
-    for p in range(3):
-        up[5 * p:5 * p + 5] = zgot[p, YC - 5:YC]
-        down[6 * p:6 * p + 6] = zgot[p, 0:6]
-    for q in range(2):
-        up[15 + 4 * q:19 + 4 * q] = zgot[3 + q, YC - 4:YC]
-        down[18 + 4 * q:22 + 4 * q] = zgot[3 + q, 0:4]
-    up[23:24] = jnp.zeros((1, 128), F32)
-    down[26:32] = jnp.zeros((6, 128), F32)
-
-
-MID = slice(8, 8 + YC)
-
-
-def edge_lanes():
-    lane = lane_iota((FR, 128))
+def corner_kernel(lo, hi, out):
+    out[0:15] = lo[65:80]
+    out[15:33] = hi[78:96]
+    out[33:41] = lo[136:144]
+    out[41:49] = hi[152:160]
+    out[49:56] = jnp.zeros((7, 128), F32)
+
+
+INNER, OUTER = ((8, YC),), ((0, 16), (YC, 16))
+
+
+def edge_lanes(count):
+    lane = lane_iota((count, 128))
     return lane == 0, lane == 127
 
 
-def level(frame, p, shift=0):
-    return frame[p, 8 + shift:8 + shift + FR]
-
-
-def set_nu(p, field, right, nu, iron, last):
-    u, uz = level(field, p), level(field, p + 1)
+def level(frame, p, span, shift=0):
+    return frame[p, pl.ds(8 + span[0] + shift, span[1])]
+
+
+def set_nu(p, span, field, right, nu, iron, last):
+    u, uz = level(field, p, span), level(field, p + 1, span)
     if p == 2:
         uz = jnp.where(lax.axis_index("gz") == 0, 0.0, uz)
     ux = jnp.where(last, 0.0, roll(u, -1, 1))
-    right[p] = ux
+    right[p, pl.ds(*span)] = ux
     dz = uz - u
-    dy = level(field, p, 1) - u
+    dy = level(field, p, span, 1) - u
     dx = ux - u
     bsq = dz * dz + dy * dy + dx * dx
     bsq = bsq * bsq
-    nu[p, 8:8 + FR] = jnp.where(iron, 0.05 + bsq / (bsq + 9.0), 1.0)
-
-
-def set_residuals(count, field, right, nu, drive, flat, rows, resid, message, first, last):
+    nu[p, pl.ds(8 + span[0], span[1])] = jnp.where(iron, 0.05 + bsq / (bsq + 9.0), 1.0)
+
+
+def set_residuals(span, steps, field, right, nu, drive, flat, rows, resid, message, first, last):
     start = lax.axis_index("gz") == 0
-    copper, held = flat[0] == 1.0, flat[1] == 1.0
-    flux = 0.5 * (level(nu, 0) + level(nu, 1)) * (level(field, 0) - level(field, 1))
-    for t in range(count):
+    begin, count = span
+    copper, held = flat[0, pl.ds(*span)] == 1.0, flat[1, pl.ds(*span)] == 1.0
+    own = max(begin, 8)
+    own = slice(own - begin, min(begin + count, 8 + YC) - begin)
+    kept = pl.ds(begin + own.start - 8, own.stop - own.start)
+    p = steps[0]
+    flux = 0.5 * (level(nu, p, span) + level(nu, p + 1, span)) * (
+        level(field, p, span) - level(field, p + 1, span)
+    )
+    for t in steps:
         p = t + 1
-        u, n = level(field, p), level(nu, p)
-        uz, nz = level(field, p + 1), level(nu, p + 1)
+        u, n = level(field, p, span), level(nu, p, span)
+        uz, nz = level(field, p + 1, span), level(nu, p + 1, span)
         if p == 2:
             uz, nz = jnp.where(start, 0.0, uz), jnp.where(start, 1.0, nz)
         if p == 3:
@@ -163,26 +156,53 @@
         ahead = 0.5 * (n + nz) * (u - uz)
         flow = ahead - flux
         flux = ahead
-        flow = flow + 0.5 * (n + level(nu, p, 1)) * (u - level(field, p, 1))
-        flow = flow + 0.5 * (n + level(nu, p, -1)) * (u - level(field, p, -1))
+        flow = flow + 0.5 * (n + level(nu, p, span, 1)) * (u - level(field, p, span, 1))
+        flow = flow + 0.5 * (n + level(nu, p, span, -1)) * (u - level(field, p, span, -1))
         nx = jnp.where(last, 1.0, roll(n, -1, 1))
-        fx = 0.5 * (n + nx) * (u - right[p])
+        fx = 0.5 * (n + nx) * (u - right[p, pl.ds(*span)])
         flow = flow + (fx - jnp.where(first, -0.5 * (n + 1.0) * u, roll(fx, 1, 1)))
-        value = -jnp.where(held, u, flow - jnp.where(copper, drive[t], 0.0))
-        rows[t * FR:t * FR + FR, :] = value
+        value = -jnp.where(held, u, flow - jnp.where(copper, drive[t, pl.ds(*span)], 0.0))
+        rows[pl.ds(t * FR + begin, count), :] = value
         if t < 2:
-            message[3 * FR + YC * t:3 * FR + YC * t + YC, :] = value[MID]
+            message[pl.ds(3 * FR + YC * t + kept.start, kept.size), :] = value[own]
         else:
-            resid[t - 2] = value[MID]
-
-
-def set_means(total, rows, first, last):
-    rows[16 * FR:17 * FR, :] = total
-    rows[17 * FR:18 * FR, :] = 2.0 * total + 0.5 * (
-        roll(total, -1, 0) + roll(total, 1, 0)
+            resid[t - 2, kept] = value[own]
+
+
+def set_means(span, rows, first, last):
+    begin, count = 16 * FR + span[0], span[1]
+    total = rows[pl.ds(begin, count), :]
+    rows[pl.ds(begin + FR, count), :] = 2.0 * total + 0.5 * (
+        rows[pl.ds(begin - 1, count), :] + rows[pl.ds(begin + 1, count), :]
         + jnp.where(last, float(ZC), roll(total, -1, 1))
         + jnp.where(first, float(ZC), roll(total, 1, 1))
     )
+
+
+def work(spans, planes, steps, field, right, nu, drive, flat, rows, resid, message):
+    for span in spans:
+        first, last = edge_lanes(span[1])
+        iron = flat[0, pl.ds(*span)] == 2.0
+        for p in planes:
+            set_nu(p, span, field, right, nu, iron, last)
+        for p in planes:
+            if 1 <= p < 4:
+                message[pl.ds(FR * (p - 1) + span[0], span[1]), :] = level(nu, p, span)
+    for span in spans:
+        first, last = edge_lanes(span[1])
+        set_residuals(
+            span, steps, field, right, nu, drive, flat, rows, resid, message, first, last
+        )
+
+
+def sum_planes(spans, nu, rows):
+    for span in spans:
+        total = level(nu, 1, span)
+        for p in range(2, 17):
+            total = total + level(nu, p, span)
+        rows[pl.ds(16 * FR + span[0], span[1]), :] = total
+    for span in spans:
+        set_means(span, rows, *edge_lanes(span[1]))
 
 
 def pack(rows, chunks, parts_y, tiles):
@@ -214,8 +234,30 @@
                         chunks[peer, 64 + 2 * block:66 + 2 * block, :] = value[0:2]
 
 
-def residual_kernel(it, src, reg, msk, zgot, lo, hi,
-                    chunks, nu, resid, message, rows, field, right, drive, flat, rest):
+BEHIND, HERE = range(0, 3), range(3, 18)
+
+
+def inner_kernel(it, src, reg, msk, chunks, nu, resid, message, rows, field, right, drive, flat,
+                 reg_in, msk_in, sems):
+    own = slice(8, 8 + YC)
+    copies = start_all(
+        (
+            (it, field.at[3:19, 16:16 + YC]), (src.at[0:ZC - 2], drive.at[2:ZC, own]),
+            (reg.at[0:1], reg_in), (msk.at[0:1], msk_in),
+        ),
+        sems,
+    )
+    rows[18 * FR:24 * FR, :] = jnp.zeros((6 * FR, 128), F32)
+    for copy in copies:
+        copy.wait()
+    flat[0, own] = reg_in[0].astype(F32)
+    flat[1, own] = msk_in[0].astype(F32)
+    work(INNER, HERE, range(3, ZC), field, right, nu, drive, flat, rows, resid, message)
+    pack(rows, chunks, (1, 2), (1,))
+
+
+def halo_kernel(zgot, lo, hi, *refs):
+    chunks, nu, resid, message, rows, field, right, drive, flat = refs[9:]
     column = lax.axis_index("gy")
 
     def below(value):
@@ -227,55 +269,35 @@
     for p in range(3):
         field[p, 16:16 + YC] = zgot[p]
     for z in range(ZC):
-        field[z + 3, 16:16 + YC] = it[z]
         field[z + 3, 11:16] = below(lo[5 * z:5 * z + 5])
         field[z + 3, 80:86] = above(hi[6 * z:6 * z + 6])
     for t in range(2):
-        drive[t, MID] = zgot[3 + t]
+        drive[t, 8:8 + YC] = zgot[3 + t]
     for z in range(ZC - 2):
-        drive[z + 2, MID] = src[z]
         drive[z + 2, 4:8] = lo[80 + 4 * z:84 + 4 * z]
         drive[z + 2, 72:76] = hi[96 + 4 * z:100 + 4 * z]
-    flat[0, MID] = reg[0].astype(F32)
-    flat[0, 3:8] = below(lo[136:141])
-    flat[0, 72:77] = above(hi[152:157])
-    flat[1, MID] = msk[0].astype(F32)
-    flat[1, 4:8] = lo[141:145]
-    flat[1, 72:76] = hi[157:161]
-    first, last = edge_lanes()
-    iron = flat[0] == 2.0
-    for p in range(18):
-        set_nu(p, field, right, nu, iron, last)
-    total = level(nu, 3)
-    for p in range(4, 17):
-        total = total + level(nu, p)
-    rest[...] = total
-    for k in range(3):
-        message[FR * k:FR * k + FR, :] = level(nu, 1 + k)
-    set_residuals(ZC, field, right, nu, drive, flat, rows, resid, message, first, last)
-    set_means(total + (level(nu, 1) + level(nu, 2)), rows, first, last)
-    rows[18 * FR:24 * FR, :] = jnp.zeros((6 * FR, 128), F32)
-    pack(rows, chunks, (1, 2), (0, 1, 2))
+    flat[0, 3:8] = below(lo[144:149])
+    flat[0, 72:77] = above(hi[160:165])
+    flat[1, 4:8] = lo[149:153]
+    flat[1, 72:76] = hi[165:169]
+    work(INNER, BEHIND, range(0, 3), field, right, nu, drive, flat, rows, resid, message)
+    work(OUTER, HERE, range(3, ZC), field, right, nu, drive, flat, rows, resid, message)
+    sum_planes(INNER, nu, rows)
+    pack(rows, chunks, (1, 2), (0, 2))
     pack(rows, chunks, (0, 3), (1,))
 
 
-def corner_residual_kernel(corner_lo, corner_hi, flat, rest, *refs):
-    chunks, nu, resid, message, rows, field, right, drive = refs[8:]
+def corner_residual_kernel(corners, *refs):
+    chunks, nu, resid, message, rows, field, right, drive, flat = refs[9:]
     column = lax.axis_index("gy")
     for p in range(3):
-        field[p, 11:16] = jnp.where(column == 0, 0.0, corner_lo[5 * p:5 * p + 5])
-        field[p, 80:86] = jnp.where(column == GY - 1, 0.0, corner_hi[6 * p:6 * p + 6])
+        field[p, 11:16] = jnp.where(column == 0, 0.0, corners[5 * p:5 * p + 5])
+        field[p, 80:86] = jnp.where(column == GY - 1, 0.0, corners[15 + 6 * p:21 + 6 * p])
     for t in range(2):
-        drive[t, 4:8] = corner_lo[15 + 4 * t:19 + 4 * t]
-        drive[t, 72:76] = corner_hi[18 + 4 * t:22 + 4 * t]
-    first, last = edge_lanes()
-    iron = flat[0] == 2.0
-    for p in range(3):
-        set_nu(p, field, right, nu, iron, last)
-    for k in range(2):
-        message[FR * k:FR * k + FR, :] = level(nu, 1 + k)
-    set_residuals(3, field, right, nu, drive, flat, rows, resid, message, first, last)
-    set_means(rest[...] + (level(nu, 1) + level(nu, 2)), rows, first, last)
+        drive[t, 4:8] = corners[33 + 4 * t:37 + 4 * t]
+        drive[t, 72:76] = corners[41 + 4 * t:45 + 4 * t]
+    work(OUTER, BEHIND, range(0, 3), field, right, nu, drive, flat, rows, resid, message)
+    sum_planes(OUTER, nu, rows)
     pack(rows, chunks, (0, 3), (0, 2))
 
 
@@ -316,26 +338,6 @@
     above.append(0.5 * (mean[3] + roll(mean[0], -WC, 1)))
     below = [roll(above[3], WC, 1)] + above[:3]
 
-    lam_rows = lam[...]
-    vhat = [lines[:, 128 * b:128 * b + 128] for b in range(4)]
-    factor = [
-        jnp.where(inside[:, 128 * b:128 * b + 128], 0.6 / (faces[b] + lam_rows * mean[b]), 0.0)
-        for b in range(4)
-    ]
-    w = [factor[b] * vhat[b] for b in range(4)]
-    for _ in range(3):
-        after = w[1:] + [roll(w[0], -WC, 1)]
-        before = [roll(w[3], WC, 1)] + w[:3]
-        near = [
-            above[b] * after[b] + below[b] * before[b]
-            + right[b] * roll(w[b], -1, 1) + left[b] * roll(w[b], 1, 1)
-            for b in range(4)
-        ]
-        w = [0.4 * w[b] + factor[b] * (vhat[b] + near[b]) for b in range(4)]
-    w = jnp.concatenate(w, axis=1)
-    w_high = w.astype(BF16)
-    w_low = (w - w_high.astype(F32)).astype(BF16)
-
     spot = lane_iota((LANES, 384))
     own = jnp.where(yp == 0, 1, 0)
     halo = jnp.where(yp == 0, 0, 16)
@@ -345,9 +347,33 @@
     choose = jnp.where(lax.broadcasted_iota(jnp.int32, (LANES, 384), 0) == pick, 1.0, 0.0)
     choose = choose.astype(BF16)
     s_high, s_low = high[...], low[...]
-    w_high = jnp.dot(w_high, choose, preferred_element_type=F32).astype(BF16)
-    w_low = jnp.dot(w_low, choose, preferred_element_type=F32).astype(BF16)
-    back[8:8 + NZ, :] = product(s_high, s_low, w_high, w_low)
+    total = None
+    for start in range(0, NZ, 128):
+        part = slice(start, start + 128)
+        lam_rows = lam[part, :]
+        vhat = [lines[part, 128 * b:128 * b + 128] for b in range(4)]
+        factor = [
+            jnp.where(inside[:, 128 * b:128 * b + 128], 0.6 / (faces[b] + lam_rows * mean[b]), 0.0)
+            for b in range(4)
+        ]
+        w = [factor[b] * vhat[b] for b in range(4)]
+        for _ in range(3):
+            after = w[1:] + [roll(w[0], -WC, 1)]
+            before = [roll(w[3], WC, 1)] + w[:3]
+            near = [
+                above[b] * after[b] + below[b] * before[b]
+                + right[b] * roll(w[b], -1, 1) + left[b] * roll(w[b], 1, 1)
+                for b in range(4)
+            ]
+            w = [0.4 * w[b] + factor[b] * (vhat[b] + near[b]) for b in range(4)]
+        w = jnp.concatenate(w, axis=1)
+        w_high = w.astype(BF16)
+        w_low = (w - w_high.astype(F32)).astype(BF16)
+        w_high = jnp.dot(w_high, choose, preferred_element_type=F32).astype(BF16)
+        w_low = jnp.dot(w_low, choose, preferred_element_type=F32).astype(BF16)
+        term = product(high[:, part], low[:, part], w_high, w_low)
+        total = term if total is None else total + term
+    back[8:8 + NZ, :] = total
     back[0:8, :] = jnp.zeros((8, 384), F32)
     back[8 + NZ:, :] = jnp.zeros((8, 384), F32)
 
@@ -373,7 +399,7 @@
     return message[at:at + YC, :]
 
 
-def image_kernel(got, nu, resid, message, msk, zdir, image, sums, frame):
+def image_kernel(got, nu, resid, message, flat, zdir, image, sums, frame):
     lane = lane_iota((8, 128))
     places = [(lane >> 4) == k for k in range(8)]
 
@@ -413,7 +439,7 @@
 
     lane = lane_iota((YC, 128))
     first, last = lane == 0, lane == 127
-    held = msk[0] == 1
+    held = flat[1, 8:8 + YC] == 1.0
 
     group = lax.axis_index("gz")
 
@@ -504,42 +530,45 @@
         for argument in (iterate, source, region, fixed_mask)
     ]
     edge = (2, ZC, 8, 128)
-    flat = jax.ShapeDtypeStruct((1, YC, 128), jnp.int32)
-    zmsg = call(
-        behind_kernel, struct(5, YC, 128),
-        scratch=[pltpu.SemaphoreType.DMA((2,))], in_specs=[far] * 2,
-    )(*arguments[:2])
-    zgot = lax.ppermute(zmsg, "gz", cyclic(GZ, 1))
-    up, down, it, src, reg, msk = call(
+    zmsg, up, down = call(
         edge_kernel,
-        (
-            struct(152, 128), struct(168, 128),
-            struct(*cells), struct(ZC - 2, YC, 128), flat, flat,
-        ),
+        (struct(5, YC, 128), struct(160, 128), struct(176, 128)),
         scratch=[
             pltpu.VMEM(edge, F32), pltpu.VMEM(edge, F32),
             pltpu.VMEM((2, 1, 8, 128), jnp.int32), pltpu.VMEM((2, 1, 8, 128), jnp.int32),
-            pltpu.SemaphoreType.DMA((12,)),
+            pltpu.SemaphoreType.DMA((10,)),
         ],
         in_specs=[far] * 4,
     )(*arguments)
     lo = lax.ppermute(up, "gy", cyclic(GY, 1))
     hi = lax.ppermute(down, "gy", cyclic(GY, -1))
-    corner_up, corner_down = call(corner_kernel, (struct(24, 128), struct(32, 128)))(zgot)
-    corner_lo = lax.ppermute(corner_up, "gy", cyclic(GY, 1))
-    corner_hi = lax.ppermute(corner_down, "gy", cyclic(GY, -1))
-
+    zgot = lax.ppermute(zmsg, "gz", cyclic(GZ, 1))
     kept = (
         struct(GZ, 72, 128), struct(18, WIDE, 128), struct(ZC - 2, YC, 128),
         struct(3 * FR + 2 * YC, 128), struct(24 * FR, 128), struct(19, WIDE, 128),
-        struct(18, FR, 128), struct(ZC, FR, 128),
+        struct(18, FR, 128), struct(ZC, FR, 128), struct(2, FR, 128),
     )
-    *early, frames, rest = call(
-        residual_kernel, kept + (struct(2, FR, 128), struct(FR, 128))
-    )(it, src, reg, msk, zgot, lo, hi)
-    chunks, nu, resid, message, *_ = call(
-        corner_residual_kernel, kept, input_output_aliases={4 + k: k for k in range(len(kept))}
-    )(corner_lo, corner_hi, frames, rest, *early)
+    *state, frames = call(
+        inner_kernel,
+        kept,
+        scratch=[
+            pltpu.VMEM((1, YC, 128), jnp.int32), pltpu.VMEM((1, YC, 128), jnp.int32),
+            pltpu.SemaphoreType.DMA((4,)),
+        ],
+        in_specs=[far] * 4,
+        cost_estimate=COST,
+    )(*arguments)
+    lo, frames = lax.optimization_barrier((lo, frames))
+    corners = call(corner_kernel, struct(56, 128))(lo, hi)
+    corners = lax.ppermute(corners, "gz", cyclic(GZ, 1))
+    state = call(
+        halo_kernel, kept, cost_estimate=COST,
+        input_output_aliases={3 + k: k for k in range(len(kept))},
+    )(zgot, lo, hi, *state, frames)
+    chunks, nu, resid, message, *_, frames = call(
+        corner_residual_kernel, kept,
+        input_output_aliases={1 + k: k for k in range(len(kept))},
+    )(corners, *state)
     message = lax.ppermute(message, "gz", cyclic(GZ, -1))
     windows = lax.all_to_all(chunks, "gz", 0, 0, tiled=True)
     sent = call(
@@ -554,7 +583,7 @@
         image_kernel,
         (struct(*cells), struct(*cells), struct(GZ * GY, 1, 128)),
         scratch=[pltpu.VMEM((18 * FR, 128), F32)],
-    )(returned, nu, resid, message, msk)
+    )(returned, nu, resid, message, frames)
     sums = lax.all_to_all(sums, ("gz", "gy"), 0, 0, tiled=True)
     correction, lin_residual, rms = call(
         output_kernel, (struct(*cells), struct(*cells), struct(1, 128))

time: 83.8 us -> 83 us (level)
  starting transfers between devices: 13.6 us -> 12.3 us
    ppermute x2 -> x1, starting transfers between devices: 2.74 us -> 1.55 us  [shards(): corners = lax.ppermute(corners, 'gz', cyclic(GZ, 1))]
    pallas_call x5, Pallas kernels: 5.38 us -> 6.48 us  [the longest x1 2.5 us: shards(): call(inner_kernel, kept, scratch=[pltpu.VMEM((1, YC, 128), jnp.int32), pl...]
  transfers between devices with their start and end apart: 7 -> 6, of which waited for: 3 -> 3; matrix products, arithmetic and copies ran while one was open for 0% -> 0% of each run, Pallas kernels for 5% -> 6%
where the time goes in v4:
time: 83 us; the launch traced here: 82.7 us
  blocking collectives  40.1 us (48%)
  waiting for transfers between devices  15.2 us (18%)
  Pallas kernels  14.2 us (17%)
  starting transfers between devices  12.3 us (15%)
    all_to_all x1, blocking collectives, shards(): windows = lax.all_to_all(chunks, 'gz', 0, 0, tiled=True)  26 us
    all_to_all x1, blocking collectives, shards(): sums = lax.all_to_all(sums, ('gz', 'gy'), 0, 0, tiled=True)  14.1 us
    ppermute x1, waiting for transfers between devices, shards(): message = lax.ppermute(message, 'gz', cyclic(GZ, -1))  11.4 us
    pallas_call x1, Pallas kernels, shards(): call(modes_kernel, struct(GZ, 40, 128), scratch=[pltpu.VMEM((NZ, LANES),...  4.64 us
    all_to_all x1, starting transfers between devices, shards(): returned = lax.all_to_all(sent, 'gz', 0, 0, tiled=True)  3.95 us
    ppermute x1, starting transfers between devices, shards(): hi = lax.ppermute(down, 'gy', cyclic(GY, -1))  3.76 us
    ppermute x1, starting transfers between devices, shards(): zgot = lax.ppermute(zmsg, 'gz', cyclic(GZ, 1))  2.67 us
    ppermute x1, waiting for transfers between devices, shards(): lo = lax.ppermute(up, 'gy', cyclic(GY, 1))  2.61 us
  transfers between devices with their start and end apart: 6, of which 3 were waited for; matrix products, arithmetic and copies ran while one was open for 0% of the time, Pallas kernels for 6%

profile of v4, /device:TPU:1, one launch (start us, length us, event | category | flops | bytes accessed | tf_op | source)
XLA Modules:
  0.0 82.7 jit_solution(5710292774245592747)
XLA Ops:
  0.6 1.2 %shard_map.121 = (f32[5,64,128]{2,1,0:T(8,128)S(1)}, f32[160,128]{1,0:T(8,128)S(1)}, f32[176,128]{1,0:T(8,128)S(1)}) custom-call(f32[16,64,128]{2,1,0:T(8,128)} %it.3, f32[16,64,128]{2,1,0:T(8,128)} %src.3, s32[16,64,128]{2,1,0:T(8,128)} %reg.3, s32[16,64,128]{2,1,0:T(8,128)} %msk.3), custom_call_target="tpu_custom_call" | custom-call | tf_op jit(solution)/shard_map/pallas_call | solution.py:533
  1.8 2.7 %collective-permute-start.3 = (f32[5,64,128]{2,1,0:T(8,128)S(1)}, f32[5,64,128]{2,1,0:T(8,128)S(1)}, u32[]{:S(2)}, u32[]{:S(2)}) collective-permute-start(f32[5,64,128]{2,1,0:T(8,128)S(1)} %get-tuple-element.41), channel_id=1, source_target_pairs={{0,4},{4,8},{8,12},{12,16},{16,20},{20,24},{24,28},{28,32},{32,36}... | collective-permute-start | bytes 491528 | tf_op jit(solution)/shard_map/ppermute | solution.py:545
  4.5 3.8 %collective-permute-start.1 = (f32[176,128]{1,0:T(8,128)S(1)}, f32[176,128]{1,0:T(8,128)S(1)}, u32[]{:S(2)}, u32[]{:S(2)}) collective-permute-start(f32[176,128]{1,0:T(8,128)S(1)} %get-tuple-element.40), channel_id=1, source_target_pairs={{0,3},{1,0},{2,1},{3,2},{4,7},{5,4},{6,5},{7,6},{8,11},{9,8},{10,9... | collective-permute-start | bytes 270344 | tf_op jit(solution)/shard_map/ppermute | solution.py:544
  8.2 0.0 collective-permute-start
  8.2 2.5 %shard_map.122 = (f32[32,72,128]{2,1,0:T(8,128)S(1)}, f32[18,96,128]{2,1,0:T(8,128)S(1)}, f32[14,64,128]{2,1,0:T(8,128)S(1)}, f32[368,128]{1,0:T(8,128)S(1)}, f3...) custom-call(f32[16,64,128]{2,1,0:T(8,128)} %it.3, ...), custom_call_target="tpu_custom_call" | custom-call | flops 4000000 | bytes 8000000 | tf_op jit(solution)/shard_map/pallas_call | solution.py:551
  10.8 2.6 %collective-permute-done.lo = f32[160,128]{1,0:T(8,128)S(1)} collective-permute-done((f32[160,128]{1,0:T(8,128)S(1)}, f32[160,128]{1,0:T(8,128)S(1)}, u32[]{:S(2)}, u32[]{:S(2)}) %collective-permute-start) | collective-permute-done | bytes 81952 | tf_op jit(solution)/shard_map/ppermute | solution.py:543
  13.4 1.6 %collective-permute-start.2 = (f32[56,128]{1,0:T(8,128)S(1)}, f32[56,128]{1,0:T(8,128)S(1)}, u32[]{:S(2)}, u32[]{:S(2)}) collective-permute-start(f32[56,128]{1,0:T(8,128)S(1)} %shard_map.123), channel_id=1, source_target_pairs={{0,4},{4,8},{8,12},{12,16},{16,20},{20,24},{24,28},{28,32},{32,36}... | collective-permute-start | bytes 86024 | tf_op jit(solution)/shard_map/ppermute | solution.py:563
  14.9 2.3 %shard_map.124 = (f32[32,72,128]{2,1,0:T(8,128)S(1)}, f32[18,96,128]{2,1,0:T(8,128)S(1)}, f32[14,64,128]{2,1,0:T(8,128)S(1)}, f32[368,128]{1,0:T(8,128)S(1)}, f3...) custom-call(f32[5,64,128]{2,1,0:T(8,128)S(1)} %collective-permute-do, ...), custom_call_target="tpu_custom_call", output_to_operand_aliasing={{0}: (3, {}), {1}: (4, {}), {2}: (5, {}), {3}: (6, {}), {4}... | custom-call | flops 4000000 | bytes 8000000 | tf_op jit(solution)/shard_map/pallas_call | solution.py:564
  17.2 0.0 copy-start.5
  17.2 0.5 shard_map.125
  17.8 0.0 copy-start
  17.8 0.0 copy-start.1
  17.8 0.0 copy-start.2
  17.8 0.0 copy-start.3
  17.8 0.0 copy-start.4
  17.8 26.0 %all_to_all.15.got = f32[32,72,128]{2,1,0:T(8,128)S(1)} all-to-all(f32[32,72,128]{2,1,0:T(8,128)S(1)} %get-tuple-element.60), channel_id=1, replica_groups=mesh['gz'=32,'gy'=4] {'gz'}, dimensions={0} | all-to-all | bytes 2359296 | tf_op jit(solution)/shard_map/all_to_all | solution.py:573
  43.9 4.6 %shard_map.126 = f32[32,40,128]{2,1,0:T(8,128)} custom-call(f32[32,72,128]{2,1,0:T(8,128)S(1)} %all_to_all.15.got, bf16[512,512]{1,0:T(8,128)(2,1)S(1)} %copy-done.3, bf16[512,512]{1,0:T(8,128)(2,1)S(1)} %copy-done.2, bf16[512,512]{1,0:T(8,128)(2,1)S(1)} %copy-done.1, bf16[512,512]{1,0:T(8,128)(2,1)S(1)} %copy-done, f32[512,128]{1,0:T(8,128)S(1)} %copy-done.4, ...), custom_call_target="tpu_custom_call" | custom-call | tf_op jit(solution)/shard_map/pallas_call | solution.py:574
  48.5 3.9 %all-to-all-start.1 = ((f32[32,40,128]{2,1,0:T(8,128)}), f32[32,40,128]{2,1,0:T(8,128)S(1)}, u32[]{:S(2)}, u32[]{:S(2)}) async-start(f32[32,40,128]{2,1,0:T(8,128)} %shard_map.126), calls=%async_computation.1 | async-start | bytes 1310720 | tf_op jit(solution)/shard_map/all_to_all | solution.py:581
  52.5 0.4 collective-permute-start.4
  52.9 11.4 %collective-permute-done.4.message = f32[368,128]{1,0:T(8,128)S(1)} collective-permute-done((f32[368,128]{1,0:T(8,128)S(1)}, f32[368,128]{1,0:T(8,128)S(1)}, u32[]{:S(2)}, u32[]{:S(2)}) %collective-permute-start.4) | collective-permute-done | bytes 188448 | tf_op jit(solution)/shard_map/ppermute | solution.py:572
  64.3 1.2 %all-to-all-done.1.got = f32[32,40,128]{2,1,0:T(8,128)S(1)} async-done(((f32[32,40,128]{2,1,0:T(8,128)}), f32[32,40,128]{2,1,0:T(8,128)S(1)}, u32[]{:S(2)}, u32[]{:S(2)}) %all-to-all-start.1) | async-done | bytes 655392 | tf_op jit(solution)/shard_map/all_to_all | solution.py:581
  65.5 1.6 %shard_map.127 = (f32[16,64,128]{2,1,0:T(8,128)S(1)}, f32[16,64,128]{2,1,0:T(8,128)S(1)}, f32[128,1,128]{2,1,0:T(1,128)S(1)}) custom-call(f32[32,40,128]{2,1,0:T(8,128)S(1)} %all-to-all-done.1.got, f32[18,96,128]{2,1,0:T(8,128)S(1)} %get-tuple-element.61.nu, f32[14,64,128]{2,1,0:T(8,128)S(1)} %get-tuple-element.62.resid, ...), custom_call_target="tpu_custom_call" | custom-call | tf_op jit(solution)/shard_map/pallas_call | solution.py:582
  67.1 14.1 %all_to_all.16.sums = f32[128,1,128]{2,1,0:T(1,128)S(1)} all-to-all(f32[128,1,128]{2,1,0:T(1,128)S(1)} %get-tuple-element.65), channel_id=1, replica_groups=mesh['gz'=32,'gy'=4] {'gz','gy'}, dimensions={0} | all-to-all | bytes 131072 | tf_op jit(solution)/shard_map/all_to_all | solution.py:587
  81.2 1.5 %shard_map.128 = (f32[16,64,128]{2,1,0:T(8,128)}, f32[16,64,128]{2,1,0:T(8,128)}, f32[1,128]{1,0:T(1,128)}) custom-call(f32[128,1,128]{2,1,0:T(1,128)S(1)} %all_to_all.16.sums, f32[16,64,128]{2,1,0:T(8,128)S(1)} %get-tuple-element.66.zdir, f32[16,64,128]{2,1,0:T(8,128)S(1)} %get-tuple-element.67.image, f32[14,64,128]{2,1,0:T(8,128)S(1)} %get-tuple-element.62.resid, ...), custom_call_target="tpu_custom_call" | custom-call | tf_op jit(solution)/shard_map/pallas_call | solution.py:588
  (10 shorter events, 0.0 us)
Async XLA Ops:
  1.8 13.1 %collective-permute-start.3 = (f32[5,64,128]{2,1,0:T(8,128)S(1)}, f32[5,64,128]{2,1,0:T(8,128)S(1)}, u32[]{:S(2)}, u32[]{:S(2)}) collective-permute-start(f32[5,64,128]{2,1,0:T(8,128)S(1)} %get-tuple-element.41), channel_id=1, source_target_pairs={{0,4},{4,8},{8,12},{12,16},{16,20},{20,24},{24,28},{28,32},{32,36}... | collective-permute-start | bytes 491528 | tf_op jit(solution)/shard_map/ppermute | solution.py:545
  4.5 8.9 %collective-permute-start.1 = (f32[176,128]{1,0:T(8,128)S(1)}, f32[176,128]{1,0:T(8,128)S(1)}, u32[]{:S(2)}, u32[]{:S(2)}) collective-permute-start(f32[176,128]{1,0:T(8,128)S(1)} %get-tuple-element.40), channel_id=1, source_target_pairs={{0,3},{1,0},{2,1},{3,2},{4,7},{5,4},{6,5},{7,6},{8,11},{9,8},{10,9... | collective-permute-start | bytes 270344 | tf_op jit(solution)/shard_map/ppermute | solution.py:544
  8.2 5.1 %collective-permute-start = (f32[160,128]{1,0:T(8,128)S(1)}, f32[160,128]{1,0:T(8,128)S(1)}, u32[]{:S(2)}, u32[]{:S(2)}) collective-permute-start(f32[160,128]{1,0:T(8,128)S(1)} %get-tuple-element.37), channel_id=1, source_target_pairs={{0,1},{1,2},{2,3},{3,0},{4,5},{5,6},{6,7},{7,4},{8,9},{9,10},{10,1... | collective-permute-start | bytes 245768 | tf_op jit(solution)/shard_map/ppermute | solution.py:543
  13.4 3.8 %collective-permute-start.2 = (f32[56,128]{1,0:T(8,128)S(1)}, f32[56,128]{1,0:T(8,128)S(1)}, u32[]{:S(2)}, u32[]{:S(2)}) collective-permute-start(f32[56,128]{1,0:T(8,128)S(1)} %shard_map.123), channel_id=1, source_target_pairs={{0,4},{4,8},{8,12},{12,16},{16,20},{20,24},{24,28},{28,32},{32,36}... | collective-permute-start | bytes 86024 | tf_op jit(solution)/shard_map/ppermute | solution.py:563
  17.2 26.6 %copy-start.5 = (s32[8,512]{1,0:T(8,128)S(1)}, s32[8,512]{1,0:T(8,128)}, u32[]{:S(2)}) copy-start(s32[8,512]{1,0:T(8,128)} %constant.17.clone.spots) | copy-start | bytes 49156
  17.8 26.1 %copy-start = (bf16[512,512]{1,0:T(8,128)(2,1)S(1)}, bf16[512,512]{1,0:T(8,128)(2,1)}, u32[]{:S(2)}) copy-start(bf16[512,512]{1,0:T(8,128)(2,1)} %constant.15.clone.low) | copy-start | bytes 1572868
  17.8 26.1 %copy-start.1 = (bf16[512,512]{1,0:T(8,128)(2,1)S(1)}, bf16[512,512]{1,0:T(8,128)(2,1)}, u32[]{:S(2)}) copy-start(bf16[512,512]{1,0:T(8,128)(2,1)} %constant.14.clone.high) | copy-start | bytes 1572868
  17.8 26.1 %copy-start.2 = (bf16[512,512]{1,0:T(8,128)(2,1)S(1)}, bf16[512,512]{1,0:T(8,128)(2,1)}, u32[]{:S(2)}) copy-start(bf16[512,512]{1,0:T(8,128)(2,1)} %constant.13.clone.ahead_low) | copy-start | bytes 1572868
  17.8 26.1 %copy-start.3 = (bf16[512,512]{1,0:T(8,128)(2,1)S(1)}, bf16[512,512]{1,0:T(8,128)(2,1)}, u32[]{:S(2)}) copy-start(bf16[512,512]{1,0:T(8,128)(2,1)} %constant.12.clone.ahead_high) | copy-start | bytes 1572868
  17.8 26.1 %copy-start.4 = (f32[512,128]{1,0:T(8,128)S(1)}, f32[512,128]{1,0:T(8,128)}, u32[]{:S(2)}) copy-start(f32[512,128]{1,0:T(8,128)} %constant.16.clone.lam) | copy-start | bytes 786436
  48.5 17.0 %all-to-all-start.1 = ((f32[32,40,128]{2,1,0:T(8,128)}), f32[32,40,128]{2,1,0:T(8,128)S(1)}, u32[]{:S(2)}, u32[]{:S(2)}) async-start(f32[32,40,128]{2,1,0:T(8,128)} %shard_map.126), calls=%async_computation.1 | async-start | bytes 1310720 | tf_op jit(solution)/shard_map/all_to_all | solution.py:581
  52.5 11.8 %collective-permute-start.4 = (f32[368,128]{1,0:T(8,128)S(1)}, f32[368,128]{1,0:T(8,128)S(1)}, u32[]{:S(2)}, u32[]{:S(2)}) collective-permute-start(f32[368,128]{1,0:T(8,128)S(1)} %get-tuple-element.63), channel_id=1, source_target_pairs={{0,124},{4,0},{8,4},{12,8},{16,12},{20,16},{24,20},{28,24},{32,28}... | collective-permute-start | bytes 565256 | tf_op jit(solution)/shard_map/ppermute | solution.py:572

commit v5 on v4

--- a/solution.py
+++ b/solution.py
@@ -53,8 +53,8 @@
     low = (table - high.astype(np.float32)).astype(ml_dtypes.bfloat16)
     lam = 2.0 - 2.0 * np.cos(np.pi * (index + 1.0) / (NZ + 1))
     lam = np.broadcast_to(lam.astype(np.float32)[:, None], (NZ, 128))
-    ahead_high, ahead_low = np.roll(high, 2, 1), np.roll(low, 2, 1)
-    return ahead_high, ahead_low, high, low, np.ascontiguousarray(lam), window_places()
+    there, back = [np.roll(t, 2, 1) for t in (high, low)], [np.roll(t, 2, 0) for t in (high, low)]
+    return *there, *back, np.ascontiguousarray(lam), window_places()
 
 
 def lane_iota(shape):
@@ -134,7 +134,7 @@
     nu[p, pl.ds(8 + span[0], span[1])] = jnp.where(iron, 0.05 + bsq / (bsq + 9.0), 1.0)
 
 
-def set_residuals(span, steps, field, right, nu, drive, flat, rows, resid, message, first, last):
+def set_residuals(span, steps, field, right, nu, drive, flat, rows, resid, first, last):
     start = lax.axis_index("gz") == 0
     begin, count = span
     copper, held = flat[0, pl.ds(*span)] == 1.0, flat[1, pl.ds(*span)] == 1.0
@@ -163,10 +163,7 @@
         flow = flow + (fx - jnp.where(first, -0.5 * (n + 1.0) * u, roll(fx, 1, 1)))
         value = -jnp.where(held, u, flow - jnp.where(copper, drive[t, pl.ds(*span)], 0.0))
         rows[pl.ds(t * FR + begin, count), :] = value
-        if t < 2:
-            message[pl.ds(3 * FR + YC * t + kept.start, kept.size), :] = value[own]
-        else:
-            resid[t - 2, kept] = value[own]
+        resid[t, kept] = value[own]
 
 
 def set_means(span, rows, first, last):
@@ -179,19 +176,16 @@
     )
 
 
-def work(spans, planes, steps, field, right, nu, drive, flat, rows, resid, message):
+def work(spans, planes, steps, field, right, nu, drive, flat, rows, resid):
     for span in spans:
         first, last = edge_lanes(span[1])
         iron = flat[0, pl.ds(*span)] == 2.0
         for p in planes:
             set_nu(p, span, field, right, nu, iron, last)
-        for p in planes:
-            if 1 <= p < 4:
-                message[pl.ds(FR * (p - 1) + span[0], span[1]), :] = level(nu, p, span)
     for span in spans:
         first, last = edge_lanes(span[1])
         set_residuals(
-            span, steps, field, right, nu, drive, flat, rows, resid, message, first, last
+            span, steps, field, right, nu, drive, flat, rows, resid, first, last
         )
 
 
@@ -237,7 +231,7 @@
 BEHIND, HERE = range(0, 3), range(3, 18)
 
 
-def inner_kernel(it, src, reg, msk, chunks, nu, resid, message, rows, field, right, drive, flat,
+def inner_kernel(it, src, reg, msk, chunks, nu, resid, rows, field, right, drive, flat,
                  reg_in, msk_in, sems):
     own = slice(8, 8 + YC)
     copies = start_all(
@@ -252,12 +246,12 @@
         copy.wait()
     flat[0, own] = reg_in[0].astype(F32)
     flat[1, own] = msk_in[0].astype(F32)
-    work(INNER, HERE, range(3, ZC), field, right, nu, drive, flat, rows, resid, message)
+    work(INNER, HERE, range(3, ZC), field, right, nu, drive, flat, rows, resid)
     pack(rows, chunks, (1, 2), (1,))
 
 
 def halo_kernel(zgot, lo, hi, *refs):
-    chunks, nu, resid, message, rows, field, right, drive, flat = refs[9:]
+    chunks, nu, resid, rows, field, right, drive, flat = refs[8:]
     column = lax.axis_index("gy")
 
     def below(value):
@@ -280,15 +274,15 @@
     flat[0, 72:77] = above(hi[160:165])
     flat[1, 4:8] = lo[149:153]
     flat[1, 72:76] = hi[165:169]
-    work(INNER, BEHIND, range(0, 3), field, right, nu, drive, flat, rows, resid, message)
-    work(OUTER, HERE, range(3, ZC), field, right, nu, drive, flat, rows, resid, message)
+    work(INNER, BEHIND, range(0, 3), field, right, nu, drive, flat, rows, resid)
+    work(OUTER, HERE, range(3, ZC), field, right, nu, drive, flat, rows, resid)
     sum_planes(INNER, nu, rows)
     pack(rows, chunks, (1, 2), (0, 2))
     pack(rows, chunks, (0, 3), (1,))
 
 
 def corner_residual_kernel(corners, *refs):
-    chunks, nu, resid, message, rows, field, right, drive, flat = refs[9:]
+    chunks, nu, resid, rows, field, right, drive, flat = refs[8:]
     column = lax.axis_index("gy")
     for p in range(3):
         field[p, 11:16] = jnp.where(column == 0, 0.0, corners[5 * p:5 * p + 5])
@@ -296,7 +290,7 @@
     for t in range(2):
         drive[t, 4:8] = corners[33 + 4 * t:37 + 4 * t]
         drive[t, 72:76] = corners[41 + 4 * t:45 + 4 * t]
-    work(OUTER, BEHIND, range(0, 3), field, right, nu, drive, flat, rows, resid, message)
+    work(OUTER, BEHIND, range(0, 3), field, right, nu, drive, flat, rows, resid)
     sum_planes(OUTER, nu, rows)
     pack(rows, chunks, (0, 3), (0, 2))
 
@@ -374,8 +368,8 @@
         term = product(high[:, part], low[:, part], w_high, w_low)
         total = term if total is None else total + term
     back[8:8 + NZ, :] = total
-    back[0:8, :] = jnp.zeros((8, 384), F32)
-    back[8 + NZ:, :] = jnp.zeros((8, 384), F32)
+    back[0:8, :] = total[NZ - 8:]
+    back[8 + NZ:, :] = total[:8]
 
     sub = lax.broadcasted_iota(jnp.int32, (8, 128), 0)
     pattern = (((lane_iota((8, 128)) >> 4) + sub - xp) & 7) == 0
@@ -389,17 +383,10 @@
             piece = back[at + 8 * block:at + 8 * block + 8, 256:384]
             piece = jnp.sum(jnp.where(pattern, piece, 0.0), axis=0, keepdims=True)
             out[peer, 36 + block:37 + block, :] = piece
-        out[peer, 38:40, :] = jnp.zeros((2, 128), F32)
-
-
-def resid_plane(resid, message, z):
-    if z < ZC - 2:
-        return resid[z]
-    at = 3 * FR + YC * (z - ZC + 2)
-    return message[at:at + YC, :]
-
-
-def image_kernel(got, nu, resid, message, flat, zdir, image, sums, frame):
+            out[peer, 38 + block:39 + block, :] = back[at + ZC + 1:at + ZC + 2, lanes]
+
+
+def image_kernel(got, nu, resid, flat, zdir, image, message, sums, frame):
     lane = lane_iota((8, 128))
     places = [(lane >> 4) == k for k in range(8)]
 
@@ -423,8 +410,9 @@
             y = 8 + 16 * yp + jj
             for k in range(2):
                 frame[y + 8 * k:y + 8 * k + 1, :] = value[k:k + 1]
-                at = 17 * FR + y + 8 * k
-                frame[at:at + 1, :] = value[2 + k:3 + k]
+                for p, row in ((17, 2), (18, 6)):
+                    at = p * FR + y + 8 * k
+                    frame[at:at + 1, :] = value[row + k:row + k + 1]
 
     sub = lax.broadcasted_iota(jnp.int32, (8, 128), 0)
     turn = ((lane >> 4) + sub) & 7
@@ -441,48 +429,48 @@
     first, last = lane == 0, lane == 127
     held = flat[1, 8:8 + YC] == 1.0
 
-    group = lax.axis_index("gz")
-
-    def nu_rows(z, shift):
-        at = 8 + shift
-        if z >= ZC - 2:
-            value = message[FR * (z - ZC + 2) + at:FR * (z - ZC + 2) + at + YC, :]
-        else:
-            value = nu[z + 3, at + 8:at + 8 + YC]
-        if z == -1:
-            value = jnp.where(group == 0, 1.0, value)
-        if z == ZC:
-            value = jnp.where(group == GZ - 1, 1.0, value)
-        return value
-
-    def dir_rows(z, shift):
-        at = (z + 1) * FR + 8 + shift
+    start = lax.axis_index("gz") == 0
+
+    def nu_rows(p, shift=0):
+        return nu[p, 16 + shift:16 + shift + YC]
+
+    def dir_rows(p, shift=0):
+        at = p * FR + 8 + shift
         return frame[at:at + YC, :]
 
-    d, n = dir_rows(0, 0), nu_rows(0, 0)
-    flux = 0.5 * (nu_rows(-1, 0) + n) * (dir_rows(-1, 0) - d)
+    d, n = dir_rows(1), nu_rows(1)
+    flux = 0.5 * (nu_rows(0) + n) * (dir_rows(0) - d)
     rr = ri = ii = jnp.zeros((8, 128), F32)
 
     def fold(value):
         return jnp.sum(value.reshape(YC // 8, 8, 128), axis=0)
 
-    for z in range(ZC):
-        dz, nz = dir_rows(z + 1, 0), nu_rows(z + 1, 0)
-        ahead = 0.5 * (n + nz) * (d - dz)
+    for t in range(ZC):
+        p = t + 1
+        dz, nz = dir_rows(p + 1), nu_rows(p + 1)
+        up, nup = dz, nz
+        if p == 2:
+            up, nup = jnp.where(start, 0.0, dz), jnp.where(start, 1.0, nz)
+        if p == 3:
+            flux = jnp.where(start, -0.5 * (1.0 + n) * d, flux)
+        ahead = 0.5 * (n + nup) * (d - up)
         flow = ahead - flux
-        flow = flow + 0.5 * (n + nu_rows(z, 1)) * (d - dir_rows(z, 1))
-        flow = flow + 0.5 * (n + nu_rows(z, -1)) * (d - dir_rows(z, -1))
+        flow = flow + 0.5 * (n + nu_rows(p, 1)) * (d - dir_rows(p, 1))
+        flow = flow + 0.5 * (n + nu_rows(p, -1)) * (d - dir_rows(p, -1))
         nx = jnp.where(last, 1.0, roll(n, -1, 1))
         dx = jnp.where(last, 0.0, roll(d, -1, 1))
         fx = 0.5 * (n + nx) * (d - dx)
         flow = flow + (fx - jnp.where(first, -0.5 * (n + 1.0) * d, roll(fx, 1, 1)))
         value = jnp.where(held, d, flow)
-        zdir[z] = d
-        image[z] = value
-        r = resid_plane(resid, message, z)
+        r = resid[t]
+        zdir[t] = d
+        image[t] = value
+        if t < 2:
+            message[t], message[2 + t] = value, r
         rr, ri, ii = rr + fold(r * r), ri + fold(r * value), ii + fold(value * value)
         d, n, flux = dz, nz, ahead
 
+    zdir[ZC], zdir[ZC + 1] = dir_rows(ZC + 1), dir_rows(ZC + 2)
     parts = (rr, ri, ii)
     line = lane_iota((1, 128))
     packed = jnp.zeros((1, 128), F32)
@@ -498,9 +486,9 @@
     h_one = total[0:1, 1:2] / beta_sq
     denom = total[0:1, 2:3] / beta_sq - h_one * h_one * (1e-06 / beta_sq) + 1e-06
     gamma = h_one / denom
-    correction[...] = zdir[...] * gamma[None]
-    for z in range(ZC):
-        lin_residual[z] = resid_plane(resid, message, z) - gamma * image[z]
+    correction[...] = zdir[2:] * gamma[None]
+    lin_residual[0:ZC - 2] = resid[2:] - gamma[None] * image[2:]
+    lin_residual[ZC - 2:ZC] = message[2:4] - gamma[None] * message[0:2]
     rms[...] = jnp.broadcast_to(beta * (1.0 / np.sqrt(float(NZ * NY * NX))), rms.shape)
 
 
@@ -544,9 +532,8 @@
     hi = lax.ppermute(down, "gy", cyclic(GY, -1))
     zgot = lax.ppermute(zmsg, "gz", cyclic(GZ, 1))
     kept = (
-        struct(GZ, 72, 128), struct(18, WIDE, 128), struct(ZC - 2, YC, 128),
-        struct(3 * FR + 2 * YC, 128), struct(24 * FR, 128), struct(19, WIDE, 128),
-        struct(18, FR, 128), struct(ZC, FR, 128), struct(2, FR, 128),
+        struct(GZ, 72, 128), struct(18, WIDE, 128), struct(*cells), struct(24 * FR, 128),
+        struct(19, WIDE, 128), struct(18, FR, 128), struct(ZC, FR, 128), struct(2, FR, 128),
     )
     *state, frames = call(
         inner_kernel,
@@ -565,11 +552,10 @@
         halo_kernel, kept, cost_estimate=COST,
         input_output_aliases={3 + k: k for k in range(len(kept))},
     )(zgot, lo, hi, *state, frames)
-    chunks, nu, resid, message, *_, frames = call(
+    chunks, nu, resid, *_, frames = call(
         corner_residual_kernel, kept,
         input_output_aliases={1 + k: k for k in range(len(kept))},
     )(corners, *state)
-    message = lax.ppermute(message, "gz", cyclic(GZ, -1))
     windows = lax.all_to_all(chunks, "gz", 0, 0, tiled=True)
     sent = call(
         modes_kernel,
@@ -579,11 +565,15 @@
         ],
     )(windows, *[jnp.asarray(table) for table in tables()])
     returned = lax.all_to_all(sent, "gz", 0, 0, tiled=True)
-    zdir, image, sums = call(
+    zdir, image, message, sums = call(
         image_kernel,
-        (struct(*cells), struct(*cells), struct(GZ * GY, 1, 128)),
-        scratch=[pltpu.VMEM((18 * FR, 128), F32)],
-    )(returned, nu, resid, message, frames)
+        (
+            struct(ZC + 2, YC, 128), struct(*cells), struct(4, YC, 128),
+            struct(GZ * GY, 1, 128),
+        ),
+        scratch=[pltpu.VMEM((19 * FR, 128), F32)],
+    )(returned, nu, resid, frames)
+    message = lax.ppermute(message, "gz", cyclic(GZ, -1))
     sums = lax.all_to_all(sums, ("gz", "gy"), 0, 0, tiled=True)
     correction, lin_residual, rms = call(
         output_kernel, (struct(*cells), struct(*cells), struct(1, 128))

time: 83 us -> 82.6 us (level)
  blocking collectives: 40.1 us -> 56.9 us
  waiting for transfers between devices: 15.2 us -> 2.59 us
  starting transfers between devices: 12.3 us -> 8.6 us
    all_to_all x0 -> x1, blocking collectives: none -> 16.5 us  [shards(): returned = lax.all_to_all(sent, 'gz', 0, 0, tiled=True)]
    ppermute x1, waiting for transfers between devices: 11.4 us -> 0.01 us  [shards(): message = lax.ppermute(message, 'gz', cyclic(GZ, -1))]
    all_to_all x1 -> x0, starting transfers between devices: 3.95 us -> none  [shards(): returned = lax.all_to_all(sent, 'gz', 0, 0, tiled=True)]
    all_to_all x1 -> x0, waiting for transfers between devices: 1.25 us -> none  [shards(): returned = lax.all_to_all(sent, 'gz', 0, 0, tiled=True)]
    pallas_call x1, Pallas kernels: 4.64 us -> 3.79 us  [shards(): call(modes_kernel, struct(GZ, 40, 128), scratch=[pltpu.VMEM((NZ, LANES),...]
  transfers between devices with their start and end apart: 6 -> 5, of which waited for: 3 -> 1; matrix products, arithmetic and copies ran while one was open for 0% -> 0% of each run, Pallas kernels for 6% -> 6%
where the time goes in v5:
time: 82.6 us; the launch traced here: 82.3 us
  blocking collectives  56.9 us (69%)
  Pallas kernels  13.4 us (16%)
  starting transfers between devices  8.6 us (10%)
  waiting for transfers between devices  2.59 us (3%)
    all_to_all x1, blocking collectives, shards(): windows = lax.all_to_all(chunks, 'gz', 0, 0, tiled=True)  26 us
    all_to_all x1, blocking collectives, shards(): returned = lax.all_to_all(sent, 'gz', 0, 0, tiled=True)  16.5 us
    all_to_all x1, blocking collectives, shards(): sums = lax.all_to_all(sums, ('gz', 'gy'), 0, 0, tiled=True)  14.3 us
    pallas_call x1, Pallas kernels, shards(): call(modes_kernel, struct(GZ, 40, 128), scratch=[pltpu.VMEM((NZ, LANES),...  3.79 us
    ppermute x1, starting transfers between devices, shards(): hi = lax.ppermute(down, 'gy', cyclic(GY, -1))  3.76 us
    ppermute x1, starting transfers between devices, shards(): zgot = lax.ppermute(zmsg, 'gz', cyclic(GZ, 1))  2.67 us
    ppermute x1, waiting for transfers between devices, shards(): lo = lax.ppermute(up, 'gy', cyclic(GY, 1))  2.58 us
    pallas_call x1, Pallas kernels, shards(): call(inner_kernel, kept, scratch=[pltpu.VMEM((1, YC, 128), jnp.int32), pl...  2.53 us
  transfers between devices with their start and end apart: 5, of which 1 were waited for; matrix products, arithmetic and copies ran while one was open for 0% of the time, Pallas kernels for 6%

profile of v5, /device:TPU:1, one launch (start us, length us, event | category | flops | bytes accessed | tf_op | source)
XLA Modules:
  0.0 82.3 jit_solution(3640204029312285904)
XLA Ops:
  0.6 1.2 %shard_map.121 = (f32[5,64,128]{2,1,0:T(8,128)S(1)}, f32[160,128]{1,0:T(8,128)S(1)}, f32[176,128]{1,0:T(8,128)S(1)}) custom-call(f32[16,64,128]{2,1,0:T(8,128)} %it.3, f32[16,64,128]{2,1,0:T(8,128)} %src.3, s32[16,64,128]{2,1,0:T(8,128)} %reg.3, s32[16,64,128]{2,1,0:T(8,128)} %msk.3), custom_call_target="tpu_custom_call" | custom-call | tf_op jit(solution)/shard_map/pallas_call | solution.py:521
  1.8 2.7 %collective-permute-start.3 = (f32[5,64,128]{2,1,0:T(8,128)S(1)}, f32[5,64,128]{2,1,0:T(8,128)S(1)}, u32[]{:S(2)}, u32[]{:S(2)}) collective-permute-start(f32[5,64,128]{2,1,0:T(8,128)S(1)} %get-tuple-element.39), channel_id=1, source_target_pairs={{0,4},{4,8},{8,12},{12,16},{16,20},{20,24},{24,28},{28,32},{32,36}... | collective-permute-start | bytes 491528 | tf_op jit(solution)/shard_map/ppermute | solution.py:533
  4.5 3.8 %collective-permute-start.1 = (f32[176,128]{1,0:T(8,128)S(1)}, f32[176,128]{1,0:T(8,128)S(1)}, u32[]{:S(2)}, u32[]{:S(2)}) collective-permute-start(f32[176,128]{1,0:T(8,128)S(1)} %get-tuple-element.38), channel_id=1, source_target_pairs={{0,3},{1,0},{2,1},{3,2},{4,7},{5,4},{6,5},{7,6},{8,11},{9,8},{10,9... | collective-permute-start | bytes 270344 | tf_op jit(solution)/shard_map/ppermute | solution.py:532
  8.2 0.0 collective-permute-start
  8.2 2.5 %shard_map.122 = (f32[32,72,128]{2,1,0:T(8,128)S(1)}, f32[18,96,128]{2,1,0:T(8,128)S(1)}, f32[16,64,128]{2,1,0:T(8,128)S(1)}, f32[1920,128]{1,0:T(8,128)S(1)}, f...) custom-call(f32[16,64,128]{2,1,0:T(8,128)} %it.3, ...), custom_call_target="tpu_custom_call" | custom-call | flops 4000000 | bytes 8000000 | tf_op jit(solution)/shard_map/pallas_call | solution.py:538
  10.8 2.6 %collective-permute-done.lo = f32[160,128]{1,0:T(8,128)S(1)} collective-permute-done((f32[160,128]{1,0:T(8,128)S(1)}, f32[160,128]{1,0:T(8,128)S(1)}, u32[]{:S(2)}, u32[]{:S(2)}) %collective-permute-start) | collective-permute-done | bytes 81952 | tf_op jit(solution)/shard_map/ppermute | solution.py:531
  13.4 0.0 collective-permute-done.1.hi
  13.4 1.6 %collective-permute-start.2 = (f32[56,128]{1,0:T(8,128)S(1)}, f32[56,128]{1,0:T(8,128)S(1)}, u32[]{:S(2)}, u32[]{:S(2)}) collective-permute-start(f32[56,128]{1,0:T(8,128)S(1)} %shard_map.123), channel_id=1, source_target_pairs={{0,4},{4,8},{8,12},{12,16},{16,20},{20,24},{24,28},{28,32},{32,36}... | collective-permute-start | bytes 86024 | tf_op jit(solution)/shard_map/ppermute | solution.py:550
  14.9 0.0 collective-permute-done.3.zgot
  14.9 2.3 %shard_map.124 = (f32[32,72,128]{2,1,0:T(8,128)S(1)}, f32[18,96,128]{2,1,0:T(8,128)S(1)}, f32[16,64,128]{2,1,0:T(8,128)S(1)}, f32[1920,128]{1,0:T(8,128)S(1)}, f...) custom-call(f32[5,64,128]{2,1,0:T(8,128)S(1)} %collective-permute-do, ...), custom_call_target="tpu_custom_call", output_to_operand_aliasing={{0}: (3, {}), {1}: (4, {}), {2}: (5, {}), {3}: (6, {}), {4}... | custom-call | flops 4000000 | bytes 8000000 | tf_op jit(solution)/shard_map/pallas_call | solution.py:551
  17.2 0.0 copy-start.5
  17.2 0.5 shard_map.125
  17.8 0.0 copy-start
  17.8 0.0 copy-start.1
  17.8 0.0 copy-start.2
  17.8 0.0 copy-start.3
  17.8 0.0 copy-start.4
  17.8 26.0 %all_to_all.15.got = f32[32,72,128]{2,1,0:T(8,128)S(1)} all-to-all(f32[32,72,128]{2,1,0:T(8,128)S(1)} %get-tuple-element.56), channel_id=1, replica_groups=mesh['gz'=32,'gy'=4] {'gz'}, dimensions={0} | all-to-all | bytes 2359296 | tf_op jit(solution)/shard_map/all_to_all | solution.py:559
  43.9 3.8 %shard_map.126 = f32[32,40,128]{2,1,0:T(8,128)S(1)} custom-call(f32[32,72,128]{2,1,0:T(8,128)S(1)} %all_to_all.15.got, bf16[512,512]{1,0:T(8,128)(2,1)S(1)} %copy-done.3, bf16[512,512]{1,0:T(8,128)(2,1)S(1)} %copy-done.2, bf16[512,512]{1,0:T(8,128)(2,1)S(1)} %copy-done.1, bf16[512,512]{1,0:T(8,128)(2,1)S(1)} %copy-done, f32[512,128]{1,0:T(8,128)S(1)} %copy-done.4, ...), custom_call_target="tpu_custom_call" | custom-call | tf_op jit(solution)/shard_map/pallas_call | solution.py:560
  47.7 16.5 %all_to_all.16.got = f32[32,40,128]{2,1,0:T(8,128)S(1)} all-to-all(f32[32,40,128]{2,1,0:T(8,128)S(1)} %shard_map.126), channel_id=1, replica_groups=mesh['gz'=32,'gy'=4] {'gz'}, dimensions={0} | all-to-all | bytes 1310720 | tf_op jit(solution)/shard_map/all_to_all | solution.py:567
  64.2 1.6 %shard_map.127 = (f32[18,64,128]{2,1,0:T(8,128)S(1)}, f32[16,64,128]{2,1,0:T(8,128)S(1)}, f32[4,64,128]{2,1,0:T(8,128)S(1)}, f32[128,1,128]{2,1,0:T(1,128)S(1)}) custom-call(f32[32,40,128]{2,1,0:T(8,128)S(1)} %all_to_all.16.got, f32[18,96,128]{2,1,0:T(8,128)S(1)} %get-tuple-element.57.nu, f32[16,64,128]{2,1,0:T(8,128)S(1)} %get-tuple-element.58.resid, ...), custom_call_target="tpu_custom_call" | custom-call | tf_op jit(solution)/shard_map/pallas_call | solution.py:568
  65.8 0.6 collective-permute-start.4
  66.4 14.3 %all_to_all.17.sums = f32[128,1,128]{2,1,0:T(1,128)S(1)} all-to-all(f32[128,1,128]{2,1,0:T(1,128)S(1)} %get-tuple-element.60), channel_id=1, replica_groups=mesh['gz'=32,'gy'=4] {'gz','gy'}, dimensions={0} | all-to-all | bytes 131072 | tf_op jit(solution)/shard_map/all_to_all | solution.py:577
  80.8 1.5 %shard_map.128 = (f32[16,64,128]{2,1,0:T(8,128)}, f32[16,64,128]{2,1,0:T(8,128)}, f32[1,128]{1,0:T(1,128)}) custom-call(f32[128,1,128]{2,1,0:T(1,128)S(1)} %all_to_all.17.sums, f32[18,64,128]{2,1,0:T(8,128)S(1)} %get-tuple-element.61.zdir, f32[16,64,128]{2,1,0:T(8,128)S(1)} %get-tuple-element.62.image, f32[16,64,128]{2,1,0:T(8,128)S(1)} %get-tuple-element.58.resid, ...), custom_call_target="tpu_custom_call" | custom-call | tf_op jit(solution)/shard_map/pallas_call | solution.py:578
  (9 shorter events, 0.0 us)
Async XLA Ops:
  1.8 13.1 %collective-permute-start.3 = (f32[5,64,128]{2,1,0:T(8,128)S(1)}, f32[5,64,128]{2,1,0:T(8,128)S(1)}, u32[]{:S(2)}, u32[]{:S(2)}) collective-permute-start(f32[5,64,128]{2,1,0:T(8,128)S(1)} %get-tuple-element.39), channel_id=1, source_target_pairs={{0,4},{4,8},{8,12},{12,16},{16,20},{20,24},{24,28},{28,32},{32,36}... | collective-permute-start | bytes 491528 | tf_op jit(solution)/shard_map/ppermute | solution.py:533
  4.5 8.9 %collective-permute-start.1 = (f32[176,128]{1,0:T(8,128)S(1)}, f32[176,128]{1,0:T(8,128)S(1)}, u32[]{:S(2)}, u32[]{:S(2)}) collective-permute-start(f32[176,128]{1,0:T(8,128)S(1)} %get-tuple-element.38), channel_id=1, source_target_pairs={{0,3},{1,0},{2,1},{3,2},{4,7},{5,4},{6,5},{7,6},{8,11},{9,8},{10,9... | collective-permute-start | bytes 270344 | tf_op jit(solution)/shard_map/ppermute | solution.py:532
  8.2 5.1 %collective-permute-start = (f32[160,128]{1,0:T(8,128)S(1)}, f32[160,128]{1,0:T(8,128)S(1)}, u32[]{:S(2)}, u32[]{:S(2)}) collective-permute-start(f32[160,128]{1,0:T(8,128)S(1)} %get-tuple-element.35), channel_id=1, source_target_pairs={{0,1},{1,2},{2,3},{3,0},{4,5},{5,6},{6,7},{7,4},{8,9},{9,10},{10,1... | collective-permute-start | bytes 245768 | tf_op jit(solution)/shard_map/ppermute | solution.py:531
  13.4 3.9 %collective-permute-start.2 = (f32[56,128]{1,0:T(8,128)S(1)}, f32[56,128]{1,0:T(8,128)S(1)}, u32[]{:S(2)}, u32[]{:S(2)}) collective-permute-start(f32[56,128]{1,0:T(8,128)S(1)} %shard_map.123), channel_id=1, source_target_pairs={{0,4},{4,8},{8,12},{12,16},{16,20},{20,24},{24,28},{28,32},{32,36}... | collective-permute-start | bytes 86024 | tf_op jit(solution)/shard_map/ppermute | solution.py:550
  17.2 26.6 %copy-start.5 = (s32[8,512]{1,0:T(8,128)S(1)}, s32[8,512]{1,0:T(8,128)}, u32[]{:S(2)}) copy-start(s32[8,512]{1,0:T(8,128)} %constant.17.clone.spots) | copy-start | bytes 49156
  17.8 26.1 %copy-start = (bf16[512,512]{1,0:T(8,128)(2,1)S(1)}, bf16[512,512]{1,0:T(8,128)(2,1)}, u32[]{:S(2)}) copy-start(bf16[512,512]{1,0:T(8,128)(2,1)} %constant.15.clone.low) | copy-start | bytes 1572868
  17.8 26.1 %copy-start.1 = (bf16[512,512]{1,0:T(8,128)(2,1)S(1)}, bf16[512,512]{1,0:T(8,128)(2,1)}, u32[]{:S(2)}) copy-start(bf16[512,512]{1,0:T(8,128)(2,1)} %constant.14.clone.high) | copy-start | bytes 1572868
  17.8 26.1 %copy-start.2 = (bf16[512,512]{1,0:T(8,128)(2,1)S(1)}, bf16[512,512]{1,0:T(8,128)(2,1)}, u32[]{:S(2)}) copy-start(bf16[512,512]{1,0:T(8,128)(2,1)} %constant.13.clone.ahead_low) | copy-start | bytes 1572868
  17.8 26.1 %copy-start.3 = (bf16[512,512]{1,0:T(8,128)(2,1)S(1)}, bf16[512,512]{1,0:T(8,128)(2,1)}, u32[]{:S(2)}) copy-start(bf16[512,512]{1,0:T(8,128)(2,1)} %constant.12.clone.ahead_high) | copy-start | bytes 1572868
  17.8 26.1 %copy-start.4 = (f32[512,128]{1,0:T(8,128)S(1)}, f32[512,128]{1,0:T(8,128)}, u32[]{:S(2)}) copy-start(f32[512,128]{1,0:T(8,128)} %constant.16.clone.lam) | copy-start | bytes 786436
  65.8 14.9 %collective-permute-start.4 = (f32[4,64,128]{2,1,0:T(8,128)S(1)}, f32[4,64,128]{2,1,0:T(8,128)S(1)}, u32[]{:S(2)}, u32[]{:S(2)}) collective-permute-start(f32[4,64,128]{2,1,0:T(8,128)S(1)} %get-tuple-element.63), channel_id=1, source_target_pairs={{0,124},{4,0},{8,4},{12,8},{16,12},{20,16},{24,20},{28,24},{32,28}... | collective-permute-start | bytes 393224 | tf_op jit(solution)/shard_map/ppermute | solution.py:576

commit v6 on v5

--- a/solution.py
+++ b/solution.py
@@ -72,8 +72,13 @@
     return copies
 
 
-def edge_kernel(it, src, reg, msk, zmsg, up, down, e_it, e_src, e_reg, e_msk, sems):
-    pairs = [(it.at[ZC - 3:ZC], zmsg.at[0:3]), (src.at[ZC - 2:ZC], zmsg.at[3:5])]
+def edge_kernel(it, src, reg, msk, z_one, z_two, up, down, e_it, e_src, e_reg, e_msk, sems):
+    half = YC // 2
+    pairs = [
+        (it.at[ZC - 3], z_one.at[0:YC]), (it.at[ZC - 2], z_one.at[YC:2 * YC]),
+        (it.at[ZC - 1, 0:half], z_one.at[2 * YC:]), (it.at[ZC - 1, half:], z_two.at[0:half]),
+        (src.at[ZC - 2], z_two.at[half:half + YC]), (src.at[ZC - 1], z_two.at[half + YC:]),
+    ]
     for side, row in enumerate((0, YC - 8)):
         rows = pl.ds(row, 8)
         pairs += [
@@ -83,7 +88,7 @@
             (msk.at[0:1, rows], e_msk.at[side]),
         ]
     copies = start_all(pairs, sems)
-    for copy in copies[2:]:
+    for copy in copies[6:]:
         copy.wait()
     for z in range(ZC):
         up[5 * z:5 * z + 5] = e_it[1, z, 3:8]
@@ -92,11 +97,11 @@
         down[96 + 4 * z:100 + 4 * z] = e_src[0, z, 0:4]
     up[144:149] = e_reg[1, 0, 3:8].astype(F32)
     up[149:153] = e_msk[1, 0, 4:8].astype(F32)
-    up[153:160] = jnp.zeros((7, 128), F32)
+    up[153:176] = jnp.zeros((23, 128), F32)
     down[160:165] = e_reg[0, 0, 0:5].astype(F32)
     down[165:169] = e_msk[0, 0, 0:4].astype(F32)
     down[169:176] = jnp.zeros((7, 128), F32)
-    for copy in copies[:2]:
+    for copy in copies[:6]:
         copy.wait()
 
 
@@ -250,7 +255,7 @@
     pack(rows, chunks, (1, 2), (1,))
 
 
-def halo_kernel(zgot, lo, hi, *refs):
+def halo_kernel(z_one, z_two, lo, hi, *refs):
     chunks, nu, resid, rows, field, right, drive, flat = refs[8:]
     column = lax.axis_index("gy")
 
@@ -260,13 +265,16 @@
     def above(value):
         return jnp.where(column == GY - 1, 0.0, value)
 
-    for p in range(3):
-        field[p, 16:16 + YC] = zgot[p]
+    half = YC // 2
+    field[0, 16:16 + YC] = z_one[0:YC]
+    field[1, 16:16 + YC] = z_one[YC:2 * YC]
+    field[2, 16:16 + half] = z_one[2 * YC:]
+    field[2, 16 + half:16 + YC] = z_two[0:half]
     for z in range(ZC):
         field[z + 3, 11:16] = below(lo[5 * z:5 * z + 5])
         field[z + 3, 80:86] = above(hi[6 * z:6 * z + 6])
     for t in range(2):
-        drive[t, 8:8 + YC] = zgot[3 + t]
+        drive[t, 8:8 + YC] = z_two[half + YC * t:half + YC * t + YC]
     for z in range(ZC - 2):
         drive[z + 2, 4:8] = lo[80 + 4 * z:84 + 4 * z]
         drive[z + 2, 72:76] = hi[96 + 4 * z:100 + 4 * z]
@@ -518,19 +526,20 @@
         for argument in (iterate, source, region, fixed_mask)
     ]
     edge = (2, ZC, 8, 128)
-    zmsg, up, down = call(
+    z_one, z_two, up, down = call(
         edge_kernel,
-        (struct(5, YC, 128), struct(160, 128), struct(176, 128)),
+        (struct(160, 128), struct(160, 128), struct(176, 128), struct(176, 128)),
         scratch=[
             pltpu.VMEM(edge, F32), pltpu.VMEM(edge, F32),
             pltpu.VMEM((2, 1, 8, 128), jnp.int32), pltpu.VMEM((2, 1, 8, 128), jnp.int32),
-            pltpu.SemaphoreType.DMA((10,)),
+            pltpu.SemaphoreType.DMA((14,)),
         ],
         in_specs=[far] * 4,
     )(*arguments)
     lo = lax.ppermute(up, "gy", cyclic(GY, 1))
     hi = lax.ppermute(down, "gy", cyclic(GY, -1))
-    zgot = lax.ppermute(zmsg, "gz", cyclic(GZ, 1))
+    z_one = lax.ppermute(z_one, "gz", cyclic(GZ, 1))
+    z_two = lax.ppermute(z_two, "gz", cyclic(GZ, 1))
     kept = (
         struct(GZ, 72, 128), struct(18, WIDE, 128), struct(*cells), struct(24 * FR, 128),
         struct(19, WIDE, 128), struct(18, FR, 128), struct(ZC, FR, 128), struct(2, FR, 128),
@@ -550,8 +559,8 @@
     corners = lax.ppermute(corners, "gz", cyclic(GZ, 1))
     state = call(
         halo_kernel, kept, cost_estimate=COST,
-        input_output_aliases={3 + k: k for k in range(len(kept))},
-    )(zgot, lo, hi, *state, frames)
+        input_output_aliases={4 + k: k for k in range(len(kept))},
+    )(z_one, z_two, lo, hi, *state, frames)
     chunks, nu, resid, *_, frames = call(
         corner_residual_kernel, kept,
         input_output_aliases={1 + k: k for k in range(len(kept))},

time: 82.6 us -> 80.6 us (0.976)
  waiting for transfers between devices: 2.59 us -> 0.02 us
    ppermute x1, waiting for transfers between devices: 2.58 us -> 0.01 us  [shards(): lo = lax.ppermute(up, 'gy', cyclic(GY, 1))]
    ppermute x1, starting transfers between devices: 0.01 us -> 2.54 us  [shards(): lo = lax.ppermute(up, 'gy', cyclic(GY, 1))]
    ppermute x1, starting transfers between devices: 3.76 us -> 2.2 us  [shards(): hi = lax.ppermute(down, 'gy', cyclic(GY, -1))]
    ppermute x1 -> x2, starting transfers between devices: 2.67 us -> 2.08 us  [the longest x1 2.05 us: shards(): z_one = lax.ppermute(z_one, 'gz', cyclic(GZ, 1))]
  transfers between devices with their start and end apart: 5 -> 6, of which waited for: 1 -> 0; matrix products, arithmetic and copies ran while one was open for 0% -> 0% of each run, Pallas kernels for 6% -> 6%
where the time goes in v6:
time: 80.6 us; the launch traced here: 80.3 us
  blocking collectives  57.1 us (71%)
  Pallas kernels  13.4 us (17%)
  starting transfers between devices  9.08 us (11%)
    all_to_all x1, blocking collectives, shards(): windows = lax.all_to_all(chunks, 'gz', 0, 0, tiled=True)  25.5 us
    all_to_all x1, blocking collectives, shards(): returned = lax.all_to_all(sent, 'gz', 0, 0, tiled=True)  16.5 us
    all_to_all x1, blocking collectives, shards(): sums = lax.all_to_all(sums, ('gz', 'gy'), 0, 0, tiled=True)  15.1 us
    pallas_call x1, Pallas kernels, shards(): call(modes_kernel, struct(GZ, 40, 128), scratch=[pltpu.VMEM((NZ, LANES),...  3.79 us
    ppermute x1, starting transfers between devices, shards(): lo = lax.ppermute(up, 'gy', cyclic(GY, 1))  2.54 us
    pallas_call x1, Pallas kernels, shards(): call(inner_kernel, kept, scratch=[pltpu.VMEM((1, YC, 128), jnp.int32), pl...  2.52 us
    pallas_call x1, Pallas kernels, shards(): call(halo_kernel, kept, cost_estimate=COST, input_output_aliases={4 + k:...  2.28 us
    ppermute x1, starting transfers between devices, shards(): hi = lax.ppermute(down, 'gy', cyclic(GY, -1))  2.2 us
  transfers between devices with their start and end apart: 6, of which 0 were waited for; matrix products, arithmetic and copies ran while one was open for 0% of the time, Pallas kernels for 6%

profile of v6, /device:TPU:1, one launch (start us, length us, event | category | flops | bytes accessed | tf_op | source)
XLA Modules:
  0.0 80.3 jit_solution(10293635088896821637)
XLA Ops:
  0.6 1.2 %shard_map.121 = (f32[160,128]{1,0:T(8,128)S(1)}, f32[160,128]{1,0:T(8,128)S(1)}, f32[176,128]{1,0:T(8,128)S(1)}, f32[176,128]{1,0:T(8,128)S(1)}) custom-call(f32[16,64,128]{2,1,0:T(8,128)} %it.3, f32[16,64,128]{2,1,0:T(8,128)} %src.3, s32[16,64,128]{2,1,0:T(8,128)} %reg.3, s32[16,64,128]{2,1,0:T(8,128)} %msk.3), custom_call_target="tpu_custom_call" | custom-call | tf_op jit(solution)/shard_map/pallas_call | solution.py:529
  1.9 2.5 %collective-permute-start = (f32[176,128]{1,0:T(8,128)S(1)}, f32[176,128]{1,0:T(8,128)S(1)}, u32[]{:S(2)}, u32[]{:S(2)}) collective-permute-start(f32[176,128]{1,0:T(8,128)S(1)} %get-tuple-element.36), channel_id=1, source_target_pairs={{0,1},{1,2},{2,3},{3,0},{4,5},{5,6},{6,7},{7,4},{8,9},{9,10},{10,1... | collective-permute-start | bytes 270344 | tf_op jit(solution)/shard_map/ppermute | solution.py:539
  4.4 2.2 %collective-permute-start.1 = (f32[176,128]{1,0:T(8,128)S(1)}, f32[176,128]{1,0:T(8,128)S(1)}, u32[]{:S(2)}, u32[]{:S(2)}) collective-permute-start(f32[176,128]{1,0:T(8,128)S(1)} %get-tuple-element.39), channel_id=1, source_target_pairs={{0,3},{1,0},{2,1},{3,2},{4,7},{5,4},{6,5},{7,6},{8,11},{9,8},{10,9... | collective-permute-start | bytes 270344 | tf_op jit(solution)/shard_map/ppermute | solution.py:540
  6.6 2.1 %collective-permute-start.3 = (f32[160,128]{1,0:T(8,128)S(1)}, f32[160,128]{1,0:T(8,128)S(1)}, u32[]{:S(2)}, u32[]{:S(2)}) collective-permute-start(f32[160,128]{1,0:T(8,128)S(1)} %get-tuple-element.40), channel_id=1, source_target_pairs={{0,4},{4,8},{8,12},{12,16},{16,20},{20,24},{24,28},{28,32},{32,36}... | collective-permute-start | bytes 245768 | tf_op jit(solution)/shard_map/ppermute | solution.py:541
  8.6 0.0 collective-permute-start.4
  8.7 2.5 %shard_map.122 = (f32[32,72,128]{2,1,0:T(8,128)S(1)}, f32[18,96,128]{2,1,0:T(8,128)S(1)}, f32[16,64,128]{2,1,0:T(8,128)S(1)}, f32[1920,128]{1,0:T(8,128)S(1)}, f...) custom-call(f32[16,64,128]{2,1,0:T(8,128)} %it.3, ...), custom_call_target="tpu_custom_call" | custom-call | flops 4000000 | bytes 8000000 | tf_op jit(solution)/shard_map/pallas_call | solution.py:547
  11.2 0.0 collective-permute-done.1.hi
  11.2 1.6 %collective-permute-start.2 = (f32[56,128]{1,0:T(8,128)S(1)}, f32[56,128]{1,0:T(8,128)S(1)}, u32[]{:S(2)}, u32[]{:S(2)}) collective-permute-start(f32[56,128]{1,0:T(8,128)S(1)} %shard_map.123), channel_id=1, source_target_pairs={{0,4},{4,8},{8,12},{12,16},{16,20},{20,24},{24,28},{28,32},{32,36}... | collective-permute-start | bytes 86024 | tf_op jit(solution)/shard_map/ppermute | solution.py:559
  12.9 0.0 collective-permute-done.4.z_two
  12.9 2.3 %shard_map.124 = (f32[32,72,128]{2,1,0:T(8,128)S(1)}, f32[18,96,128]{2,1,0:T(8,128)S(1)}, f32[16,64,128]{2,1,0:T(8,128)S(1)}, f32[1920,128]{1,0:T(8,128)S(1)}, f...) custom-call(f32[160,128]{1,0:T(8,128)S(1)} %collective-permute-done., ...), custom_call_target="tpu_custom_call", output_to_operand_aliasing={{0}: (4, {}), {1}: (5, {}), {2}: (6, {}), {3}: (7, {}), {4}... | custom-call | flops 4000000 | bytes 8000000 | tf_op jit(solution)/shard_map/pallas_call | solution.py:560
  15.2 0.0 copy-start.5
  15.2 0.5 shard_map.125
  15.7 0.0 copy-start
  15.7 0.0 copy-start.1
  15.7 0.0 copy-start.2
  15.8 0.0 copy-start.3
  15.8 0.0 copy-start.4
  15.8 25.5 %all_to_all.15.got = f32[32,72,128]{2,1,0:T(8,128)S(1)} all-to-all(f32[32,72,128]{2,1,0:T(8,128)S(1)} %get-tuple-element.58), channel_id=1, replica_groups=mesh['gz'=32,'gy'=4] {'gz'}, dimensions={0} | all-to-all | bytes 2359296 | tf_op jit(solution)/shard_map/all_to_all | solution.py:568
  41.3 3.8 %shard_map.126 = f32[32,40,128]{2,1,0:T(8,128)S(1)} custom-call(f32[32,72,128]{2,1,0:T(8,128)S(1)} %all_to_all.15.got, bf16[512,512]{1,0:T(8,128)(2,1)S(1)} %copy-done.3, bf16[512,512]{1,0:T(8,128)(2,1)S(1)} %copy-done.2, bf16[512,512]{1,0:T(8,128)(2,1)S(1)} %copy-done.1, bf16[512,512]{1,0:T(8,128)(2,1)S(1)} %copy-done, f32[512,128]{1,0:T(8,128)S(1)} %copy-done.4, ...), custom_call_target="tpu_custom_call" | custom-call | tf_op jit(solution)/shard_map/pallas_call | solution.py:569
  45.1 16.5 %all_to_all.16.got = f32[32,40,128]{2,1,0:T(8,128)S(1)} all-to-all(f32[32,40,128]{2,1,0:T(8,128)S(1)} %shard_map.126), channel_id=1, replica_groups=mesh['gz'=32,'gy'=4] {'gz'}, dimensions={0} | all-to-all | bytes 1310720 | tf_op jit(solution)/shard_map/all_to_all | solution.py:576
  61.6 1.5 %shard_map.127 = (f32[18,64,128]{2,1,0:T(8,128)S(1)}, f32[16,64,128]{2,1,0:T(8,128)S(1)}, f32[4,64,128]{2,1,0:T(8,128)S(1)}, f32[128,1,128]{2,1,0:T(1,128)S(1)}) custom-call(f32[32,40,128]{2,1,0:T(8,128)S(1)} %all_to_all.16.got, f32[18,96,128]{2,1,0:T(8,128)S(1)} %get-tuple-element.59.nu, f32[16,64,128]{2,1,0:T(8,128)S(1)} %get-tuple-element.60.resid, ...), custom_call_target="tpu_custom_call" | custom-call | tf_op jit(solution)/shard_map/pallas_call | solution.py:577
  63.2 0.6 collective-permute-start.5
  63.8 15.1 %all_to_all.17.sums = f32[128,1,128]{2,1,0:T(1,128)S(1)} all-to-all(f32[128,1,128]{2,1,0:T(1,128)S(1)} %get-tuple-element.62), channel_id=1, replica_groups=mesh['gz'=32,'gy'=4] {'gz','gy'}, dimensions={0} | all-to-all | bytes 131072 | tf_op jit(solution)/shard_map/all_to_all | solution.py:586
  78.8 1.5 %shard_map.128 = (f32[16,64,128]{2,1,0:T(8,128)}, f32[16,64,128]{2,1,0:T(8,128)}, f32[1,128]{1,0:T(1,128)}) custom-call(f32[128,1,128]{2,1,0:T(1,128)S(1)} %all_to_all.17.sums, f32[18,64,128]{2,1,0:T(8,128)S(1)} %get-tuple-element.63.zdir, f32[16,64,128]{2,1,0:T(8,128)S(1)} %get-tuple-element.64.image, f32[16,64,128]{2,1,0:T(8,128)S(1)} %get-tuple-element.60.resid, ...), custom_call_target="tpu_custom_call" | custom-call | tf_op jit(solution)/shard_map/pallas_call | solution.py:587
  (11 shorter events, 0.0 us)
Async XLA Ops:
  1.9 9.4 %collective-permute-start = (f32[176,128]{1,0:T(8,128)S(1)}, f32[176,128]{1,0:T(8,128)S(1)}, u32[]{:S(2)}, u32[]{:S(2)}) collective-permute-start(f32[176,128]{1,0:T(8,128)S(1)} %get-tuple-element.36), channel_id=1, source_target_pairs={{0,1},{1,2},{2,3},{3,0},{4,5},{5,6},{6,7},{7,4},{8,9},{9,10},{10,1... | collective-permute-start | bytes 270344 | tf_op jit(solution)/shard_map/ppermute | solution.py:539
  4.4 6.8 %collective-permute-start.1 = (f32[176,128]{1,0:T(8,128)S(1)}, f32[176,128]{1,0:T(8,128)S(1)}, u32[]{:S(2)}, u32[]{:S(2)}) collective-permute-start(f32[176,128]{1,0:T(8,128)S(1)} %get-tuple-element.39), channel_id=1, source_target_pairs={{0,3},{1,0},{2,1},{3,2},{4,7},{5,4},{6,5},{7,6},{8,11},{9,8},{10,9... | collective-permute-start | bytes 270344 | tf_op jit(solution)/shard_map/ppermute | solution.py:540
  6.6 6.3 %collective-permute-start.3 = (f32[160,128]{1,0:T(8,128)S(1)}, f32[160,128]{1,0:T(8,128)S(1)}, u32[]{:S(2)}, u32[]{:S(2)}) collective-permute-start(f32[160,128]{1,0:T(8,128)S(1)} %get-tuple-element.40), channel_id=1, source_target_pairs={{0,4},{4,8},{8,12},{12,16},{16,20},{20,24},{24,28},{28,32},{32,36}... | collective-permute-start | bytes 245768 | tf_op jit(solution)/shard_map/ppermute | solution.py:541
  8.6 4.2 %collective-permute-start.4 = (f32[160,128]{1,0:T(8,128)S(1)}, f32[160,128]{1,0:T(8,128)S(1)}, u32[]{:S(2)}, u32[]{:S(2)}) collective-permute-start(f32[160,128]{1,0:T(8,128)S(1)} %get-tuple-element.41), channel_id=1, source_target_pairs={{0,4},{4,8},{8,12},{12,16},{16,20},{20,24},{24,28},{28,32},{32,36}... | collective-permute-start | bytes 245768 | tf_op jit(solution)/shard_map/ppermute | solution.py:542
  11.2 3.9 %collective-permute-start.2 = (f32[56,128]{1,0:T(8,128)S(1)}, f32[56,128]{1,0:T(8,128)S(1)}, u32[]{:S(2)}, u32[]{:S(2)}) collective-permute-start(f32[56,128]{1,0:T(8,128)S(1)} %shard_map.123), channel_id=1, source_target_pairs={{0,4},{4,8},{8,12},{12,16},{16,20},{20,24},{24,28},{28,32},{32,36}... | collective-permute-start | bytes 86024 | tf_op jit(solution)/shard_map/ppermute | solution.py:559
  15.2 26.1 %copy-start.5 = (s32[8,512]{1,0:T(8,128)S(1)}, s32[8,512]{1,0:T(8,128)}, u32[]{:S(2)}) copy-start(s32[8,512]{1,0:T(8,128)} %constant.17.clone.spots) | copy-start | bytes 49156
  15.7 25.5 %copy-start = (bf16[512,512]{1,0:T(8,128)(2,1)S(1)}, bf16[512,512]{1,0:T(8,128)(2,1)}, u32[]{:S(2)}) copy-start(bf16[512,512]{1,0:T(8,128)(2,1)} %constant.15.clone.low) | copy-start | bytes 1572868
  15.7 25.5 %copy-start.1 = (bf16[512,512]{1,0:T(8,128)(2,1)S(1)}, bf16[512,512]{1,0:T(8,128)(2,1)}, u32[]{:S(2)}) copy-start(bf16[512,512]{1,0:T(8,128)(2,1)} %constant.14.clone.high) | copy-start | bytes 1572868
  15.7 25.5 %copy-start.2 = (bf16[512,512]{1,0:T(8,128)(2,1)S(1)}, bf16[512,512]{1,0:T(8,128)(2,1)}, u32[]{:S(2)}) copy-start(bf16[512,512]{1,0:T(8,128)(2,1)} %constant.13.clone.ahead_low) | copy-start | bytes 1572868
  15.8 25.5 %copy-start.3 = (bf16[512,512]{1,0:T(8,128)(2,1)S(1)}, bf16[512,512]{1,0:T(8,128)(2,1)}, u32[]{:S(2)}) copy-start(bf16[512,512]{1,0:T(8,128)(2,1)} %constant.12.clone.ahead_high) | copy-start | bytes 1572868
  15.8 25.5 %copy-start.4 = (f32[512,128]{1,0:T(8,128)S(1)}, f32[512,128]{1,0:T(8,128)}, u32[]{:S(2)}) copy-start(f32[512,128]{1,0:T(8,128)} %constant.16.clone.lam) | copy-start | bytes 786436
  63.2 15.7 %collective-permute-start.5 = (f32[4,64,128]{2,1,0:T(8,128)S(1)}, f32[4,64,128]{2,1,0:T(8,128)S(1)}, u32[]{:S(2)}, u32[]{:S(2)}) collective-permute-start(f32[4,64,128]{2,1,0:T(8,128)S(1)} %get-tuple-element.65), channel_id=1, source_target_pairs={{0,124},{4,0},{8,4},{12,8},{16,12},{20,16},{24,20},{28,24},{32,28}... | collective-permute-start | bytes 393224 | tf_op jit(solution)/shard_map/ppermute | solution.py:585

commit v7 on v6

--- a/solution.py
+++ b/solution.py
@@ -255,7 +255,7 @@
     pack(rows, chunks, (1, 2), (1,))
 
 
-def halo_kernel(z_one, z_two, lo, hi, *refs):
+def halo_kernel(lo, hi, *refs):
     chunks, nu, resid, rows, field, right, drive, flat = refs[8:]
     column = lax.axis_index("gy")
 
@@ -265,16 +265,9 @@
     def above(value):
         return jnp.where(column == GY - 1, 0.0, value)
 
-    half = YC // 2
-    field[0, 16:16 + YC] = z_one[0:YC]
-    field[1, 16:16 + YC] = z_one[YC:2 * YC]
-    field[2, 16:16 + half] = z_one[2 * YC:]
-    field[2, 16 + half:16 + YC] = z_two[0:half]
     for z in range(ZC):
         field[z + 3, 11:16] = below(lo[5 * z:5 * z + 5])
         field[z + 3, 80:86] = above(hi[6 * z:6 * z + 6])
-    for t in range(2):
-        drive[t, 8:8 + YC] = z_two[half + YC * t:half + YC * t + YC]
     for z in range(ZC - 2):
         drive[z + 2, 4:8] = lo[80 + 4 * z:84 + 4 * z]
         drive[z + 2, 72:76] = hi[96 + 4 * z:100 + 4 * z]
@@ -282,11 +275,22 @@
     flat[0, 72:77] = above(hi[160:165])
     flat[1, 4:8] = lo[149:153]
     flat[1, 72:76] = hi[165:169]
+    work(OUTER, HERE, range(3, ZC), field, right, nu, drive, flat, rows, resid)
+    pack(rows, chunks, (0, 3), (1,))
+
+
+def behind_kernel(z_one, z_two, *refs):
+    chunks, nu, resid, rows, field, right, drive, flat = refs[8:]
+    half = YC // 2
+    field[0, 16:16 + YC] = z_one[0:YC]
+    field[1, 16:16 + YC] = z_one[YC:2 * YC]
+    field[2, 16:16 + half] = z_one[2 * YC:]
+    field[2, 16 + half:16 + YC] = z_two[0:half]
+    for t in range(2):
+        drive[t, 8:8 + YC] = z_two[half + YC * t:half + YC * t + YC]
     work(INNER, BEHIND, range(0, 3), field, right, nu, drive, flat, rows, resid)
-    work(OUTER, HERE, range(3, ZC), field, right, nu, drive, flat, rows, resid)
     sum_planes(INNER, nu, rows)
     pack(rows, chunks, (1, 2), (0, 2))
-    pack(rows, chunks, (0, 3), (1,))
 
 
 def corner_residual_kernel(corners, *refs):
@@ -559,8 +563,12 @@
     corners = lax.ppermute(corners, "gz", cyclic(GZ, 1))
     state = call(
         halo_kernel, kept, cost_estimate=COST,
-        input_output_aliases={4 + k: k for k in range(len(kept))},
-    )(z_one, z_two, lo, hi, *state, frames)
+        input_output_aliases={2 + k: k for k in range(len(kept))},
+    )(lo, hi, *state, frames)
+    state = call(
+        behind_kernel, kept, cost_estimate=COST,
+        input_output_aliases={2 + k: k for k in range(len(kept))},
+    )(z_one, z_two, *state)
     chunks, nu, resid, *_, frames = call(
         corner_residual_kernel, kept,
         input_output_aliases={1 + k: k for k in range(len(kept))},

time: 80.6 us -> 80.6 us (level)
  Pallas kernels: 13.4 us -> 12.3 us
  blocking collectives: 57.1 us -> 58.1 us
    pallas_call x1 -> x2, Pallas kernels: 2.28 us -> 1.26 us  [the longest x1 0.72 us: shards(): call(halo_kernel, kept, cost_estimate=COST, input_output_aliases={2 + k:...]
    all_to_all x1, blocking collectives: 25.5 us -> 26.5 us  [shards(): windows = lax.all_to_all(chunks, 'gz', 0, 0, tiled=True)]
  transfers between devices with their start and end apart: 6 -> 6, of which waited for: 0 -> 0; matrix products, arithmetic and copies ran while one was open for 0% -> 0% of each run, Pallas kernels for 6% -> 5%
where the time goes in v7:
time: 80.6 us; the launch traced here: 80.3 us
  blocking collectives  58.1 us (72%)
  Pallas kernels  12.3 us (15%)
  starting transfers between devices  9.08 us (11%)
  between operations  0.81 us (1%)
    all_to_all x1, blocking collectives, shards(): windows = lax.all_to_all(chunks, 'gz', 0, 0, tiled=True)  26.5 us
    all_to_all x1, blocking collectives, shards(): returned = lax.all_to_all(sent, 'gz', 0, 0, tiled=True)  16.5 us
    all_to_all x1, blocking collectives, shards(): sums = lax.all_to_all(sums, ('gz', 'gy'), 0, 0, tiled=True)  15 us
    pallas_call x1, Pallas kernels, shards(): call(modes_kernel, struct(GZ, 40, 128), scratch=[pltpu.VMEM((NZ, LANES),...  3.79 us
    ppermute x1, starting transfers between devices, shards(): lo = lax.ppermute(up, 'gy', cyclic(GY, 1))  2.54 us
    pallas_call x1, Pallas kernels, shards(): call(inner_kernel, kept, scratch=[pltpu.VMEM((1, YC, 128), jnp.int32), pl...  2.52 us
    ppermute x1, starting transfers between devices, shards(): hi = lax.ppermute(down, 'gy', cyclic(GY, -1))  2.2 us
    ppermute x1, starting transfers between devices, shards(): z_one = lax.ppermute(z_one, 'gz', cyclic(GZ, 1))  2.05 us
  transfers between devices with their start and end apart: 6, of which 0 were waited for; matrix products, arithmetic and copies ran while one was open for 0% of the time, Pallas kernels for 5%

profile of v7, /device:TPU:1, one launch (start us, length us, event | category | flops | bytes accessed | tf_op | source)
XLA Modules:
  0.0 80.3 jit_solution(5916061382271513440)
XLA Ops:
  0.6 1.2 %shard_map.121 = (f32[160,128]{1,0:T(8,128)S(1)}, f32[160,128]{1,0:T(8,128)S(1)}, f32[176,128]{1,0:T(8,128)S(1)}, f32[176,128]{1,0:T(8,128)S(1)}) custom-call(f32[16,64,128]{2,1,0:T(8,128)} %it.3, f32[16,64,128]{2,1,0:T(8,128)} %src.3, s32[16,64,128]{2,1,0:T(8,128)} %reg.3, s32[16,64,128]{2,1,0:T(8,128)} %msk.3), custom_call_target="tpu_custom_call" | custom-call | tf_op jit(solution)/shard_map/pallas_call | solution.py:533
  1.9 2.5 %collective-permute-start = (f32[176,128]{1,0:T(8,128)S(1)}, f32[176,128]{1,0:T(8,128)S(1)}, u32[]{:S(2)}, u32[]{:S(2)}) collective-permute-start(f32[176,128]{1,0:T(8,128)S(1)} %get-tuple-element.44), channel_id=1, source_target_pairs={{0,1},{1,2},{2,3},{3,0},{4,5},{5,6},{6,7},{7,4},{8,9},{9,10},{10,1... | collective-permute-start | bytes 270344 | tf_op jit(solution)/shard_map/ppermute | solution.py:543
  4.4 2.2 %collective-permute-start.1 = (f32[176,128]{1,0:T(8,128)S(1)}, f32[176,128]{1,0:T(8,128)S(1)}, u32[]{:S(2)}, u32[]{:S(2)}) collective-permute-start(f32[176,128]{1,0:T(8,128)S(1)} %get-tuple-element.47), channel_id=1, source_target_pairs={{0,3},{1,0},{2,1},{3,2},{4,7},{5,4},{6,5},{7,6},{8,11},{9,8},{10,9... | collective-permute-start | bytes 270344 | tf_op jit(solution)/shard_map/ppermute | solution.py:544
  6.6 2.1 %collective-permute-start.3 = (f32[160,128]{1,0:T(8,128)S(1)}, f32[160,128]{1,0:T(8,128)S(1)}, u32[]{:S(2)}, u32[]{:S(2)}) collective-permute-start(f32[160,128]{1,0:T(8,128)S(1)} %get-tuple-element.48), channel_id=1, source_target_pairs={{0,4},{4,8},{8,12},{12,16},{16,20},{20,24},{24,28},{28,32},{32,36}... | collective-permute-start | bytes 245768 | tf_op jit(solution)/shard_map/ppermute | solution.py:545
  8.6 0.0 collective-permute-start.4
  8.7 2.5 %shard_map.122 = (f32[32,72,128]{2,1,0:T(8,128)S(1)}, f32[18,96,128]{2,1,0:T(8,128)S(1)}, f32[16,64,128]{2,1,0:T(8,128)S(1)}, f32[1920,128]{1,0:T(8,128)S(1)}, f...) custom-call(f32[16,64,128]{2,1,0:T(8,128)} %it.3, ...), custom_call_target="tpu_custom_call" | custom-call | flops 4000000 | bytes 8000000 | tf_op jit(solution)/shard_map/pallas_call | solution.py:551
  11.2 0.0 collective-permute-done.lo
  11.2 1.6 %collective-permute-start.2 = (f32[56,128]{1,0:T(8,128)S(1)}, f32[56,128]{1,0:T(8,128)S(1)}, u32[]{:S(2)}, u32[]{:S(2)}) collective-permute-start(f32[56,128]{1,0:T(8,128)S(1)} %shard_map.123), channel_id=1, source_target_pairs={{0,4},{4,8},{8,12},{12,16},{16,20},{20,24},{24,28},{28,32},{32,36}... | collective-permute-start | bytes 86024 | tf_op jit(solution)/shard_map/ppermute | solution.py:563
  12.9 0.7 shard_map.124
  13.6 0.5 shard_map.125
  14.2 0.0 copy-start.5
  14.2 0.5 shard_map.126
  14.7 0.0 copy-start
  14.7 0.0 copy-start.1
  14.8 0.0 copy-start.2
  14.8 0.0 copy-start.3
  14.8 0.0 copy-start.4
  14.8 26.5 %all_to_all.15.got = f32[32,72,128]{2,1,0:T(8,128)S(1)} all-to-all(f32[32,72,128]{2,1,0:T(8,128)S(1)} %get-tuple-element.74), channel_id=1, replica_groups=mesh['gz'=32,'gy'=4] {'gz'}, dimensions={0} | all-to-all | bytes 2359296 | tf_op jit(solution)/shard_map/all_to_all | solution.py:576
  41.3 3.8 %shard_map.127 = f32[32,40,128]{2,1,0:T(8,128)S(1)} custom-call(f32[32,72,128]{2,1,0:T(8,128)S(1)} %all_to_all.15.got, bf16[512,512]{1,0:T(8,128)(2,1)S(1)} %copy-done.3, bf16[512,512]{1,0:T(8,128)(2,1)S(1)} %copy-done.2, bf16[512,512]{1,0:T(8,128)(2,1)S(1)} %copy-done.1, bf16[512,512]{1,0:T(8,128)(2,1)S(1)} %copy-done, f32[512,128]{1,0:T(8,128)S(1)} %copy-done.4, ...), custom_call_target="tpu_custom_call" | custom-call | tf_op jit(solution)/shard_map/pallas_call | solution.py:577
  45.1 16.5 %all_to_all.16.got = f32[32,40,128]{2,1,0:T(8,128)S(1)} all-to-all(f32[32,40,128]{2,1,0:T(8,128)S(1)} %shard_map.127), channel_id=1, replica_groups=mesh['gz'=32,'gy'=4] {'gz'}, dimensions={0} | all-to-all | bytes 1310720 | tf_op jit(solution)/shard_map/all_to_all | solution.py:584
  61.6 1.5 %shard_map.128 = (f32[18,64,128]{2,1,0:T(8,128)S(1)}, f32[16,64,128]{2,1,0:T(8,128)S(1)}, f32[4,64,128]{2,1,0:T(8,128)S(1)}, f32[128,1,128]{2,1,0:T(1,128)S(1)}) custom-call(f32[32,40,128]{2,1,0:T(8,128)S(1)} %all_to_all.16.got, f32[18,96,128]{2,1,0:T(8,128)S(1)} %get-tuple-element.75.nu, f32[16,64,128]{2,1,0:T(8,128)S(1)} %get-tuple-element.76.resid, ...), custom_call_target="tpu_custom_call" | custom-call | tf_op jit(solution)/shard_map/pallas_call | solution.py:585
  63.2 0.6 collective-permute-start.5
  63.8 15.0 %all_to_all.17.sums = f32[128,1,128]{2,1,0:T(1,128)S(1)} all-to-all(f32[128,1,128]{2,1,0:T(1,128)S(1)} %get-tuple-element.78), channel_id=1, replica_groups=mesh['gz'=32,'gy'=4] {'gz','gy'}, dimensions={0} | all-to-all | bytes 131072 | tf_op jit(solution)/shard_map/all_to_all | solution.py:594
  78.8 1.5 %shard_map.129 = (f32[16,64,128]{2,1,0:T(8,128)}, f32[16,64,128]{2,1,0:T(8,128)}, f32[1,128]{1,0:T(1,128)}) custom-call(f32[128,1,128]{2,1,0:T(1,128)S(1)} %all_to_all.17.sums, f32[18,64,128]{2,1,0:T(8,128)S(1)} %get-tuple-element.79.zdir, f32[16,64,128]{2,1,0:T(8,128)S(1)} %get-tuple-element.80.image, f32[16,64,128]{2,1,0:T(8,128)S(1)} %get-tuple-element.76.resid, ...), custom_call_target="tpu_custom_call" | custom-call | tf_op jit(solution)/shard_map/pallas_call | solution.py:595
  (12 shorter events, 0.0 us)
Async XLA Ops:
  1.9 9.4 %collective-permute-start = (f32[176,128]{1,0:T(8,128)S(1)}, f32[176,128]{1,0:T(8,128)S(1)}, u32[]{:S(2)}, u32[]{:S(2)}) collective-permute-start(f32[176,128]{1,0:T(8,128)S(1)} %get-tuple-element.44), channel_id=1, source_target_pairs={{0,1},{1,2},{2,3},{3,0},{4,5},{5,6},{6,7},{7,4},{8,9},{9,10},{10,1... | collective-permute-start | bytes 270344 | tf_op jit(solution)/shard_map/ppermute | solution.py:543
  4.4 6.8 %collective-permute-start.1 = (f32[176,128]{1,0:T(8,128)S(1)}, f32[176,128]{1,0:T(8,128)S(1)}, u32[]{:S(2)}, u32[]{:S(2)}) collective-permute-start(f32[176,128]{1,0:T(8,128)S(1)} %get-tuple-element.47), channel_id=1, source_target_pairs={{0,3},{1,0},{2,1},{3,2},{4,7},{5,4},{6,5},{7,6},{8,11},{9,8},{10,9... | collective-permute-start | bytes 270344 | tf_op jit(solution)/shard_map/ppermute | solution.py:544
  6.6 7.0 %collective-permute-start.3 = (f32[160,128]{1,0:T(8,128)S(1)}, f32[160,128]{1,0:T(8,128)S(1)}, u32[]{:S(2)}, u32[]{:S(2)}) collective-permute-start(f32[160,128]{1,0:T(8,128)S(1)} %get-tuple-element.48), channel_id=1, source_target_pairs={{0,4},{4,8},{8,12},{12,16},{16,20},{20,24},{24,28},{28,32},{32,36}... | collective-permute-start | bytes 245768 | tf_op jit(solution)/shard_map/ppermute | solution.py:545
  8.6 5.0 %collective-permute-start.4 = (f32[160,128]{1,0:T(8,128)S(1)}, f32[160,128]{1,0:T(8,128)S(1)}, u32[]{:S(2)}, u32[]{:S(2)}) collective-permute-start(f32[160,128]{1,0:T(8,128)S(1)} %get-tuple-element.49), channel_id=1, source_target_pairs={{0,4},{4,8},{8,12},{12,16},{16,20},{20,24},{24,28},{28,32},{32,36}... | collective-permute-start | bytes 245768 | tf_op jit(solution)/shard_map/ppermute | solution.py:546
  11.2 2.9 %collective-permute-start.2 = (f32[56,128]{1,0:T(8,128)S(1)}, f32[56,128]{1,0:T(8,128)S(1)}, u32[]{:S(2)}, u32[]{:S(2)}) collective-permute-start(f32[56,128]{1,0:T(8,128)S(1)} %shard_map.123), channel_id=1, source_target_pairs={{0,4},{4,8},{8,12},{12,16},{16,20},{20,24},{24,28},{28,32},{32,36}... | collective-permute-start | bytes 86024 | tf_op jit(solution)/shard_map/ppermute | solution.py:563
  14.2 27.1 %copy-start.5 = (s32[8,512]{1,0:T(8,128)S(1)}, s32[8,512]{1,0:T(8,128)}, u32[]{:S(2)}) copy-start(s32[8,512]{1,0:T(8,128)} %constant.17.clone.spots) | copy-start | bytes 49156
  14.7 26.5 %copy-start = (bf16[512,512]{1,0:T(8,128)(2,1)S(1)}, bf16[512,512]{1,0:T(8,128)(2,1)}, u32[]{:S(2)}) copy-start(bf16[512,512]{1,0:T(8,128)(2,1)} %constant.15.clone.low) | copy-start | bytes 1572868
  14.7 26.5 %copy-start.1 = (bf16[512,512]{1,0:T(8,128)(2,1)S(1)}, bf16[512,512]{1,0:T(8,128)(2,1)}, u32[]{:S(2)}) copy-start(bf16[512,512]{1,0:T(8,128)(2,1)} %constant.14.clone.high) | copy-start | bytes 1572868
  14.8 26.5 %copy-start.2 = (bf16[512,512]{1,0:T(8,128)(2,1)S(1)}, bf16[512,512]{1,0:T(8,128)(2,1)}, u32[]{:S(2)}) copy-start(bf16[512,512]{1,0:T(8,128)(2,1)} %constant.13.clone.ahead_low) | copy-start | bytes 1572868
  14.8 26.5 %copy-start.3 = (bf16[512,512]{1,0:T(8,128)(2,1)S(1)}, bf16[512,512]{1,0:T(8,128)(2,1)}, u32[]{:S(2)}) copy-start(bf16[512,512]{1,0:T(8,128)(2,1)} %constant.12.clone.ahead_high) | copy-start | bytes 1572868
  14.8 26.5 %copy-start.4 = (f32[512,128]{1,0:T(8,128)S(1)}, f32[512,128]{1,0:T(8,128)}, u32[]{:S(2)}) copy-start(f32[512,128]{1,0:T(8,128)} %constant.16.clone.lam) | copy-start | bytes 786436
  63.2 15.7 %collective-permute-start.5 = (f32[4,64,128]{2,1,0:T(8,128)S(1)}, f32[4,64,128]{2,1,0:T(8,128)S(1)}, u32[]{:S(2)}, u32[]{:S(2)}) collective-permute-start(f32[4,64,128]{2,1,0:T(8,128)S(1)} %get-tuple-element.81), channel_id=1, source_target_pairs={{0,124},{4,0},{8,4},{12,8},{16,12},{20,16},{24,20},{28,24},{32,28}... | collective-permute-start | bytes 393224 | tf_op jit(solution)/shard_map/ppermute | solution.py:593
